TPU v7x, 32 devices: a whole 2x2x4 slice. The times are simulated.
32 devices in a mesh: dp: 8 (over z, y), row: 2 (over x), col: 2 (over core).
Axes of the slice: x: 2, y: 2, z: 4, core: 2. Of those that a mesh axis runs over, the one named last changes fastest.
Arguments:
- block_input: bfloat16 [73856, 1024], P(('dp', 'col'), 'row'), may hold values from -6 to 6
- image_valid: int32 [128], P('dp'), may hold values 0 or 1
- first_gain: bfloat16 [1024], P('row'), may hold values from 0.5 to 1.5
- first_shift: bfloat16 [1024], P('row'), may hold values from -1.5 to 1.5
- attend_weight: bfloat16 [1024, 3072], P('row', 'col'), may hold values from -0.1875 to 0.1875
- attend_bias: bfloat16 [2048], P('col'), may hold values from -2.5 to 2.5
- output_weight: bfloat16 [1024, 1024], P('col', 'row'), may hold values from -0.75 to 0.75
- output_bias: bfloat16 [1024], P('row'), may hold values from -2.5 to 2.5
- second_gain: bfloat16 [1024], P('row'), may hold values from 0.5 to 1.5
- second_shift: bfloat16 [1024], P('row'), may hold values from -1.5 to 1.5
- expand_weight: bfloat16 [1024, 4096], P('row', 'col'), may hold values from -0.1875 to 0.1875
- expand_bias: bfloat16 [4096], P('col'), may hold values from -2.5 to 2.5
- reduce_weight: bfloat16 [4096, 1024], P('col', 'row'), may hold values from -0.09375 to 0.09375
- reduce_bias: bfloat16 [1024], P('row'), may hold values from -2.5 to 2.5
- output_grad: bfloat16 [73856, 1024], P(('dp', 'col'), 'row'), may hold values from -6 to 6
Outputs:
- block_output: bfloat16 [73856, 1024], P(('dp', 'col'), 'row')
- input_grad: float32 [73856, 1024], P(('dp', 'col'), 'row')
- first_gain_grad: float32 [1024], P('row')
- first_shift_grad: float32 [1024], P('row')
- attend_weight_grad: float32 [1024, 3072], P('row', 'col')
- attend_bias_grad: float32 [2048], P('col')
- output_weight_grad: float32 [1024, 1024], P('col', 'row')
- output_bias_grad: float32 [1024], P('row')
- second_gain_grad: float32 [1024], P('row')
- second_shift_grad: float32 [1024], P('row')
- expand_weight_grad: float32 [1024, 4096], P('row', 'col')
- expand_bias_grad: float32 [4096], P('col')
- reduce_weight_grad: float32 [4096, 1024], P('col', 'row')
- reduce_bias_grad: float32 [1024], P('row')
Inputs may be any that keep to these rules, and one draw needn't show every extreme that they name: `image_valid`: 1 marks a real image, 0 a padded slot.
All inputs are finite; a program needn't handle non-finite values. No bound on the sum of `image_valid` on one device may be relied on, other than what follows from the above.
Results may differ from a plain program's by a relative error of at most 0.015.
Values may be sent and summed in bfloat16 or wider, within the bound.
No kernel may reach another device: no remote copies, remote signals or barrier semaphores. Data moves between devices by JAX's collectives and lax.ppermute only.
A program may use at most 576 MiB of HBM per device.

v0:
```python
from functools import partial

import jax
import jax.numpy as jnp
from jax import lax
from jax.sharding import PartitionSpec as P

D = 1024
HEADS = 16
HD = 64
SEQ = 577


EPSILON = 1e-06


def contract_first(left, right):
    return lax.dot_general(
        left, right, (((0,), (0,)), ((), ())), preferred_element_type=jnp.float32
    )


def contract_last(left, right):
    return lax.dot_general(
        left, right, (((1,), (1,)), ((), ())), preferred_element_type=jnp.float32
    )


def attend_image(packed_image):
    queries = packed_image[:, :, 0]
    keys_in = packed_image[:, :, 1]
    values_in = packed_image[:, :, 2]
    scaling = queries.shape[-1] ** (-0.5)
    scores = (
        jnp.einsum("qhd,khd->hqk", queries, keys_in, preferred_element_type=jnp.float32) * scaling
    )
    highest = jnp.max(scores, -1, keepdims=True)
    expo = jnp.exp(scores - highest)
    totals = jnp.sum(expo, -1, keepdims=True)
    weights = (expo / totals).astype(jnp.bfloat16)
    mixed = jnp.einsum("hqk,khd->qhd", weights, values_in, preferred_element_type=jnp.float32)
    return (mixed.astype(jnp.bfloat16), (highest + jnp.log(totals))[..., 0])


def attend_image_back(pieces):
    packed_image, grad_mixed, log_totals = pieces
    queries = packed_image[:, :, 0]
    keys_in = packed_image[:, :, 1]
    values_in = packed_image[:, :, 2]
    scaling = queries.shape[-1] ** (-0.5)
    scores = (
        jnp.einsum("qhd,khd->hqk", queries, keys_in, preferred_element_type=jnp.float32) * scaling
    )
    weights = jnp.exp(scores - log_totals[..., None])
    weight_grad = jnp.einsum(
        "qhd,khd->hqk", grad_mixed, values_in, preferred_element_type=jnp.float32
    )
    value_grad = jnp.einsum(
        "hqk,qhd->khd", weights.astype(jnp.bfloat16), grad_mixed, preferred_element_type=jnp.float32
    )
    row_dot = jnp.sum(weights * weight_grad, -1, keepdims=True)
    score_low = (weights * (weight_grad - row_dot)).astype(jnp.bfloat16)
    query_grad = (
        jnp.einsum("hqk,khd->qhd", score_low, keys_in, preferred_element_type=jnp.float32) * scaling
    )
    key_grad = (
        jnp.einsum("hqk,qhd->khd", score_low, queries, preferred_element_type=jnp.float32) * scaling
    )
    return jnp.stack([query_grad, key_grad, value_grad], 2).astype(jnp.bfloat16)


def grid_block(
    block_input,
    image_valid,
    first_gain,
    first_shift,
    attend_weight,
    attend_bias,
    output_weight,
    output_bias,
    second_gain,
    second_shift,
    expand_weight,
    expand_bias,
    reduce_weight,
    reduce_bias,
    output_grad,
):
    col_size = lax.axis_size("col")
    row_size = lax.axis_size("row")
    row_index = lax.axis_index("row")
    col_index = lax.axis_index("col")
    local_rows = block_input.shape[0]
    group_rows = local_rows * col_size
    group_images = group_rows // SEQ
    images_here = image_valid.shape[0] // col_size
    heads_here = HEADS // (row_size * col_size)
    valid_local = lax.dynamic_slice_in_dim(
        image_valid, col_index * images_here, images_here
    ).astype(jnp.float32)
    valid_rows = jnp.repeat(valid_local, SEQ)
    inputs = block_input.astype(jnp.float32)

    def gather_tokens(values):
        return lax.all_gather(values, "col", axis=0, tiled=True)

    def gather_heads(values):
        return lax.all_gather(values, "row", axis=1, tiled=True)

    def sum_heads(values):
        return lax.psum_scatter(values, "row", scatter_dimension=1, tiled=True)

    def sum_tokens(term):
        return lax.psum_scatter(
            term(jnp.int32(0), local_rows * lax.axis_size("col")),
            "col",
            scatter_dimension=0,
            tiled=True,
        )

    def row_statistics(first, second):
        return lax.psum((first, second), "row")

    def norm_forward(values, gain, shift):
        sums, squares = row_statistics(jnp.sum(values, 1), jnp.sum(values * values, 1))
        center = sums / D
        inverse = lax.rsqrt(squares / D - center * center + EPSILON)
        scaled = (values - center[:, None]) * inverse[:, None]
        normed = (scaled * gain.astype(jnp.float32) + shift.astype(jnp.float32)).astype(
            jnp.bfloat16
        )
        return (scaled, inverse, normed)

    def norm_back(upstream, scaled, inverse, gain):
        scaled_grad = upstream * gain.astype(jnp.float32)
        sum_plain, sum_cross = row_statistics(
            jnp.sum(scaled_grad, 1), jnp.sum(scaled_grad * scaled, 1)
        )
        values_grad = inverse[:, None] * (
            scaled_grad - sum_plain[:, None] / D - scaled * sum_cross[:, None] / D
        )
        return (values_grad, jnp.sum(upstream * scaled, 0), jnp.sum(upstream, 0))

    def project_up(normed, weight):
        gathered = gather_tokens(normed)
        partial_sum = jnp.dot(gathered, weight, preferred_element_type=jnp.float32)
        return (gathered, sum_heads(partial_sum))

    def project_down(gathered, weight):

        def term(start, count):
            return jnp.dot(gathered, weight, preferred_element_type=jnp.float32)

        return sum_tokens(term)

    def back_down(upstream, gathered, weight):
        grad_group = gather_tokens(upstream.astype(jnp.bfloat16))
        weight_grad = contract_first(gathered, grad_group)
        partial_sum = contract_last(grad_group, weight)
        return (weight_grad, sum_heads(partial_sum))

    def back_up(grad_low, gathered, weight):
        grad_all = gather_heads(grad_low)
        weight_grad = contract_first(gathered, grad_all)

        def term(start, count):
            return contract_last(grad_all, weight)

        return (grad_all, weight_grad, sum_tokens(term))

    first_scaled, first_inverse, first_normed = norm_forward(inputs, first_gain, first_shift)
    first_rows, projected = project_up(first_normed, attend_weight)
    pair_width = heads_here * 2 * HD
    bias_pairs = (
        lax.dynamic_slice_in_dim(attend_bias, row_index * pair_width, pair_width)
        .astype(jnp.float32)
        .reshape(heads_here, 2, HD)
    )
    bias_full = jnp.stack(
        [bias_pairs[:, 0], jnp.zeros_like(bias_pairs[:, 0]), bias_pairs[:, 1]], 1
    ).reshape(-1)
    packed = (
        (projected + bias_full).astype(jnp.bfloat16).reshape(group_images, SEQ, heads_here, 3, HD)
    )
    mixed, log_totals = lax.map(attend_image, packed)
    mixed_rows = gather_heads(mixed.reshape(group_rows, heads_here * HD))
    middle = inputs + project_down(mixed_rows, output_weight) + output_bias.astype(jnp.float32)
    second_scaled, second_inverse, second_normed = norm_forward(middle, second_gain, second_shift)
    second_rows, before_part = project_up(second_normed, expand_weight)
    hidden_width = before_part.shape[1]
    expand_slice = lax.dynamic_slice_in_dim(
        expand_bias, row_index * hidden_width, hidden_width
    ).astype(jnp.float32)
    before = before_part + expand_slice
    hidden = jax.nn.gelu(before, approximate=False).astype(jnp.bfloat16)
    hidden_rows = gather_heads(hidden)
    final = project_down(hidden_rows, reduce_weight)
    block_output = (
        (middle + final + reduce_bias.astype(jnp.float32)) * valid_rows[:, None]
    ).astype(jnp.bfloat16)
    out_grad = output_grad.astype(jnp.float32) * valid_rows[:, None]
    reduce_bias_grad = jnp.sum(out_grad, 0)
    reduce_weight_grad, hidden_grad = back_down(out_grad, hidden_rows, reduce_weight)
    _, gelu_back = jax.vjp(partial(jax.nn.gelu, approximate=False), before)
    before_low = gelu_back(hidden_grad)[0].astype(jnp.bfloat16)
    before_all, expand_weight_grad, second_normed_grad = back_up(
        before_low, second_rows, expand_weight
    )
    expand_bias_grad = jnp.sum(before_all.astype(jnp.float32), 0)
    middle_part, second_gain_grad, second_shift_grad = norm_back(
        second_normed_grad, second_scaled, second_inverse, second_gain
    )
    middle_grad = out_grad + middle_part
    output_bias_grad = jnp.sum(middle_grad, 0)
    output_weight_grad, mixed_grad = back_down(middle_grad, mixed_rows, output_weight)
    mixed_low = mixed_grad.astype(jnp.bfloat16).reshape(group_images, SEQ, heads_here, HD)
    packed_low = lax.map(attend_image_back, (packed, mixed_low, log_totals)).reshape(
        group_rows, heads_here * 3 * HD
    )
    packed_all, attend_weight_grad, first_normed_grad = back_up(
        packed_low, first_rows, attend_weight
    )
    bias_sums = jnp.sum(packed_all.astype(jnp.float32), 0).reshape(-1, 3, HD)
    attend_bias_grad = jnp.stack([bias_sums[:, 0], bias_sums[:, 2]], 1).reshape(-1)
    input_part, first_gain_grad, first_shift_grad = norm_back(
        first_normed_grad, first_scaled, first_inverse, first_gain
    )
    input_grad = middle_grad + input_part
    return (
        block_output,
        input_grad,
        first_gain_grad,
        first_shift_grad,
        attend_weight_grad,
        attend_bias_grad,
        output_weight_grad,
        output_bias_grad,
        second_gain_grad,
        second_shift_grad,
        expand_weight_grad,
        expand_bias_grad,
        reduce_weight_grad,
        reduce_bias_grad,
    )


def body(
    block_input,
    image_valid,
    first_gain,
    first_shift,
    attend_weight,
    attend_bias,
    output_weight,
    output_bias,
    second_gain,
    second_shift,
    expand_weight,
    expand_bias,
    reduce_weight,
    reduce_bias,
    output_grad,
):
    results = grid_block(
        block_input,
        image_valid,
        first_gain,
        first_shift,
        attend_weight,
        attend_bias,
        output_weight,
        output_bias,
        second_gain,
        second_shift,
        expand_weight,
        expand_bias,
        reduce_weight,
        reduce_bias,
        output_grad,
    )
    (
        block_output,
        input_grad,
        first_gain_grad,
        first_shift_grad,
        attend_weight_grad,
        attend_bias_grad,
        output_weight_grad,
        output_bias_grad,
        second_gain_grad,
        second_shift_grad,
        expand_weight_grad,
        expand_bias_grad,
        reduce_weight_grad,
        reduce_bias_grad,
    ) = results
    shares = (
        lax.psum_scatter(
            attend_weight_grad.astype(jnp.bfloat16), "dp", scatter_dimension=0, tiled=True
        ).astype(jnp.float32),
        lax.psum_scatter(
            output_weight_grad.astype(jnp.bfloat16), "dp", scatter_dimension=1, tiled=True
        ).astype(jnp.float32),
        lax.psum_scatter(
            expand_weight_grad.astype(jnp.bfloat16), "dp", scatter_dimension=0, tiled=True
        ).astype(jnp.float32),
        lax.psum_scatter(
            reduce_weight_grad.astype(jnp.bfloat16), "dp", scatter_dimension=1, tiled=True
        ).astype(jnp.float32),
        lax.psum_scatter(
            attend_bias_grad.astype(jnp.bfloat16), "dp", scatter_dimension=0, tiled=True
        ).astype(jnp.float32),
        lax.psum_scatter(
            expand_bias_grad.astype(jnp.bfloat16), "dp", scatter_dimension=0, tiled=True
        ).astype(jnp.float32),
    )
    (
        attend_weight_grad,
        output_weight_grad,
        expand_weight_grad,
        reduce_weight_grad,
        attend_bias_grad,
        expand_bias_grad,
    ) = (
        lax.all_gather(shares[0].astype(jnp.bfloat16), "dp", axis=0, tiled=True).astype(
            jnp.float32
        ),
        lax.all_gather(shares[1].astype(jnp.bfloat16), "dp", axis=1, tiled=True).astype(
            jnp.float32
        ),
        lax.all_gather(shares[2].astype(jnp.bfloat16), "dp", axis=0, tiled=True).astype(
            jnp.float32
        ),
        lax.all_gather(shares[3].astype(jnp.bfloat16), "dp", axis=1, tiled=True).astype(
            jnp.float32
        ),
        lax.all_gather(shares[4].astype(jnp.bfloat16), "dp", axis=0, tiled=True).astype(
            jnp.float32
        ),
        lax.all_gather(shares[5].astype(jnp.bfloat16), "dp", axis=0, tiled=True).astype(
            jnp.float32
        ),
    )
    (
        first_gain_grad,
        first_shift_grad,
        output_bias_grad,
        second_gain_grad,
        second_shift_grad,
        reduce_bias_grad,
    ) = lax.psum(
        (
            first_gain_grad,
            first_shift_grad,
            output_bias_grad,
            second_gain_grad,
            second_shift_grad,
            reduce_bias_grad,
        ),
        ("dp", "col"),
    )
    return (
        block_output,
        input_grad,
        first_gain_grad,
        first_shift_grad,
        attend_weight_grad,
        attend_bias_grad,
        output_weight_grad,
        output_bias_grad,
        second_gain_grad,
        second_shift_grad,
        expand_weight_grad,
        expand_bias_grad,
        reduce_weight_grad,
        reduce_bias_grad,
    )


def solution(mesh):
    return jax.shard_map(
        body,
        mesh=mesh,
        in_specs=(
            P(("dp", "col"), "row"),
            P("dp"),
            P("row"),
            P("row"),
            P("row", "col"),
            P("col"),
            P("col", "row"),
            P("row"),
            P("row"),
            P("row"),
            P("row", "col"),
            P("col"),
            P("col", "row"),
            P("row"),
            P(("dp", "col"), "row"),
        ),
        out_specs=(
            P(("dp", "col"), "row"),
            P(("dp", "col"), "row"),
            P("row"),
            P("row"),
            P("row", "col"),
            P("col"),
            P("col", "row"),
            P("row"),
            P("row"),
            P("row"),
            P("row", "col"),
            P("col"),
            P("col", "row"),
            P("row"),
        ),
        check_vma=False,
    )
```

profile of v0, /device:TPU:0, one launch (start us, length us, event | category | flops | bytes accessed | tf_op | source)
XLA Modules:
  0.0 5356.9 jit_solution(5407980144849507353)
XLA Ops:
  80.5 625.2 %reduce-scatter.37.cloned.1.call-done = f32[768,9232]{1,0:T(8,128)} async-done(((f32[1536,9232]{1,0:T(8,128)}), f32[768,9232]{1,0:T(8,128)}) %reduce-scatter.37.cloned.1.call-update) | async-done | bytes 28360720
  814.8 100.0 %while.22 = (s32[]{:T(128)}, bf16[16,577,4,64]{1,3,2,0:T(8,128)(2,1)}, f32[16,4,577]{2,1,0:T(4,128)}, bf16[16,577,4,3,64]{1,4,2,3,0:T(8,128)(2,1)}, s32[]{:T(128)}) while((s32[]{:T(128)}, bf16[16,577,4,64]{1,3,2,0:T(8,128)(2,1)}, f32[16,4,577]{2,1,0:T(4,128)}, bf16[16,577,4,3,64]{1,4,2,3,0:T(8,128)(2,1)}, s32[]{:T(128)}) %tuple.67), condition=%wide.region_8.9_spmd, body=%wide.region_5.8_spmd.sunk | while | flops 353050112 | bytes 19794112 | solution.py:185
  932.0 119.4 %all-gather.16.cloned.1.call-done = bf16[9232,512]{0,1:T(8,128)(2,1)} async-done(((bf16[9232,256]{0,1:T(8,128)(2,1)}), bf16[9232,512]{0,1:T(8,128)(2,1)}) %all-gather.16.cloned.1.call-update) | async-done | bytes 9453584 | tf_op jit(solution)/shard_map/all_gather | solution.py:108
  1127.1 36.8 convolution_bitcast_fusion
  1164.3 32.1 convolution_bitcast_fusion.1
  1197.1 797.6 %reduce-scatter.41.cloned.1.call-done = f32[1024,9232]{1,0:T(8,128)} async-done(((f32[2048,9232]{1,0:T(8,128)}), f32[1024,9232]{1,0:T(8,128)}) %reduce-scatter.41.cloned.1.call-update) | async-done | bytes 37814288
  1994.7 38.0 copy.75
  2032.7 793.9 %reduce-scatter.39.cloned.1.call-done = f32[1024,9232]{1,0:T(8,128)} async-done(((f32[2048,9232]{1,0:T(8,128)}), f32[1024,9232]{1,0:T(8,128)}) %reduce-scatter.39.cloned.1.call-update) | async-done | bytes 37814288
  2826.6 37.7 copy.73
  2864.3 94.0 %add_convert_fusion = (bf16[9232,1024]{1,0:T(8,128)(2,1)}, f32[9232,1024]{1,0:T(8,128)}) fusion(f32[9232,1024]{1,0:T(8,128)} %copy.75, f32[9232,1024]{1,0:T(8,128)} %copy.73, f32[1024]{0:T(1024)S(1)} %dynamic-slice_convert_fusion), kind=kLoop, calls=%fused_computation.50 | loop fusion | flops 690110464 | bytes 132354048 | tf_op jit(solution)/shard_map/convert_element_type | solution.py:205
  2958.4 43.5 multiply_convert_fusion.1
  3002.0 394.3 %all-gather.24.cloned.1.call-done = bf16[9232,2048]{1,0:T(8,128)(2,1)} async-done(((bf16[9232,1024]{1,0:T(8,128)(2,1)}), bf16[9232,2048]{1,0:T(8,128)(2,1)}) %all-gather.24.cloned.1.call-update) | async-done | bytes 37814288 | tf_op jit(solution)/shard_map/all_gather | solution.py:108
  3396.3 33.8 fusion.62
  3430.6 405.0 %all-gather.20.cloned.1.call-done = bf16[9232,2048]{1,0:T(8,128)(2,1)} async-done(((bf16[9232,1024]{1,0:T(8,128)(2,1)}), bf16[9232,2048]{1,0:T(8,128)(2,1)}) %all-gather.20.cloned.1.call-update) | async-done | bytes 37814288 | tf_op jit(solution)/shard_map/all_gather | solution.py:108
  3969.0 213.9 %reduce-scatter.25.cloned.1.call-done = f32[9232,256]{1,0:T(8,128)} async-done(((f32[9232,512]{1,0:T(8,128)}), f32[9232,256]{1,0:T(8,128)}) %reduce-scatter.25.cloned.1.call-update) | async-done | bytes 9453584 | tf_op jit(solution)/shard_map/reduce_scatter | solution.py:111
  4216.6 190.3 %while.23 = (s32[]{:T(128)}, bf16[16,577,4,3,64]{1,4,2,3,0:T(8,128)(2,1)}, bf16[16,577,4,3,64]{1,4,2,3,0:T(8,128)(2,1)}, f32[16,4,577]{2,1,0:T(4,128)}, bf16[16,577,4,64]{1,3,2,0:T(8,128)(2,1)}, /*index=5*/s32[]{:T(128)}) while((s32[]{:T(128)}, bf16[16,577,4,3,64]{1,4,2,3,0:T(8,128)(2,1)}, bf16[16,577,4,3,64]{1,4,2,3,0:T(8,128)(2,1)}, ...), condition=%wide.region_25.26_spmd, body=%wide.region_23.25_spmd.sunk | while | flops 871673856 | bytes 48145688 | solution.py:217
  4509.3 273.8 %all-gather.28.cloned.1.call-done = bf16[9232,1536]{0,1:T(8,128)(2,1)} async-done(((bf16[9232,768]{0,1:T(8,128)(2,1)}), bf16[9232,1536]{0,1:T(8,128)(2,1)}) %all-gather.28.cloned.1.call-update) | async-done | bytes 28360720 | tf_op jit(solution)/shard_map/all_gather | solution.py:108
  4806.2 48.8 reduce-scatter.33.cloned.1.call-done
  4855.0 70.8 %reduce-scatter.35.cloned.1.call-done = bf16[2048,64]{0,1:T(8,128)(2,1)} async-done(((bf16[2048,512]{0,1:T(8,128)(2,1)}), bf16[2048,64]{0,1:T(8,128)(2,1)}) %reduce-scatter.35.cloned.1.call-update) | async-done | bytes 262160 | tf_op jit(solution)/shard_map/reduce_scatter | solution.py:307
  4939.6 54.0 %reduce-scatter.29.cloned.1.call-done = bf16[64,1536]{1,0:T(8,128)(2,1)} async-done(((bf16[512,1536]{1,0:T(8,128)(2,1)}), bf16[64,1536]{1,0:T(8,128)(2,1)}) %reduce-scatter.29.cloned.1.call-update) | async-done | bytes 196624 | tf_op jit(solution)/shard_map/reduce_scatter | solution.py:298
  5048.5 45.9 all-gather.34.cloned.1.call-done
  5098.5 60.6 %reduce-scatter.31.cloned.1.call-done = bf16[512,64]{0,1:T(8,128)(2,1)} async-done(((bf16[512,512]{0,1:T(8,128)(2,1)}), bf16[512,64]{0,1:T(8,128)(2,1)}) %reduce-scatter.31.cloned.1.call-update) | async-done | bytes 65552 | tf_op jit(solution)/shard_map/reduce_scatter | solution.py:301
  5159.1 32.0 all_gather.52
  5280.1 57.6 %all-reduce.2 = (f32[512]{0:T(512)}, f32[512]{0:T(512)}, f32[512]{0:T(512)}, f32[512]{0:T(512)}, f32[512]{0:T(512)}, /*index=5*/f32[512]{0:T(512)}) all-reduce(f32[512]{0:T(512)S(1)} %get-tuple-element.138, f32[512]{0:T(512)S(1)} %get-tuple-element.143, f32[512]{0:T(512)S(1)} %copy-done.21, ...), channel_id=1, replica_groups=mesh['dp'=8,'row'=2,'col'=2] {'dp','col'}, use_global_device_ids=true, to_apply=%region_32.33 | all-reduce | flops 3072 | bytes 24576 | tf_op jit(solution)/shard_map/psum | solution.py:351
  (423 shorter events, 1031.1 us)
Async XLA Ops:
  7.2 1157.1 %copy-start = (bf16[512,2048]{1,0:T(8,128)(2,1)S(1)}, bf16[512,2048]{1,0:T(8,128)(2,1)}, u32[]{:S(2)}) copy-start(bf16[512,2048]{1,0:T(8,128)(2,1)} %param.29) | copy-start | bytes 6291460
  7.2 44.9 all-gather.14.cloned.1.call-start
  29.9 675.8 %reduce-scatter.37.cloned.1.call-start = ((), (), s32[]{:S(2)}) async-start(), calls=%async_computation.32 | async-start | bytes 86114304
  79.4 971.9 %all-gather.16.cloned.1.call-start = ((), (), s32[]{:S(2)}) async-start(), calls=%async_computation.13 | async-start | bytes 14352384 | tf_op jit(solution)/shard_map/all_gather | solution.py:108
  931.8 167.8 %reduce-scatter.19.cloned.1.call-start = ((), (), s32[]{:S(2)}) async-start(), calls=%async_computation.14 | async-start | bytes 28360704 | tf_op jit(solution)/shard_map/reduce_scatter | solution.py:114
  1064.3 62.8 %all-gather.22.cloned.1.call-start = ((), (), s32[]{:S(2)}) async-start(), calls=%async_computation.18 | async-start | bytes 14180352 | tf_op jit(solution)/shard_map/all_gather | solution.py:105
  1070.2 94.0 %all-gather.18.cloned.1.call-start = ((), (), s32[]{:S(2)}) async-start(), calls=%async_computation.15 | async-start | bytes 14180352 | tf_op jit(solution)/shard_map/all_gather | solution.py:105
  1127.0 867.6 %reduce-scatter.41.cloned.1.call-start = ((), (), s32[]{:S(2)}) async-start(), calls=%async_computation.34 | async-start | bytes 114819072
  1164.0 1662.6 %reduce-scatter.39.cloned.1.call-start = ((), (), s32[]{:S(2)}) async-start(), calls=%async_computation.33 | async-start | bytes 114819072
  1196.4 2199.9 %all-gather.24.cloned.1.call-start = ((), (), s32[]{:S(2)}) async-start(), calls=%async_computation.19 | async-start | bytes 56721408 | tf_op jit(solution)/shard_map/all_gather | solution.py:108
  2958.4 877.2 %all-gather.20.cloned.1.call-start = ((), (), s32[]{:S(2)}) async-start(), calls=%async_computation.16 | async-start | bytes 56721408 | tf_op jit(solution)/shard_map/all_gather | solution.py:108
  3002.0 871.2 %reduce-scatter.23.cloned.1.call-start = ((), (), s32[]{:S(2)}) async-start(), calls=%async_computation.20 | async-start | bytes 28360704 | tf_op jit(solution)/shard_map/reduce_scatter | solution.py:114
  3430.1 481.7 %reduce-scatter.21.cloned.1.call-start = ((), (), s32[]{:S(2)}) async-start(), calls=%async_computation.17 | async-start | bytes 28360704 | tf_op jit(solution)/shard_map/reduce_scatter | solution.py:114
  3866.5 89.3 %all-gather.26.cloned.1.call-start = ((), (), s32[]{:S(2)}) async-start(), calls=%async_computation.21 | async-start | bytes 14180352 | tf_op jit(solution)/shard_map/all_gather | solution.py:105
  3932.6 250.3 %reduce-scatter.25.cloned.1.call-start = ((), (), s32[]{:S(2)}) async-start(), calls=%async_computation.22 | async-start | bytes 28360704 | tf_op jit(solution)/shard_map/reduce_scatter | solution.py:111
  3968.9 814.3 %all-gather.28.cloned.1.call-start = ((), (), s32[]{:S(2)}) async-start(), calls=%async_computation.23 | async-start | bytes 43057152 | tf_op jit(solution)/shard_map/all_gather | solution.py:108
  4448.0 407.0 %reduce-scatter.33.cloned.1.call-start = ((), (), s32[]{:S(2)}) async-start(), calls=%async_computation.28 | async-start | bytes 2359296 | tf_op jit(solution)/shard_map/reduce_scatter | solution.py:304
  4479.0 446.8 %reduce-scatter.35.cloned.1.call-start = ((), (), s32[]{:S(2)}) async-start(), calls=%async_computation.30 | async-start | bytes 2359296 | tf_op jit(solution)/shard_map/reduce_scatter | solution.py:307
  4508.9 484.7 %reduce-scatter.29.cloned.1.call-start = ((), (), s32[]{:S(2)}) async-start(), calls=%async_computation.25 | async-start | bytes 1769472 | tf_op jit(solution)/shard_map/reduce_scatter | solution.py:298
  4806.1 238.2 %all-gather.32.cloned.1.call-start = ((), (), s32[]{:S(2)}) async-start(), calls=%async_computation.29 | async-start | bytes 2359296 | tf_op jit(solution)/shard_map/all_gather | solution.py:331
  4855.0 239.4 %all-gather.34.cloned.1.call-start = ((), (), s32[]{:S(2)}) async-start(), calls=%async_computation.31 | async-start | bytes 2359296 | tf_op jit(solution)/shard_map/all_gather | solution.py:334
  4925.8 233.2 %reduce-scatter.31.cloned.1.call-start = ((), (), s32[]{:S(2)}) async-start(), calls=%async_computation.27 | async-start | bytes 589824 | tf_op jit(solution)/shard_map/reduce_scatter | solution.py:301
  4939.5 318.7 %all-gather.30.cloned.1.call-start = ((), (), s32[]{:S(2)}) async-start(), calls=%async_computation.26 | async-start | bytes 1769472 | tf_op jit(solution)/shard_map/all_gather | solution.py:325
  4993.6 268.1 %reduce-scatter.27.cloned.1.call-start = ((), (), s32[]{:S(2)}) async-start(), calls=%async_computation.24 | async-start | bytes 28360704 | tf_op jit(solution)/shard_map/reduce_scatter | solution.py:114
  (32 other events, 1143.3 us)
Sparse Core Ops, SparseCore 0:
  30.0 22.0 all-gather.13
  79.6 626.1 reduce-scatter.36
  931.9 119.4 all-gather.15
  1064.4 35.0 reduce-scatter.18
  1101.6 23.1 all-gather.21
  1127.2 22.4 all-gather.17
  1164.1 830.5 reduce-scatter.40
  1997.0 829.6 reduce-scatter.38
  2958.5 437.7 all-gather.23
  3397.8 437.7 all-gather.19
  3838.0 35.0 reduce-scatter.22
  3875.3 36.3 reduce-scatter.20
  3932.7 23.1 all-gather.25
  3969.0 213.8 reduce-scatter.24
  4448.1 335.0 all-gather.27
  4787.1 67.7 reduce-scatter.32
  4858.9 66.8 reduce-scatter.34
  4929.6 63.8 reduce-scatter.28
  4995.9 48.3 all-gather.31
  5046.5 47.7 all-gather.33
  5098.6 60.3 reduce-scatter.30
  5161.2 44.2 all-gather.29
  5207.9 34.2 reduce-scatter.26
where the time goes:
time: 5370 us; the launch traced here: 5360 us
  waiting for transfers between devices  4010 us (75%)
  matrix products  479 us (9%)
  other arithmetic  343 us (6%)
  local copies, waits for them, and re-layouts  321 us (6%)
  blocking collectives  180 us (3%)
    unnamed x26, waiting for transfers between devices  2220 us
    all_gather x4, waiting for transfers between devices, gather_heads(): return lax.all_gather(values, 'row', axis=1, tiled=True)  1190 us
    reduce_scatter x1, waiting for transfers between devices, sum_heads(): return lax.psum_scatter(values, 'row', scatter_dimension=1, tiled=True)  214 us
    unnamed x75, local copies, waits for them, and re-layouts  118 us
  transfers between devices with their start and end apart: 23, of which 19 were waited for; matrix products, arithmetic and copies ran while one was open for 8% of the time, Pallas kernels for 0%

commit v1 on v0

v1 whole, which is shorter than its diff:
```python
from functools import partial

import jax
import jax.numpy as jnp
from jax import lax
from jax.experimental import pallas as pl
from jax.experimental.pallas import tpu as pltpu
from jax.sharding import PartitionSpec as P

D = 1024
HD = 64
SEQ = 577
PAD = 592
EPSILON = 1e-06
BF = jnp.bfloat16
F32 = jnp.float32
LOG2E = 1.4426950408889634
ROOT_HALF = 0.7071067811865476
DENSITY = 0.3989422804014327
KEYS_A = 512
MEBI = 1 << 20


def dot_nn(left, right):
    return lax.dot_general(left, right, (((1,), (0,)), ((), ())), preferred_element_type=F32)


def dot_nt(left, right):
    return lax.dot_general(left, right, (((1,), (1,)), ((), ())), preferred_element_type=F32)


def dot_tn(left, right):
    return lax.dot_general(left, right, (((0,), (0,)), ((), ())), preferred_element_type=F32)


def whole(array):
    return pl.BlockSpec(array.shape, lambda *_: (0,) * array.ndim, pipeline_mode=pl.Buffered(1))


def by_image(width):
    return pl.BlockSpec((PAD, width), lambda i: (i, 0))


def call(kernel, name, grid, operands, outputs, macs, after=(), into=None):
    if into is not None:
        after = (into, *after)
    size = sum(a.size * a.dtype.itemsize for _, a in operands)
    size += sum(jnp.dtype(t).itemsize * s[0] * s[1] for _, s, t in outputs)
    used = len(operands)

    def body_of(*refs):
        kernel(*refs[:used], *refs[used + len(after) :])

    return pl.pallas_call(
        body_of,
        grid=grid,
        in_specs=[s for s, _ in operands] + [pl.BlockSpec(memory_space=pl.ANY)] * len(after),
        out_specs=[s for s, _, _ in outputs],
        out_shape=[jax.ShapeDtypeStruct(s, t) for _, s, t in outputs],
        compiler_params=pltpu.CompilerParams(vmem_limit_bytes=60 * MEBI),
        cost_estimate=pl.CostEstimate(flops=4 * macs, bytes_accessed=size, transcendentals=0),
        input_output_aliases={} if into is None else {used: 0},
        name=name,
    )(*[a for _, a in operands], *after)


def shift(values, axis, step):
    size = lax.axis_size(axis)
    return lax.ppermute(values, axis, [(i, (i + step) % size) for i in range(size)])


def gather_blocks(block, axis):
    return [block] + [shift(block, axis, -s) for s in range(1, lax.axis_size(axis))]


def gather_weight(weight):
    return [gather_blocks(block, "col") for block in gather_blocks(weight, "row")]


def fetch_shares(weight):
    depth = weight.shape[0] // lax.axis_size("dp")
    share = lax.dynamic_slice_in_dim(weight, lax.axis_index("dp") * depth, depth)
    return gather_blocks(share, "row")[1:]


def gather_shares(weight, shares):
    blocks = [weight] + [lax.all_gather(s, "dp", axis=0, tiled=True) for s in shares]
    return [gather_blocks(block, "col") for block in blocks]


def hold(values, after):
    return lax.optimization_barrier((values, after))[0]


def swap(values, axis, step):
    return lax.ppermute(values, axis, [(i, i ^ step) for i in range(lax.axis_size(axis))])


def steps_of(axis):
    steps = [1]
    while steps[-1] * 2 < lax.axis_size(axis):
        steps.append(steps[-1] * 2)
    return steps


def sum_all(values, axis):
    for step in steps_of(axis):
        values = values + swap(values, axis, step)
    return values


def halve(values, axis, step):
    half = values.shape[0] // 2
    bit = lax.axis_index(axis) // step % 2
    keep = lax.dynamic_slice_in_dim(values, bit * half, half)
    give = lax.dynamic_slice_in_dim(values, (1 - bit) * half, half)
    return (keep.astype(F32) + swap(give, axis, step).astype(F32)).astype(BF)


def join(values, axis, step):
    other = swap(values, axis, step)
    low = lax.axis_index(axis) // step % 2 == 0
    return jnp.where(low, jnp.concatenate([values, other]), jnp.concatenate([other, values]))


def finish_sum(values, axis):
    steps = steps_of(axis)
    for step in steps[1:]:
        values = halve(values, axis, step)
    for step in reversed(steps):
        values = join(values, axis, step)
    return values


def pack_kernel(place_ref, x_ref, *refs):
    o_refs = refs[-lax.axis_size("row") :]
    images = o_refs[0].shape[0] // PAD
    for place in range(len(o_refs)):

        @pl.when(place_ref[0] == place)
        def _(place=place):
            for s, o_ref in enumerate(o_refs):
                at = (place - s) % len(o_refs) * images
                for i in range(images):
                    rows = x_ref[(at + i) * SEQ : (at + i + 1) * SEQ]
                    o_ref[i * PAD : i * PAD + SEQ] = rows
                    rest = (PAD - SEQ, x_ref.shape[1])
                    o_ref[i * PAD + SEQ : (i + 1) * PAD] = jnp.zeros(rest, x_ref.dtype)


def pack_rows(values, place, after=()):
    rows, width = values.shape
    parts = lax.axis_size("row")
    vmem = pl.BlockSpec(memory_space=pltpu.VMEM)
    part = jax.ShapeDtypeStruct((rows // SEQ // parts * PAD, width), values.dtype)
    return pl.pallas_call(
        pack_kernel,
        in_specs=[pl.BlockSpec(memory_space=pltpu.SMEM), vmem]
        + [pl.BlockSpec(memory_space=pl.ANY)] * len(after),
        out_specs=[vmem] * parts,
        out_shape=[part] * parts,
        compiler_params=pltpu.CompilerParams(vmem_limit_bytes=60 * MEBI),
        cost_estimate=pl.CostEstimate(flops=0, bytes_accessed=8 * values.size, transcendentals=0),
        name="pack_rows",
    )(place.reshape(1), values, *after)


def unpack_kernel(counts, place_ref, *refs):
    o_ref = refs[-1]
    for place in range(len(counts)):

        @pl.when(place_ref[0] == place)
        def _(place=place):
            n = 0
            for s, some in enumerate(counts):
                at = (place - s) % len(counts) * sum(some)
                for count in some:
                    for i in range(count):
                        rows = refs[n][i * PAD : i * PAD + SEQ].astype(o_ref.dtype)
                        o_ref[at * SEQ : (at + 1) * SEQ] = rows
                        at += 1
                    n += 1


def unpack_rows(parts, place, dtype):
    counts = tuple(tuple(a.shape[0] // PAD for a in some) for some in parts)
    arrays = [a for some in parts for a in some]
    vmem = pl.BlockSpec(memory_space=pltpu.VMEM)
    return pl.pallas_call(
        partial(unpack_kernel, counts),
        in_specs=[pl.BlockSpec(memory_space=pltpu.SMEM)] + [vmem] * len(arrays),
        out_specs=vmem,
        out_shape=jax.ShapeDtypeStruct(
            (sum(map(sum, counts)) * SEQ, arrays[0].shape[1]), dtype
        ),
        compiler_params=pltpu.CompilerParams(vmem_limit_bytes=60 * MEBI),
        cost_estimate=pl.CostEstimate(
            flops=0, bytes_accessed=16 * len(parts) * arrays[0].size, transcendentals=0
        ),
        name="unpack_rows",
    )(place.reshape(1), *arrays)


def row_mean(blocks):
    return sum(jnp.sum(b, 1, keepdims=True) for b in blocks) / (len(blocks) * blocks[0].shape[1])


def normalize(blocks):
    center = row_mean(blocks)
    inverse = lax.rsqrt(row_mean([b * b for b in blocks]) - center * center + EPSILON)
    return [(b - center) * inverse for b in blocks], inverse


def norm_back(upstream, scaled, inverse, gains):
    grads = [u * g for u, g in zip(upstream, gains)]
    plain = row_mean(grads)
    cross = row_mean([g * x for g, x in zip(grads, scaled)])
    return [inverse * (g - plain - x * cross) for g, x in zip(grads, scaled)]


def cut(values, width):
    return [values[:, at : at + width] for at in range(0, values.shape[1], width)]


def add_rows(ref, values, at=0):
    ref[:, at : at + values.shape[1]] += jnp.sum(values, 0, keepdims=True)


def grid_of(refs, shape):
    outer, inner = shape
    return [refs[i * inner : (i + 1) * inner] for i in range(outer)]


def project_kernel(shape, gain_ref, shift_ref, bias_ref, *refs):
    rows, cols = shape
    x_refs, weights = refs[:rows], grid_of(refs[rows : rows + rows * cols], shape)
    normed_ref, packed_ref = refs[rows + rows * cols :]
    scaled, _ = normalize([x[...].astype(F32) for x in x_refs])
    width = scaled[0].shape[1]
    gains, shifts = cut(gain_ref[...], width), cut(shift_ref[...], width)
    normed = [(x * g + b).astype(BF) for x, g, b in zip(scaled, gains, shifts)]
    for i, n in enumerate(normed):
        normed_ref[:, i * width : (i + 1) * width] = n
    block = weights[0][0].shape[1]
    for j in range(cols):
        total = sum(dot_nn(n, weights[i][j][...]) for i, n in enumerate(normed))
        where = slice(j * block, (j + 1) * block)
        packed_ref[:, where] = (total + bias_ref[:, where]).astype(BF)


def swap_halves(values):
    return jnp.concatenate([values[:, HD:], values[:, :HD]], 1)


def attend_kernel(p_ref, o_ref):
    first, second, third = p_ref[:, :128], p_ref[:, 128:256], p_ref[:, 256:]
    low = lax.broadcasted_iota(jnp.int32, (1, 128), 1) < HD
    zero, one = jnp.zeros((), BF), jnp.ones((), BF)
    queries = (jnp.where(low, first, zero), jnp.where(low, swap_halves(second), zero))
    keys = (swap_halves(first), third)
    values = (jnp.where(low, second, one), jnp.where(low, one, third))
    scale = HD**-0.5 * LOG2E
    keep = lax.broadcasted_iota(jnp.int32, (1, PAD - KEYS_A), 1) < SEQ - KEYS_A
    chunk = PAD // 2
    for start in range(0, PAD, chunk):
        outs = []
        for h in range(2):
            query = queries[h][start : start + chunk]
            sa = dot_nt(query, keys[h][:KEYS_A])
            sb = jnp.where(keep, dot_nt(query, keys[h][KEYS_A:]), -1e30)
            top = jnp.maximum(jnp.max(sa, 1, keepdims=True), jnp.max(sb, 1, keepdims=True))
            top = top * scale
            pa = jnp.exp2(sa * scale - top).astype(BF)
            pb = jnp.exp2(sb * scale - top).astype(BF)
            outs.append(dot_nn(pa, values[h][:KEYS_A]) + dot_nn(pb, values[h][KEYS_A:]))
        mixed, totals = jnp.where(low, outs[0], outs[1]), jnp.where(low, outs[1], outs[0])
        o_ref[start : start + chunk, :] = (mixed / swap_halves(totals)).astype(BF)


def attend(packed, after):
    tokens, width = packed.shape
    pairs = width // (6 * HD)
    return call(
        attend_kernel,
        "attend",
        (pairs, tokens // PAD),
        [(pl.BlockSpec((PAD, 6 * HD), lambda h, i: (i, h)), packed)],
        [(pl.BlockSpec((PAD, 2 * HD), lambda h, i: (i, h)), (tokens, pairs * 2 * HD), BF)],
        tokens * PAD * pairs * 2 * HD * 13,
        after,
    )[0]


def attend_back_kernel(p_ref, g_ref, o_ref):
    first, second, third = p_ref[:, :128], p_ref[:, 128:256], p_ref[:, 256:]
    grad = g_ref[...]
    low = lax.broadcasted_iota(jnp.int32, (1, 128), 1) < HD
    zero = jnp.zeros((), BF)
    turned = [swap_halves(v) for v in (first, second, third)]
    queries = (jnp.where(low, first, zero), jnp.where(low, turned[1], zero))
    keys, values = (turned[0], third), (second, third)
    grads = (jnp.where(low, grad, zero), jnp.where(low, zero, grad))
    query_right = (turned[0], turned[1])
    key_right = (turned[0], turned[2])
    scale = HD**-0.5
    edge = PAD - 16
    keep = lax.broadcasted_iota(jnp.int32, (PAD - edge, 1), 0) < SEQ - edge
    value_grad, key_grad, query_grad = [0.0, 0.0], [0.0, 0.0], [[], []]
    for start in range(0, PAD, 256):
        some = slice(start, min(PAD, start + 256))
        for h in range(2):
            scores = dot_nt(keys[h], queries[h][some])
            weight_grad = dot_nt(values[h], grads[h][some])
            sa, sb = scores[:edge], jnp.where(keep, scores[edge:], -1e30)
            top = jnp.maximum(jnp.max(sa, 0, keepdims=True), jnp.max(sb, 0, keepdims=True))
            top = top * (scale * LOG2E)
            weights = jnp.concatenate(
                [jnp.exp2(s * (scale * LOG2E) - top) for s in (sa, sb)], 0
            )
            weights = weights * (1.0 / jnp.sum(weights, 0, keepdims=True))
            product = weights * weight_grad
            score_low = (product - weights * jnp.sum(product, 0, keepdims=True)).astype(BF)
            value_grad[h] += dot_nn(weights.astype(BF), grad[some])
            key_grad[h] += dot_nn(score_low, query_right[h][some])
            query_grad[h].append(dot_tn(score_low, key_right[h]))
    query_grad = [jnp.concatenate(q, 0) for q in query_grad]
    o_ref[:, :128] = (jnp.where(low, query_grad[0], key_grad[0]) * scale).astype(BF)
    o_ref[:, 128:256] = jnp.where(low, value_grad[0], query_grad[1] * scale).astype(BF)
    o_ref[:, 256:] = jnp.where(low, key_grad[1] * scale, value_grad[1]).astype(BF)


def attend_back(packed, grad, cols, pair, slot, slots, into, after):
    tokens, width = packed.shape
    block = width // (6 * HD) // cols
    return call(
        attend_back_kernel,
        "attend_back",
        (cols, tokens // PAD),
        [
            (pl.BlockSpec((PAD, 6 * HD), lambda j, i: (i, j * block + pair)), packed),
            (pl.BlockSpec((PAD, 2 * HD), lambda j, i: (i, j * block + pair)), grad),
        ],
        [
            (
                pl.BlockSpec((PAD, 6 * HD), lambda j, i: (i, j * slots + slot)),
                (tokens, cols * slots * 6 * HD),
                BF,
            )
        ],
        tokens * PAD * cols * 2 * HD * 32,
        after,
        into,
    )[0]


def output_kernel(shape, bias_ref, gain_ref, shift_ref, mixed_ref, *refs):
    rows, cols = shape
    x_refs, weights = refs[:rows], grid_of(refs[rows : rows + rows * cols], shape)
    middle_ref, normed_ref = refs[rows + rows * cols :]
    block, width = weights[0][0].shape
    mixed = cut(mixed_ref[...], block)
    middle = []
    for i in range(rows):
        total = sum(dot_nn(m, weights[i][j][...]) for j, m in enumerate(mixed))
        where = slice(i * width, (i + 1) * width)
        middle.append(x_refs[i][...].astype(F32) + total + bias_ref[:, where])
        middle_ref[:, where] = middle[-1]
    scaled, _ = normalize(middle)
    for i, x in enumerate(scaled):
        where = slice(i * width, (i + 1) * width)
        normed_ref[:, where] = (x * gain_ref[:, where] + shift_ref[:, where]).astype(BF)


def expand_kernel(shape, bias_ref, normed_ref, *refs):
    rows, cols = shape
    weights = grid_of(refs[: rows * cols], shape)
    hidden_ref, slope_ref = refs[rows * cols :]
    depth, block = weights[0][0].shape
    normed = cut(normed_ref[...], depth)
    for j in range(cols):
        total = sum(dot_nn(n, weights[i][j][...]) for i, n in enumerate(normed))
        where = slice(j * block, (j + 1) * block)
        before = total + bias_ref[:, where]
        below = 0.5 + 0.5 * lax.erf(before * ROOT_HALF)
        hidden_ref[:, where] = (before * below).astype(BF)
        density = jnp.exp2(before * before * (-0.5 * LOG2E)) * DENSITY
        slope_ref[:, where] = (below + before * density).astype(BF)


def reduce_kernel(shape, valid_ref, bias_ref, hidden_ref, middle_ref, *refs):
    rows, cols = shape
    weights, o_refs = grid_of(refs[: rows * cols], shape), refs[rows * cols :]
    block, width = weights[0][0].shape
    valid = valid_ref[pl.program_id(0)].astype(F32)
    for i in range(rows):
        total = sum(
            dot_nn(hidden_ref[:, j * block : (j + 1) * block], weights[i][j][...])
            for j in range(cols)
        )
        where = slice(i * width, (i + 1) * width)
        o_refs[i][...] = ((middle_ref[:, where] + total + bias_ref[:, where]) * valid).astype(BF)


def reduce_back_kernel(shape, valid_ref, slope_ref, *refs):
    rows, cols = shape
    g_refs, weights = refs[:rows], grid_of(refs[rows : rows + rows * cols], shape)
    out_low_ref, before_ref, reduce_bias_ref, expand_bias_ref = refs[rows + rows * cols :]

    @pl.when(pl.program_id(0) == 0)
    def _():
        reduce_bias_ref[...] = jnp.zeros_like(reduce_bias_ref)
        expand_bias_ref[...] = jnp.zeros_like(expand_bias_ref)

    valid = valid_ref[pl.program_id(0)].astype(F32)
    block, width = weights[0][0].shape
    lows = []
    for i, g in enumerate(g_refs):
        grad = g[...].astype(F32) * valid
        add_rows(reduce_bias_ref, grad, i * width)
        lows.append(grad.astype(BF))
        out_low_ref[:, i * width : (i + 1) * width] = lows[-1]
    for j in range(cols):
        total = sum(dot_nt(low, weights[i][j][...]) for i, low in enumerate(lows))
        where = slice(j * block, (j + 1) * block)
        total = total * slope_ref[:, where].astype(F32)
        add_rows(expand_bias_ref, total, j * block)
        before_ref[:, where] = total.astype(BF)


def expand_back_kernel(shape, gain_ref, before_ref, middle_ref, out_low_ref, *refs):
    rows, cols = shape
    count = rows * cols
    expand, output = grid_of(refs[:count], shape), grid_of(refs[count : 2 * count], shape)
    middle_grad_ref, middle_low_ref, mixed_low_ref, gain_grad, shift_grad, bias_grad = refs[2 * count :]

    @pl.when(pl.program_id(0) == 0)
    def _():
        for ref in (gain_grad, shift_grad, bias_grad):
            ref[...] = jnp.zeros_like(ref)

    width, block = expand[0][0].shape
    upstream = [
        sum(dot_nt(before_ref[:, j * block : (j + 1) * block], expand[i][j][...]) for j in range(cols))
        for i in range(rows)
    ]
    scaled, inverse = normalize(cut(middle_ref[...], width))
    parts = norm_back(upstream, scaled, inverse, cut(gain_ref[...], width))
    lows = []
    for i, part in enumerate(parts):
        where = slice(i * width, (i + 1) * width)
        add_rows(gain_grad, upstream[i] * scaled[i], i * width)
        add_rows(shift_grad, upstream[i], i * width)
        grad = out_low_ref[:, where].astype(F32) + part
        add_rows(bias_grad, grad, i * width)
        middle_grad_ref[:, where] = grad
        lows.append(grad.astype(BF))
        middle_low_ref[:, where] = lows[-1]
    heads = output[0][0].shape[0]
    for j in range(cols):
        total = sum(dot_nt(low, output[i][j][...]) for i, low in enumerate(lows))
        mixed_low_ref[:, j * heads : (j + 1) * heads] = total.astype(BF)


def project_back_kernel(shape, parts, gain_ref, middle_ref, *refs):
    rows, cols = shape
    packed, refs = refs[:parts], refs[parts:]
    x_refs, weights = refs[:rows], grid_of(refs[rows : rows + rows * cols], shape)
    refs = refs[rows + rows * cols :]
    o_refs, (gain_grad, shift_grad), bias_grads = refs[:rows], refs[rows : rows + 2], refs[rows + 2 :]

    @pl.when(pl.program_id(0) == 0)
    def _():
        for ref in refs[rows:]:
            ref[...] = jnp.zeros_like(ref)

    width = weights[0][0].shape[0]
    upstream = [0.0] * rows
    at = 0
    for p in range(parts):
        add_rows(bias_grads[p], packed[p][...].astype(F32))
        some = packed[p].shape[1] // cols
        for j in range(cols):
            grad = packed[p][:, j * some : (j + 1) * some]
            for i in range(rows):
                upstream[i] += dot_nt(grad, weights[i][j][:, at : at + some])
        at += some
    scaled, inverse = normalize([x[...].astype(F32) for x in x_refs])
    grads = norm_back(upstream, scaled, inverse, cut(gain_ref[...], width))
    for i, grad in enumerate(grads):
        add_rows(gain_grad, upstream[i] * scaled[i], i * width)
        add_rows(shift_grad, upstream[i], i * width)
        total = middle_ref[:, i * width : (i + 1) * width] + grad
        o_refs[i][...] = total.astype(o_refs[i].dtype)


def outer_kernel(a_ref, b_ref, o_ref):
    o_ref[...] = dot_tn(a_ref[...], b_ref[...]).astype(o_ref.dtype)


def outer(left, right, left_part, right_part, name, after=()):
    tokens = left.shape[0]
    (li, lw), (ri, rw) = left_part, right_part
    bl, br = min(lw, 1024), 1024 if rw % 1024 == 0 else rw
    return call(
        outer_kernel,
        name,
        (lw // bl, rw // br),
        [
            (pl.BlockSpec((tokens, bl), lambda i, j: (0, li * (lw // bl) + i)), left),
            (pl.BlockSpec((tokens, br), lambda i, j: (0, ri * (rw // br) + j)), right),
        ],
        [(pl.BlockSpec((bl, br), lambda i, j: (i, j)), (lw, rw), BF)],
        tokens * lw * rw,
        after,
    )[0]


def body(
    block_input,
    image_valid,
    first_gain,
    first_shift,
    attend_weight,
    attend_bias,
    output_weight,
    output_bias,
    second_gain,
    second_shift,
    expand_weight,
    expand_bias,
    reduce_weight,
    reduce_bias,
    output_grad,
):
    rows, cols = lax.axis_size("row"), lax.axis_size("col")
    row_index, col_index = lax.axis_index("row"), lax.axis_index("col")
    local_rows, width = block_input.shape
    local_images = local_rows // SEQ
    images = local_images // rows
    tokens = images * PAD
    hidden_width = expand_weight.shape[1] * cols
    shape = (rows, cols)
    step = (images,)

    def to_tokens(values, after=()):
        parts = pack_rows(values, row_index, after)
        return [shift(part, "row", -s) if s else part for s, part in enumerate(parts)]

    def from_tokens(parts, dtype):
        parts = [[shift(a, "row", s) if s else a for a in some] for s, some in enumerate(parts)]
        return unpack_rows(parts, row_index, dtype)

    features = jnp.stack(
        [first_gain, first_shift, output_bias, second_gain, second_shift, reduce_bias]
    )
    features = jnp.concatenate(gather_blocks(features, "row"), 1).astype(F32)
    first_gain, first_shift, output_bias, second_gain, second_shift, reduce_bias = jnp.split(
        features, 6, 0
    )
    biases = jnp.stack(gather_blocks(jnp.concatenate([attend_bias, expand_bias]), "col"))
    biases = biases.astype(F32)
    pairs = biases[:, : attend_bias.shape[0]].reshape(-1, 2, HD)
    attend_bias = jnp.stack([pairs[:, 0], jnp.zeros_like(pairs[:, 0]), pairs[:, 1]], 1)
    attend_bias = attend_bias.reshape(1, 3 * D)
    expand_bias = biases[:, -expand_bias.shape[0] :].reshape(1, -1)
    valid = lax.dynamic_slice_in_dim(
        image_valid, col_index * local_images + row_index * images, images
    )

    inputs = to_tokens(block_input)
    attend_blocks = gather_shares(attend_weight, hold(fetch_shares(attend_weight), inputs[0]))
    expand_shares = fetch_shares(hold(expand_weight, inputs[0]))
    output_blocks = gather_weight(hold(output_weight, inputs))

    def flat(blocks):
        return [(whole(b), b) for some in blocks for b in some]

    def row_blocks(arrays):
        return [(by_image(width), a) for a in arrays]

    def full(array):
        return (whole(array), array)

    def image(array):
        return (by_image(array.shape[1]), array)

    def out(columns, dtype):
        return (by_image(columns), (tokens, columns), dtype)

    def total(columns):
        return (pl.BlockSpec((1, columns), lambda i: (0, 0)), (1, columns), F32)

    scalars = (pl.BlockSpec(memory_space=pltpu.SMEM), valid)

    first_normed, packed = call(
        partial(project_kernel, shape),
        "project",
        step,
        [full(first_gain), full(first_shift), full(attend_bias)]
        + row_blocks(inputs)
        + flat(attend_blocks),
        [out(D, BF), out(3 * D, BF)],
        tokens * 3 * D * D,
    )
    grads = to_tokens(output_grad, (packed,))
    expand_blocks = gather_shares(expand_weight, expand_shares)
    reduce_shares = fetch_shares(hold(reduce_weight, packed))
    mixed = attend(packed, (*expand_shares, *reduce_shares, *output_blocks[-1], grads[0]))
    reduce_blocks = gather_shares(reduce_weight, hold(reduce_shares, mixed))
    middle, second_normed = call(
        partial(output_kernel, shape),
        "output",
        step,
        [full(output_bias), full(second_gain), full(second_shift), image(mixed)]
        + row_blocks(inputs)
        + flat(output_blocks),
        [out(D, F32), out(D, BF)],
        tokens * D * D,
    )
    hidden, slope = call(
        partial(expand_kernel, shape),
        "expand",
        step,
        [full(expand_bias), image(second_normed)] + flat(expand_blocks),
        [out(hidden_width, BF), out(hidden_width, BF)],
        tokens * D * hidden_width,
    )
    out_low, before_low, reduce_bias_grad, expand_bias_grad = call(
        partial(reduce_back_kernel, shape),
        "reduce_back",
        step,
        [scalars, image(slope)] + row_blocks(grads) + flat(reduce_blocks),
        [out(D, BF), out(hidden_width, BF), total(D), total(hidden_width)],
        tokens * D * hidden_width,
    )

    def add_parts(parts, axis, after=None):
        held = parts[0].astype(F32)
        others = [shift(part, axis, s) for s, part in enumerate(parts) if s]
        for other in others if after is None else hold(others, after):
            held = held + other.astype(F32)
        return held

    def outer_parts(left, right, over_left, name, after=()):
        lw, rw = left.shape[1], right.shape[1]
        parts = []
        for j in reversed(range(cols)):
            places = ((j, lw // cols), (0, rw)) if over_left else ((0, lw), (j, rw // cols))
            parts.insert(0, outer(left, right, *places, name, parts[:1] or after))
        return parts

    def share_of(held, dim, after=None):
        return add_parts(jnp.split(held, rows, dim), "row", after).astype(BF)

    reduce_held = add_parts(outer_parts(hidden, out_low, True, "reduce_outer"), "col").astype(BF)
    reduce_share = share_of(reduce_held, 1)
    middle_grad, middle_low, mixed_low, second_gain_grad, second_shift_grad, output_bias_grad = call(
        partial(expand_back_kernel, shape),
        "expand_back",
        step,
        [full(second_gain), image(before_low), image(middle), image(out_low)]
        + flat(expand_blocks)
        + flat(output_blocks),
        [out(D, F32), out(D, BF), out(D, BF), total(D), total(D), total(D)],
        tokens * D * (hidden_width + D),
        (reduce_held,),
    )
    expand_held = outer_parts(second_normed, before_low, False, "expand_outer")
    expand_held = add_parts(expand_held, "col").astype(BF)
    output_held = outer_parts(mixed, middle_low, True, "output_outer", (reduce_share,))
    output_held = add_parts(output_held, "col").astype(BF)
    results = call(
        partial(reduce_kernel, shape),
        "reduce",
        step,
        [scalars, full(reduce_bias), image(hidden), image(middle)] + flat(reduce_blocks),
        [out(width, BF)] * rows,
        tokens * D * hidden_width,
        (expand_held, output_held),
    )
    block_output = from_tokens([[r] for r in results], BF)

    expand_share = share_of(expand_held, 0, results[0])
    output_share = share_of(output_held, 1, results[0])
    reduce_weight_grad = lax.psum(reduce_share, "dp")
    expand_weight_grad, output_weight_grad = lax.psum(
        hold((expand_share, output_share), reduce_weight_grad), "dp"
    )
    pairs = 3 * D // (6 * HD) // cols
    counts = [pairs - 2, 1, 1] if pairs > 2 else [pairs]
    packed_lows, held, shares, halved, pair = [], [], [], [], 0
    ready = results[:1]
    for g, count in enumerate(counts):
        packed_low = None
        for slot in range(count):
            packed_low = attend_back(
                packed, mixed_low, cols, pair, slot, count, packed_low, ready
            )
            ready = (expand_share, output_share, reduce_weight_grad) if pair == 0 else ()
            pair += 1
        packed_lows.append(packed_low)
        parts = outer_parts(first_normed, packed_low, False, "project_outer")
        held.append(add_parts(parts, "col").astype(BF))
        shares.append(share_of(held[-1], 0))
        halved.append(halve(shares[-1], "dp", 1))
        ready = (held[g],)
        ready += (shares[g - 1], expand_weight_grad) if g > 0 else ()
    late = jnp.concatenate(halved[:-1], 1) if len(counts) > 1 else halved[0]
    late = finish_sum(hold(late, held[-1]), "dp")
    attend_weight_grad = [late, finish_sum(halved[-1], "dp")] if len(counts) > 1 else [late]
    attend_weight_grad = jnp.concatenate(attend_weight_grad, 1)

    halves = 2 if images % 2 == 0 else 1
    some = images // halves
    input_grads, sums = [], 0.0
    for half in range(halves):

        def later(array):
            place = half * some
            spec = pl.BlockSpec((PAD, array.shape[1]), lambda i: (i + place, 0))
            return (spec, array)

        def here(dtype):
            return (by_image(width), (some * PAD, width), dtype)

        results = call(
            partial(project_back_kernel, shape, len(counts)),
            "project_back",
            (some,),
            [full(first_gain), later(middle_grad)]
            + [later(p) for p in packed_lows]
            + [later(x) for x in inputs]
            + flat(attend_blocks),
            [here(F32)]
            + [here(BF)] * (rows - 1)
            + [total(D), total(D)]
            + [total(p.shape[1]) for p in packed_lows],
            some * PAD * 3 * D * D,
            ready,
        )
        input_grads.append(results[:rows])
        ready = (results[0], shares[-1])
        packed_sums = [v.reshape(cols, -1, 3, HD) for v in results[rows + 2 :]]
        late = (*results[rows : rows + 2], jnp.concatenate(packed_sums, 1))
        sums = late if half == 0 else jax.tree.map(jnp.add, sums, late)
    input_grad = from_tokens(list(zip(*input_grads)), F32)
    first_gain_grad, first_shift_grad, packed_sums = sums

    feature_grads = jnp.concatenate(
        [
            first_gain_grad,
            first_shift_grad,
            output_bias_grad,
            second_gain_grad,
            second_shift_grad,
            reduce_bias_grad,
        ]
    )
    attend_bias_grad = jnp.stack([packed_sums[:, :, 0], packed_sums[:, :, 2]], 2)
    attend_bias_grad = attend_bias_grad.reshape(cols, -1)
    bias_grads = jnp.concatenate([attend_bias_grad, expand_bias_grad.reshape(cols, -1)], 1)
    bias_grads = add_parts(list(bias_grads), "col")
    feature_grads = sum_all(feature_grads.reshape(-1), "col")
    small = sum_all(jnp.concatenate([feature_grads, bias_grads]), "dp")
    feature_grads, bias_grads = small[: 6 * D].reshape(6, D), small[6 * D :]
    feature_grads = add_parts(jnp.split(feature_grads, rows, 1), "row")
    bias_grads = sum_all(bias_grads, "row")
    split = attend_bias_grad.shape[1]
    return (
        block_output,
        input_grad,
        feature_grads[0],
        feature_grads[1],
        attend_weight_grad.astype(F32),
        bias_grads[:split],
        output_weight_grad.astype(F32),
        feature_grads[2],
        feature_grads[3],
        feature_grads[4],
        expand_weight_grad.astype(F32),
        bias_grads[split:],
        reduce_weight_grad.astype(F32),
        feature_grads[5],
    )


def solution(mesh):
    tokens = P(("dp", "col"), "row")
    by_row, by_col = P("row"), P("col")
    up, down = P("row", "col"), P("col", "row")
    params = (by_row, by_row, up, by_col, down, by_row, by_row, by_row, up, by_col, down, by_row)
    return jax.shard_map(
        body,
        mesh=mesh,
        in_specs=(tokens, P("dp")) + params + (tokens,),
        out_specs=(tokens, tokens) + params,
        check_vma=False,
    )
```

time: 5370 us -> 922 us (0.17)
  waiting for transfers between devices: 4010 us -> 202 us
  Pallas kernels: 0 us -> 586 us
  matrix products: 479 us -> 0 us
  local copies, waits for them, and re-layouts: 321 us -> 20.3 us
  other arithmetic: 343 us -> 51.5 us
  blocking collectives: 180 us -> 0 us
    unnamed x26 -> x5, waiting for transfers between devices: 2220 us -> 0.08 us
    all_gather x11 -> x3, waiting for transfers between devices: 1290 us -> 72.2 us  [gather_shares(): lax.all_gather(s, 'dp', axis=0, tiled=True)]
    pallas_call x0 -> x29, Pallas kernels: none -> 586 us  [the longest x25 562 us: call(): pl.pallas_call(body_of, grid=grid, in_specs=[s for s, _ in operands] + [p...]
    reduce_scatter x9 -> x0, waiting for transfers between devices: 502 us -> none  [the longest x1 214 us: sum_heads(): return lax.psum_scatter(values, 'row', scatter_dimension=1, tiled=True)]
    dot_general x121 -> x0, matrix products: 383 us -> none  [the longest x4 97.1 us: contract_first(): lax.dot_general(left, right, (((0,), (0,)), ((), ())), preferred_element_...]
    convert_element_type x36 -> x25, other arithmetic: 215 us -> 43.2 us  [the longest x6 12.6 us: share_of(): return add_parts(jnp.split(held, rows, dim), 'row', after).astype(BF)]
    unnamed x75 -> x80, local copies, waits for them, and re-layouts: 118 us -> 9.04 us
    unnamed x3 -> x0, matrix products: 96.2 us -> none
  transfers between devices with their start and end apart: 23 -> 56, of which waited for: 19 -> 23; matrix products, arithmetic and copies ran while one was open for 8% -> 7% of each run, Pallas kernels for 0% -> 53%
where the time goes in v1:
time: 922 us; the launch traced here: 915 us
  Pallas kernels  586 us (64%)
  waiting for transfers between devices  202 us (22%)
  other arithmetic  51.5 us (6%)
  starting transfers between devices  40.1 us (4%)
  local copies, waits for them, and re-layouts  20.3 us (2%)
  between operations  14.7 us (2%)
    pallas_call x25, Pallas kernels, call(): pl.pallas_call(body_of, grid=grid, in_specs=[s for s, _ in operands] + [p...  562 us
    all_gather x3, waiting for transfers between devices, gather_shares(): lax.all_gather(s, 'dp', axis=0, tiled=True)  72.2 us
    ppermute x33, waiting for transfers between devices, shift(): lax.ppermute(values, axis, [(i, (i + step) % size) for i in range(size)])  52.3 us
    ppermute x18, waiting for transfers between devices, swap(): lax.ppermute(values, axis, [(i, i ^ step) for i in range(lax.axis_size(ax...  36.8 us
    psum x1, waiting for transfers between devices, body(): lax.psum(hold((expand_share, output_share), reduce_weight_grad), 'dp')  34 us
    ppermute x33, starting transfers between devices, shift(): lax.ppermute(values, axis, [(i, (i + step) % size) for i in range(size)])  22.5 us
  transfers between devices with their start and end apart: 56, of which 23 were waited for; matrix products, arithmetic and copies ran while one was open for 7% of the time, Pallas kernels for 53%

profile of v1, /device:TPU:0, one launch (start us, length us, event | category | flops | bytes accessed | tf_op | source)
XLA Modules:
  0.0 914.9 jit_solution(4972568118774323506)
XLA Ops:
  18.6 43.6 %all-gather.4.cloned.1.call-done.refs_7_.refs_9_ = bf16[512,1536]{1,0:T(8,128)(2,1)} async-done(((bf16[64,1536]{1,0:T(8,128)(2,1)}), bf16[512,1536]{1,0:T(8,128)(2,1)}) %all-gather.4.cloned.1.call-update) | async-done | bytes 1572880 | tf_op jit(solution)/shard_map/all_gather | solution.py:87
  76.0 13.2 %collective-permute-done.8.refs_3_.refs_8_.refs_10_ = bf16[512,512]{1,0:T(8,128)(2,1)} collective-permute-done((bf16[512,512]{1,0:T(8,128)(2,1)}, bf16[512,512]{1,0:T(8,128)(2,1)}, u32[]{:S(2)}, u32[]{:S(2)}) %collective-permute-start.8) | collective-permute-done | bytes 524320 | tf_op jit(solution)/shard_map/ppermute | solution.py:69
  89.2 22.8 %project.1 = (bf16[2368,1024]{1,0:T(8,128)(2,1)}, bf16[2368,3072]{1,0:T(8,128)(2,1)}) custom-call(f32[1,1024]{1,0:T(1,128)} %get-tuple-element.121.refs_0_, f32[1,1024]{1,0:T(1,128)} %get-tuple-element.120.refs_1_, f32[1,3072]{1,0:T(1,128)} %reshape.82.refs_2_, bf16[2368,512]{1,0:T(8,128)(2,1)} %get-tuple-element.60.refs_3_.refs_4_.refs_5_, ...), custom_call_target="tpu_custom_call" | custom-call | flops 29796335616 | bytes 30560256 | tf_op jit(solution)/shard_map/project/pallas_call | solution.py:54
  122.4 64.3 %attend.1.refs_3_.refs_0_ = bf16[2368,1024]{1,0:T(8,128)(2,1)} custom-call(bf16[2368,3072]{1,0:T(8,128)(2,1)} %get-tuple-element.63.refs_0_, bf16[64,2048]{1,0:T(8,128)(2,1)} %copy-done.16, bf16[256,512]{1,0:T(8,128)(2,1)} %copy-done.17, bf16[512,512]{1,0:T(8,128)(2,1)} %collective-permute-done.8.refs_3_.refs_8_.refs_10_, ...), custom_call_target="tpu_custom_call" | custom-call | flops 74646028288 | bytes 19398656 | tf_op jit(solution)/shard_map/attend/pallas_call | solution.py:54
  195.1 12.9 %output.1 = (f32[2368,1024]{1,0:T(8,128)}, bf16[2368,1024]{1,0:T(8,128)(2,1)}) custom-call(f32[1,1024]{1,0:T(1,128)} %get-tuple-element.124.refs_0_, f32[1,1024]{1,0:T(1,128)} %get-tuple-element.123.refs_1_.refs_0_, f32[1,1024]{1,0:T(1,128)} %get-tuple-element.122.refs_2_, bf16[2368,1024]{1,0:T(8,128)(2,1)} %attend.1.refs_3_.refs_0_, ...), custom_call_target="tpu_custom_call" | custom-call | flops 9932111872 | bytes 26357760 | tf_op jit(solution)/shard_map/output/pallas_call | solution.py:54
  208.0 28.6 %all-gather.8.cloned.1.call-done.refs_6_ = bf16[2048,512]{1,0:T(8,128)(2,1)} async-done(((bf16[256,512]{1,0:T(8,128)(2,1)}), bf16[2048,512]{1,0:T(8,128)(2,1)}) %all-gather.8.cloned.1.call-update) | async-done | bytes 2097168 | tf_op jit(solution)/shard_map/all_gather | solution.py:87
  236.6 40.8 %expand.1 = (bf16[2368,4096]{1,0:T(8,128)(2,1)}, bf16[2368,4096]{1,0:T(8,128)(2,1)}) custom-call(f32[1,4096]{1,0:T(1,128)} %bitcast.15, bf16[2368,1024]{1,0:T(8,128)(2,1)} %get-tuple-element.68.refs_1_.refs_0_, bf16[512,2048]{1,0:T(8,128)(2,1)} %refs_4_.4, bf16[512,2048]{1,0:T(8,128)(2,1)} %collective-permute-done.11.refs_3_.refs_5_, ...), custom_call_target="tpu_custom_call" | custom-call | flops 39728447488 | bytes 52051968 | tf_op jit(solution)/shard_map/expand/pallas_call | solution.py:54
  277.4 29.8 %reduce_back.1 = (bf16[2368,1024]{1,0:T(8,128)(2,1)}, bf16[2368,4096]{1,0:T(8,128)(2,1)}, f32[1,1024]{1,0:T(1,128)}, f32[1,4096]{1,0:T(1,128)}) custom-call(s32[4]{0:T(128)} %dynamic_slice.54.refs_0_, bf16[2368,4096]{1,0:T(8,128)(2,1)} %get-tuple-element.72.refs_1_, bf16[2368,512]{1,0:T(8,128)(2,1)} %get-tuple-element.67.refs_5_.refs_2_, ...), custom_call_target="tpu_custom_call" | custom-call | flops 39728447488 | bytes 56905744 | tf_op jit(solution)/shard_map/reduce_back/pallas_call | solution.py:54
  307.3 16.4 %reduce_outer.2.refs_2_ = bf16[2048,1024]{1,0:T(8,128)(2,1)} custom-call(bf16[2368,4096]{1,0:T(8,128)(2,1)} %get-tuple-element.69.refs_0_.refs_2_, bf16[2368,1024]{1,0:T(8,128)(2,1)} %get-tuple-element.75.refs_1_.refs_3_), custom_call_target="tpu_custom_call" | custom-call | flops 19864223744 | bytes 28442624 | tf_op jit(solution)/shard_map/reduce_outer/pallas_call | solution.py:54
  324.2 16.4 %expand_outer.2.refs_2_ = bf16[1024,2048]{1,0:T(8,128)(2,1)} custom-call(bf16[2368,1024]{1,0:T(8,128)(2,1)} %get-tuple-element.68.refs_1_.refs_0_, bf16[2368,4096]{1,0:T(8,128)(2,1)} %get-tuple-element.74.refs_1_), custom_call_target="tpu_custom_call" | custom-call | flops 19864223744 | bytes 28442624 | tf_op jit(solution)/shard_map/expand_outer/pallas_call | solution.py:54
  340.7 16.8 %expand_outer.3 = bf16[1024,2048]{1,0:T(8,128)(2,1)} custom-call(bf16[2368,1024]{1,0:T(8,128)(2,1)} %get-tuple-element.68.refs_1_.refs_0_, bf16[2368,4096]{1,0:T(8,128)(2,1)} %get-tuple-element.74.refs_1_, bf16[1024,2048]{1,0:T(8,128)(2,1)} %expand_outer.2.refs_2_), custom_call_target="tpu_custom_call" | custom-call | flops 19864223744 | bytes 28442624 | tf_op jit(solution)/shard_map/expand_outer/pallas_call | solution.py:54
  357.5 16.6 %reduce_outer.3 = bf16[2048,1024]{1,0:T(8,128)(2,1)} custom-call(bf16[2368,4096]{1,0:T(8,128)(2,1)} %get-tuple-element.69.refs_0_.refs_2_, bf16[2368,1024]{1,0:T(8,128)(2,1)} %get-tuple-element.75.refs_1_.refs_3_, bf16[2048,1024]{1,0:T(8,128)(2,1)} %reduce_outer.2.refs_2_), custom_call_target="tpu_custom_call" | custom-call | flops 19864223744 | bytes 28442624 | tf_op jit(solution)/shard_map/reduce_outer/pallas_call | solution.py:54
  384.7 38.2 %expand_back.1 = (f32[2368,1024]{1,0:T(8,128)}, bf16[2368,1024]{1,0:T(8,128)(2,1)}, bf16[2368,1024]{1,0:T(8,128)(2,1)}, f32[1,1024]{1,0:T(1,128)}, f32[1,1024]{1,0:T(1,128)}, /*index=5*/f32[1,1024]{1,0:T(1,128)}) custom-call(f32[1,1024]{1,0:T(1,128)} %get-tuple-element.123.refs_1_.refs_0_, bf16[2368,4096]{1,0:T(8,128)(2,1)} %get-tuple-element.74.refs_1_, ...), custom_call_target="tpu_custom_call" | custom-call | flops 49660559360 | bytes 63848448 | tf_op jit(solution)/shard_map/expand_back/pallas_call | solution.py:54
  462.2 27.5 %reduce.11 = (bf16[2368,512]{1,0:T(8,128)(2,1)}, bf16[2368,512]{1,0:T(8,128)(2,1)}) custom-call(s32[4]{0:T(128)} %dynamic_slice.54.refs_0_, f32[1,1024]{1,0:T(1,128)} %get-tuple-element.125.refs_1_, bf16[2368,4096]{1,0:T(8,128)(2,1)} %get-tuple-element.69.refs_0_.refs_2_, f32[2368,1024]{1,0:T(8,128)} %get-tuple-element.70.refs_2_.refs_3_, ...), custom_call_target="tpu_custom_call" | custom-call | flops 39728447488 | bytes 42340368 | tf_op jit(solution)/shard_map/reduce/pallas_call | solution.py:54
  489.7 40.4 %attend_back.4.refs_2_ = bf16[2368,1536]{1,0:T(8,128)(2,1)} custom-call(bf16[2368,3072]{1,0:T(8,128)(2,1)} %get-tuple-element.63.refs_0_, bf16[2368,1024]{1,0:T(8,128)(2,1)} %get-tuple-element.80.refs_1_, bf16[2368,512]{1,0:T(8,128)(2,1)} %get-tuple-element.77.refs_0_.refs_2_), custom_call_target="tpu_custom_call" | custom-call | flops 45936017408 | bytes 26673152 | tf_op jit(solution)/shard_map/attend_back/pallas_call | solution.py:54
  534.5 9.7 %collective-permute-done.22 = bf16[512,512]{1,0:T(8,128)(2,1)S(1)} collective-permute-done((bf16[512,512]{1,0:T(8,128)(2,1)S(1)}, bf16[512,512]{1,0:T(8,128)(2,1)S(1)}, u32[]{:S(2)}, u32[]{:S(2)}) %collective-permute-start.22) | collective-permute-done | bytes 524320 | tf_op jit(solution)/shard_map/ppermute | solution.py:69
  551.9 40.6 %attend_back.5.refs_1_.refs_2_ = bf16[2368,1536]{1,0:T(8,128)(2,1)} custom-call(bf16[2368,3072]{1,0:T(8,128)(2,1)} %get-tuple-element.63.refs_0_, bf16[2368,1024]{1,0:T(8,128)(2,1)} %get-tuple-element.80.refs_1_, bf16[2368,1536]{1,0:T(8,128)(2,1)} %attend_back.4.refs_2_, ...), custom_call_target="tpu_custom_call", output_to_operand_aliasing={{}: (2, {})} | custom-call | flops 45936017408 | bytes 26673152 | tf_op jit(solution)/shard_map/attend_back/pallas_call | solution.py:54
  592.5 9.0 project_outer.6.refs_2_
  614.9 40.5 %attend_back.6.refs_1_.refs_3_ = bf16[2368,768]{1,0:T(8,128)(2,1)} custom-call(bf16[2368,3072]{1,0:T(8,128)(2,1)} %get-tuple-element.63.refs_0_, bf16[2368,1024]{1,0:T(8,128)(2,1)} %get-tuple-element.80.refs_1_, bf16[1024,768]{1,0:T(8,128)(2,1)} %add_convert_fusion.4.refs_2_), custom_call_target="tpu_custom_call" | custom-call | flops 45936017408 | bytes 23035904 | tf_op jit(solution)/shard_map/attend_back/pallas_call | solution.py:54
  687.7 34.0 %all-reduce.6.cloned.1.call-done = (bf16[512,2048]{1,0:T(8,128)(2,1)}, bf16[512,512]{1,0:T(8,128)(2,1)}) async-done(((bf16[512,2048]{1,0:T(8,128)(2,1)}, bf16[512,512]{1,0:T(8,128)(2,1)}), (bf16[512,2048]{1,0:T(8,128)(2,1)}, bf16[512,512]{1,0:T(8,128)(2,1)})) %all-reduce.6.cloned.1.call-update) | async-done | bytes 2621456 | tf_op jit(solution)/shard_map/psum | solution.py:686
  721.7 40.5 %attend_back.7.refs_1_.refs_4_ = bf16[2368,768]{1,0:T(8,128)(2,1)} custom-call(bf16[2368,3072]{1,0:T(8,128)(2,1)} %get-tuple-element.63.refs_0_, bf16[2368,1024]{1,0:T(8,128)(2,1)} %get-tuple-element.80.refs_1_, bf16[1024,384]{1,0:T(8,128)(2,1)} %copy-done.4, bf16[512,768]{1,0:T(8,128)(2,1)} %copy-done.6, bf16[512,2048]{1,0:T(8,128)(2,1)} %get-tuple-element.106.refs_4_.refs_13_), custom_call_target="tpu_custom_call" | custom-call | flops 45936017408 | bytes 23035904 | tf_op jit(solution)/shard_map/attend_back/pallas_call | solution.py:54
  789.6 19.2 %project_back.2 = (f32[1184,512]{1,0:T(8,128)}, bf16[1184,512]{1,0:T(8,128)(2,1)}, f32[1,1024]{1,0:T(1,128)}, f32[1,1024]{1,0:T(1,128)}, f32[1,1536]{1,0:T(1,128)}, /*index=5*/f32[1,768]{1,0:T(1,128)}, f32[1,768]{1,0:T(1,128)}) custom-call(f32[1,1024]{1,0:T(1,128)} %get-tuple-element.121.refs_0_, f32[2368,1024]{1,0:T(8,128)} %get-tuple-element.79.refs_1_, ...), custom_call_target="tpu_custom_call" | custom-call | flops 14898167808 | bytes 39051264 | tf_op jit(solution)/shard_map/project_back/pallas_call | solution.py:54
  814.7 19.0 %project_back.3 = (f32[1184,512]{1,0:T(8,128)}, bf16[1184,512]{1,0:T(8,128)(2,1)}, f32[1,1024]{1,0:T(1,128)}, f32[1,1024]{1,0:T(1,128)}, f32[1,1536]{1,0:T(1,128)}, /*index=5*/f32[1,768]{1,0:T(1,128)}, f32[1,768]{1,0:T(1,128)}) custom-call(f32[1,1024]{1,0:T(1,128)} %get-tuple-element.121.refs_0_, f32[2368,1024]{1,0:T(8,128)} %get-tuple-element.79.refs_1_, ...), custom_call_target="tpu_custom_call" | custom-call | flops 14898167808 | bytes 39051264 | tf_op jit(solution)/shard_map/project_back/pallas_call | solution.py:54
  886.5 10.0 %collective-permute-done.49 = bf16[256,384]{1,0:T(8,128)(2,1)S(1)} collective-permute-done((bf16[256,384]{1,0:T(8,128)(2,1)S(1)}, bf16[256,384]{1,0:T(8,128)(2,1)S(1)}, u32[]{:S(2)}, u32[]{:S(2)}) %collective-permute-start.49) | collective-permute-done | bytes 196640 | tf_op jit(solution)/shard_map/ppermute | solution.py:96
  (306 shorter events, 249.4 us)
Async XLA Ops:
  7.2 55.1 %all-gather.4.cloned.1.call-start = ((), (), s32[]{:S(2)}) async-start(), calls=%async_computation | async-start | bytes 1769472 | tf_op jit(solution)/shard_map/all_gather | solution.py:87
  17.6 169.2 %all-gather.6.cloned.1.call-start = ((), (), s32[]{:S(2)}) async-start(), calls=%async_computation.1 | async-start | bytes 2359296 | tf_op jit(solution)/shard_map/all_gather | solution.py:87
  17.6 56.0 %collective-permute-start.2 = (bf16[2368,512]{1,0:T(8,128)(2,1)}, bf16[2368,512]{1,0:T(8,128)(2,1)}, u32[]{:S(2)}, u32[]{:S(2)}) collective-permute-start(bf16[2368,512]{1,0:T(8,128)(2,1)} %get-tuple-element.61), channel_id=1, source_target_pairs={{0,2},{2,0},{1,3},{3,1},{4,6},{6,4},{5,7},{7,5},{8,10},{10,8},{9,1... | collective-permute-start | bytes 7274504 | tf_op jit(solution)/shard_map/ppermute | solution.py:69
  18.6 70.5 %collective-permute-start.3 = (bf16[512,1536]{1,0:T(8,128)(2,1)}, bf16[512,1536]{1,0:T(8,128)(2,1)}, u32[]{:S(2)}, u32[]{:S(2)}) collective-permute-start(bf16[512,1536]{1,0:T(8,128)(2,1)} %refs_7_.3), channel_id=1, source_target_pairs={{0,1},{1,0},{2,3},{3,2},{4,5},{5,4},{6,7},{7,6},{8,9},{9,8},{10,11... | collective-permute-start | bytes 4718600 | tf_op jit(solution)/shard_map/ppermute | solution.py:69
  62.3 26.9 %collective-permute-start.5 = (bf16[512,1536]{1,0:T(8,128)(2,1)}, bf16[512,1536]{1,0:T(8,128)(2,1)}, u32[]{:S(2)}, u32[]{:S(2)}) collective-permute-start(bf16[512,1536]{1,0:T(8,128)(2,1)} %all-gather.4.cloned.1.call-done.refs_7_.refs_9_), channel_id=1, source_target_pairs={{0,1},{1,0},{2,3},{3,2},{4,5},{5,4},{6,7},{7,6},{8,9},{9,8},{10,11... | collective-permute-start | bytes 4718600 | tf_op jit(solution)/shard_map/ppermute | solution.py:69
  65.7 47.6 %collective-permute-start.6 = (bf16[64,2048]{1,0:T(8,128)(2,1)S(1)}, bf16[64,2048]{1,0:T(8,128)(2,1)S(1)}, u32[]{:S(2)}, u32[]{:S(2)}) collective-permute-start(bf16[64,2048]{1,0:T(8,128)(2,1)S(1)} %constant_dynamic-slice_fusion.8), channel_id=1, source_target_pairs={{0,2},{2,0},{1,3},{3,1},{4,6},{6,4},{5,7},{7,5},{8,10},{10,8},{9,1... | collective-permute-start | bytes 786440 | tf_op jit(solution)/shard_map/ppermute | solution.py:69
  89.1 30.6 %collective-permute-start.9 = (bf16[512,512]{1,0:T(8,128)(2,1)}, bf16[512,512]{1,0:T(8,128)(2,1)}, u32[]{:S(2)}, u32[]{:S(2)}) collective-permute-start(bf16[512,512]{1,0:T(8,128)(2,1)} %collective-permute-done.8.refs_3_.refs_8_.refs_10_), channel_id=1, source_target_pairs={{0,1},{1,0},{2,3},{3,2},{4,5},{5,4},{6,7},{7,6},{8,9},{9,8},{10,11... | collective-permute-start | bytes 1572872 | tf_op jit(solution)/shard_map/ppermute | solution.py:69
  114.1 122.5 %all-gather.8.cloned.1.call-start = ((), (), s32[]{:S(2)}) async-start(), calls=%async_computation.2 | async-start | bytes 2359296 | tf_op jit(solution)/shard_map/all_gather | solution.py:87
  186.7 49.9 %collective-permute-start.11 = (bf16[512,2048]{1,0:T(8,128)(2,1)S(1)}, bf16[512,2048]{1,0:T(8,128)(2,1)}, u32[]{:S(2)}, u32[]{:S(2)}) collective-permute-start(bf16[512,2048]{1,0:T(8,128)(2,1)S(1)} %copy-done.19), channel_id=1, source_target_pairs={{0,1},{1,0},{2,3},{3,2},{4,5},{5,4},{6,7},{7,6},{8,9},{9,8},{10,11... | collective-permute-start | bytes 6291464 | tf_op jit(solution)/shard_map/ppermute | solution.py:69
  186.8 49.8 %collective-permute-start.12 = (bf16[512,2048]{1,0:T(8,128)(2,1)}, bf16[512,2048]{1,0:T(8,128)(2,1)}, u32[]{:S(2)}, u32[]{:S(2)}) collective-permute-start(bf16[512,2048]{1,0:T(8,128)(2,1)} %all-gather.6.cloned.1.call-done.refs_4_.refs_6_), channel_id=1, source_target_pairs={{0,1},{1,0},{2,3},{3,2},{4,5},{5,4},{6,7},{7,6},{8,9},{9,8},{10,11... | collective-permute-start | bytes 6291464 | tf_op jit(solution)/shard_map/ppermute | solution.py:69
  187.2 90.2 %collective-permute-start.13 = (bf16[2048,512]{1,0:T(8,128)(2,1)}, bf16[2048,512]{1,0:T(8,128)(2,1)}, u32[]{:S(2)}, u32[]{:S(2)}) collective-permute-start(bf16[2048,512]{1,0:T(8,128)(2,1)} %refs_4_.5), channel_id=1, source_target_pairs={{0,1},{1,0},{2,3},{3,2},{4,5},{5,4},{6,7},{7,6},{8,9},{9,8},{10,11... | collective-permute-start | bytes 6291464 | tf_op jit(solution)/shard_map/ppermute | solution.py:69
  189.0 88.4 %collective-permute-start.15 = (bf16[2368,512]{1,0:T(8,128)(2,1)}, bf16[2368,512]{1,0:T(8,128)(2,1)}, u32[]{:S(2)}, u32[]{:S(2)}) collective-permute-start(bf16[2368,512]{1,0:T(8,128)(2,1)} %get-tuple-element.73), channel_id=1, source_target_pairs={{0,2},{2,0},{1,3},{3,1},{4,6},{6,4},{5,7},{7,5},{8,10},{10,8},{9,1... | collective-permute-start | bytes 7274504 | tf_op jit(solution)/shard_map/ppermute | solution.py:69
  236.6 40.8 %collective-permute-start.14 = (bf16[2048,512]{1,0:T(8,128)(2,1)}, bf16[2048,512]{1,0:T(8,128)(2,1)}, u32[]{:S(2)}, u32[]{:S(2)}) collective-permute-start(bf16[2048,512]{1,0:T(8,128)(2,1)} %all-gather.8.cloned.1.call-done.refs_6_), channel_id=1, source_target_pairs={{0,1},{1,0},{2,3},{3,2},{4,5},{5,4},{6,7},{7,6},{8,9},{9,8},{10,11... | collective-permute-start | bytes 6291464 | tf_op jit(solution)/shard_map/ppermute | solution.py:69
  323.7 50.3 %collective-permute-start.17 = (bf16[2048,1024]{1,0:T(8,128)(2,1)}, bf16[2048,1024]{1,0:T(8,128)(2,1)}, u32[]{:S(2)}, u32[]{:S(2)}) collective-permute-start(bf16[2048,1024]{1,0:T(8,128)(2,1)} %reduce_outer.2.refs_2_), channel_id=1, source_target_pairs={{0,1},{1,0},{2,3},{3,2},{4,5},{5,4},{6,7},{7,6},{8,9},{9,8},{10,11... | collective-permute-start | bytes 12582920 | tf_op jit(solution)/shard_map/ppermute | solution.py:69
  340.6 101.3 %collective-permute-start.16 = (bf16[1024,2048]{1,0:T(8,128)(2,1)}, bf16[1024,2048]{1,0:T(8,128)(2,1)}, u32[]{:S(2)}, u32[]{:S(2)}) collective-permute-start(bf16[1024,2048]{1,0:T(8,128)(2,1)} %expand_outer.2.refs_2_), channel_id=1, source_target_pairs={{0,1},{1,0},{2,3},{3,2},{4,5},{5,4},{6,7},{7,6},{8,9},{9,8},{10,11... | collective-permute-start | bytes 12582920 | tf_op jit(solution)/shard_map/ppermute | solution.py:69
  383.2 48.2 %collective-permute-start.18 = (bf16[2048,512]{1,0:T(8,128)(2,1)}, bf16[2048,512]{1,0:T(8,128)(2,1)S(1)}, u32[]{:S(2)}, u32[]{:S(2)}) collective-permute-start(bf16[2048,512]{1,0:T(8,128)(2,1)} %split.81), channel_id=1, source_target_pairs={{0,2},{2,0},{1,3},{3,1},{4,6},{6,4},{5,7},{7,5},{8,10},{10,8},{9,1... | collective-permute-start | bytes 6291464 | tf_op jit(solution)/shard_map/ppermute | solution.py:69
  441.9 109.9 %all-reduce.4.cloned.1.call-start = ((), (), s32[]{:S(2)}) async-start(), calls=%async_computation.3 | async-start | bytes 4194304 | tf_op jit(solution)/shard_map/psum | solution.py:685
  450.8 79.3 %collective-permute-start.21 = (bf16[512,2048]{1,0:T(8,128)(2,1)}, bf16[512,2048]{1,0:T(8,128)(2,1)S(1)}, u32[]{:S(2)}, u32[]{:S(2)}) collective-permute-start(bf16[512,2048]{1,0:T(8,128)(2,1)} %split.83), channel_id=1, source_target_pairs={{0,2},{2,0},{1,3},{3,1},{4,6},{6,4},{5,7},{7,5},{8,10},{10,8},{9,1... | collective-permute-start | bytes 6291464 | tf_op jit(solution)/shard_map/ppermute | solution.py:69
  592.5 129.1 %all-reduce.6.cloned.1.call-start = ((), (), s32[]{:S(2)}) async-start(), calls=%async_computation.4 | async-start | bytes 5242880 | tf_op jit(solution)/shard_map/psum | solution.py:686
  601.5 67.1 %collective-permute-start.20 = (bf16[2368,512]{1,0:T(8,128)(2,1)}, bf16[2368,512]{1,0:T(8,128)(2,1)}, u32[]{:S(2)}, u32[]{:S(2)}) collective-permute-start(bf16[2368,512]{1,0:T(8,128)(2,1)} %get-tuple-element.78), channel_id=1, source_target_pairs={{0,2},{2,0},{1,3},{3,1},{4,6},{6,4},{5,7},{7,5},{8,10},{10,8},{9,1... | collective-permute-start | bytes 7274504 | tf_op jit(solution)/shard_map/ppermute | solution.py:69
  682.4 97.0 %collective-permute-start.27 = (bf16[512,384]{1,0:T(8,128)(2,1)S(1)}, bf16[512,384]{1,0:T(8,128)(2,1)}, u32[]{:S(2)}, u32[]{:S(2)}) collective-permute-start(bf16[512,384]{1,0:T(8,128)(2,1)S(1)} %split.89), channel_id=1, source_target_pairs={{0,2},{2,0},{1,3},{3,1},{4,6},{6,4},{5,7},{7,5},{8,10},{10,8},{9,1... | collective-permute-start | bytes 1179656 | tf_op jit(solution)/shard_map/ppermute | solution.py:69
  686.2 94.5 %collective-permute-start.37 = (bf16[256,768]{1,0:T(8,128)(2,1)}, bf16[256,768]{1,0:T(8,128)(2,1)}, u32[]{:S(2)}, u32[]{:S(2)}) collective-permute-start(bf16[256,768]{1,0:T(8,128)(2,1)} %constant_dynamic-slice_fusion.6), channel_id=1, source_target_pairs={{0,4},{4,0},{8,12},{12,8},{16,20},{20,16},{24,28},{28,24},{1,5},{5... | collective-permute-start | bytes 1179656 | tf_op jit(solution)/shard_map/ppermute | solution.py:96
  808.8 90.4 %collective-permute-start.29 = (bf16[1184,512]{1,0:T(8,128)(2,1)}, bf16[1184,512]{1,0:T(8,128)(2,1)S(1)}, u32[]{:S(2)}, u32[]{:S(2)}) collective-permute-start(bf16[1184,512]{1,0:T(8,128)(2,1)} %get-tuple-element.87), channel_id=1, source_target_pairs={{0,2},{2,0},{1,3},{3,1},{4,6},{6,4},{5,7},{7,5},{8,10},{10,8},{9,1... | collective-permute-start | bytes 3637256 | tf_op jit(solution)/shard_map/ppermute | solution.py:69
  846.2 53.0 %collective-permute-start.30 = (bf16[1184,512]{1,0:T(8,128)(2,1)}, bf16[1184,512]{1,0:T(8,128)(2,1)S(1)}, u32[]{:S(2)}, u32[]{:S(2)}) collective-permute-start(bf16[1184,512]{1,0:T(8,128)(2,1)} %get-tuple-element.88), channel_id=1, source_target_pairs={{0,2},{2,0},{1,3},{3,1},{4,6},{6,4},{5,7},{7,5},{8,10},{10,8},{9,1... | collective-permute-start | bytes 3637256 | tf_op jit(solution)/shard_map/ppermute | solution.py:69
  (70 other events, 1296.9 us)
Sparse Core Ops, SparseCore 0:
  17.7 44.5 all-gather.3
  114.2 50.8 all-gather.5
  186.8 49.7 all-gather.7
  452.4 99.4 all-reduce.3
  603.1 118.5 all-reduce.5

commit v2 on v1

--- a/solution.py
+++ b/solution.py
@@ -18,6 +18,9 @@
 ROOT_HALF = 0.7071067811865476
 DENSITY = 0.3989422804014327
 KEYS_A = 512
+EXPAND_CUT = 1024
+LIGHT = 128
+QUERY_CUTS = (0, 208, 400, PAD)
 MEBI = 1 << 20
 
 
@@ -41,7 +44,7 @@
     return pl.BlockSpec((PAD, width), lambda i: (i, 0))
 
 
-def call(kernel, name, grid, operands, outputs, macs, after=(), into=None):
+def call(kernel, name, grid, operands, outputs, macs, after=(), into=None, weight=1):
     if into is not None:
         after = (into, *after)
     size = sum(a.size * a.dtype.itemsize for _, a in operands)
@@ -58,7 +61,7 @@
         out_specs=[s for s, _, _ in outputs],
         out_shape=[jax.ShapeDtypeStruct(s, t) for _, s, t in outputs],
         compiler_params=pltpu.CompilerParams(vmem_limit_bytes=60 * MEBI),
-        cost_estimate=pl.CostEstimate(flops=4 * macs, bytes_accessed=size, transcendentals=0),
+        cost_estimate=pl.CostEstimate(flops=2 * macs // weight, bytes_accessed=size // weight, transcendentals=0),
         input_output_aliases={} if into is None else {used: 0},
         name=name,
     )(*[a for _, a in operands], *after)
@@ -77,14 +80,19 @@
     return [gather_blocks(block, "col") for block in gather_blocks(weight, "row")]
 
 
-def fetch_shares(weight):
-    depth = weight.shape[0] // lax.axis_size("dp")
-    share = lax.dynamic_slice_in_dim(weight, lax.axis_index("dp") * depth, depth)
-    return gather_blocks(share, "row")[1:]
-
-
-def gather_shares(weight, shares):
-    blocks = [weight] + [lax.all_gather(s, "dp", axis=0, tiled=True) for s in shares]
+def fetch_shares(weights):
+    place = lax.axis_index("dp")
+    depths = [w.shape[0] // lax.axis_size("dp") for w in weights]
+    shares = [lax.dynamic_slice_in_dim(w, place * d, d) for w, d in zip(weights, depths)]
+    widths = [w.shape[1] for w in weights]
+    fetched = gather_blocks(jnp.concatenate(shares, 1), "row")[1:]
+    ends = [sum(widths[: n + 1]) for n in range(len(widths))]
+    return [[f[:, end - w : end] for f in fetched] for end, w in zip(ends, widths)]
+
+
+def gather_shares(weight, shares, after=None):
+    blocks = [lax.all_gather(s, "dp", axis=0, tiled=True) for s in shares]
+    blocks = [weight] + (blocks if after is None else hold(blocks, after))
     return [gather_blocks(block, "col") for block in blocks]
 
 
@@ -123,16 +131,15 @@
     return jnp.where(low, jnp.concatenate([values, other]), jnp.concatenate([other, values]))
 
 
-def finish_sum(values, axis):
-    steps = steps_of(axis)
-    for step in steps[1:]:
+def sum_shares(values, axis):
+    for step in steps_of(axis):
         values = halve(values, axis, step)
-    for step in reversed(steps):
+    for step in reversed(steps_of(axis)):
         values = join(values, axis, step)
     return values
 
 
-def pack_kernel(place_ref, x_ref, *refs):
+def pack_kernel(masked, place_ref, valid_ref, x_ref, *refs):
     o_refs = refs[-lax.axis_size("row") :]
     images = o_refs[0].shape[0] // PAD
     for place in range(len(o_refs)):
@@ -143,26 +150,27 @@
                 at = (place - s) % len(o_refs) * images
                 for i in range(images):
                     rows = x_ref[(at + i) * SEQ : (at + i + 1) * SEQ]
+                    if masked:
+                        rows = (rows.astype(F32) * valid_ref[at + i].astype(F32)).astype(rows.dtype)
                     o_ref[i * PAD : i * PAD + SEQ] = rows
                     rest = (PAD - SEQ, x_ref.shape[1])
                     o_ref[i * PAD + SEQ : (i + 1) * PAD] = jnp.zeros(rest, x_ref.dtype)
 
 
-def pack_rows(values, place, after=()):
+def pack_rows(values, place, valid, masked, after=()):
     rows, width = values.shape
     parts = lax.axis_size("row")
-    vmem = pl.BlockSpec(memory_space=pltpu.VMEM)
+    vmem, smem = pl.BlockSpec(memory_space=pltpu.VMEM), pl.BlockSpec(memory_space=pltpu.SMEM)
     part = jax.ShapeDtypeStruct((rows // SEQ // parts * PAD, width), values.dtype)
     return pl.pallas_call(
-        pack_kernel,
-        in_specs=[pl.BlockSpec(memory_space=pltpu.SMEM), vmem]
-        + [pl.BlockSpec(memory_space=pl.ANY)] * len(after),
+        partial(pack_kernel, masked),
+        in_specs=[smem, smem, vmem] + [pl.BlockSpec(memory_space=pl.ANY)] * len(after),
         out_specs=[vmem] * parts,
         out_shape=[part] * parts,
         compiler_params=pltpu.CompilerParams(vmem_limit_bytes=60 * MEBI),
-        cost_estimate=pl.CostEstimate(flops=0, bytes_accessed=8 * values.size, transcendentals=0),
+        cost_estimate=pl.CostEstimate(flops=0, bytes_accessed=values.size // 8, transcendentals=0),
         name="pack_rows",
-    )(place.reshape(1), values, *after)
+    )(place.reshape(1), valid, values, *after)
 
 
 def unpack_kernel(counts, place_ref, *refs):
@@ -195,7 +203,7 @@
         ),
         compiler_params=pltpu.CompilerParams(vmem_limit_bytes=60 * MEBI),
         cost_estimate=pl.CostEstimate(
-            flops=0, bytes_accessed=16 * len(parts) * arrays[0].size, transcendentals=0
+            flops=0, bytes_accessed=arrays[0].size // 8, transcendentals=0
         ),
         name="unpack_rows",
     )(place.reshape(1), *arrays)
@@ -261,33 +269,44 @@
     values = (jnp.where(low, second, one), jnp.where(low, one, third))
     scale = HD**-0.5 * LOG2E
     keep = lax.broadcasted_iota(jnp.int32, (1, PAD - KEYS_A), 1) < SEQ - KEYS_A
-    chunk = PAD // 2
-    for start in range(0, PAD, chunk):
-        outs = []
-        for h in range(2):
-            query = queries[h][start : start + chunk]
-            sa = dot_nt(query, keys[h][:KEYS_A])
-            sb = jnp.where(keep, dot_nt(query, keys[h][KEYS_A:]), -1e30)
-            top = jnp.maximum(jnp.max(sa, 1, keepdims=True), jnp.max(sb, 1, keepdims=True))
-            top = top * scale
-            pa = jnp.exp2(sa * scale - top).astype(BF)
-            pb = jnp.exp2(sb * scale - top).astype(BF)
-            outs.append(dot_nn(pa, values[h][:KEYS_A]) + dot_nn(pb, values[h][KEYS_A:]))
-        mixed, totals = jnp.where(low, outs[0], outs[1]), jnp.where(low, outs[1], outs[0])
-        o_ref[start : start + chunk, :] = (mixed / swap_halves(totals)).astype(BF)
-
-
-def attend(packed, after):
+    units = [(slice(*cut), h) for cut in zip(QUERY_CUTS, QUERY_CUTS[1:]) for h in range(2)]
+    scores = [
+        (dot_nt(queries[h][some], keys[h][:KEYS_A]), dot_nt(queries[h][some], keys[h][KEYS_A:]))
+        for some, h in units
+    ]
+    weights = []
+    for sa, sb in scores:
+        sb = jnp.where(keep, sb, -1e30)
+        top = jnp.maximum(jnp.max(sa, 1, keepdims=True), jnp.max(sb, 1, keepdims=True)) * scale
+        weights.append([jnp.exp2(v * scale - top).astype(BF) for v in (sa, sb)])
+    outs = [
+        dot_nn(pa, values[h][:KEYS_A]) + dot_nn(pb, values[h][KEYS_A:])
+        for (_, h), (pa, pb) in zip(units, weights)
+    ]
+    for n in range(0, len(units), 2):
+        mixed, totals = jnp.where(low, *outs[n : n + 2]), jnp.where(low, *outs[n : n + 2][::-1])
+        o_ref[units[n][0], :] = (mixed / swap_halves(totals)).astype(BF)
+
+
+def attend(packed, half, into, after):
     tokens, width = packed.shape
     pairs = width // (6 * HD)
+    some = pairs // 2
     return call(
         attend_kernel,
         "attend",
-        (pairs, tokens // PAD),
-        [(pl.BlockSpec((PAD, 6 * HD), lambda h, i: (i, h)), packed)],
-        [(pl.BlockSpec((PAD, 2 * HD), lambda h, i: (i, h)), (tokens, pairs * 2 * HD), BF)],
-        tokens * PAD * pairs * 2 * HD * 13,
+        (some, tokens // PAD),
+        [(pl.BlockSpec((PAD, 6 * HD), lambda h, i: (i, half * some + h)), packed)],
+        [
+            (
+                pl.BlockSpec((PAD, 2 * HD), lambda h, i: (i, half * some + h)),
+                (tokens, pairs * 2 * HD),
+                BF,
+            )
+        ],
+        tokens * PAD * some * 2 * HD * 5,
         after,
+        into,
     )[0]
 
 
@@ -305,24 +324,26 @@
     scale = HD**-0.5
     edge = PAD - 16
     keep = lax.broadcasted_iota(jnp.int32, (PAD - edge, 1), 0) < SEQ - edge
+    units = [(slice(at, min(PAD, at + 256)), h) for at in range(0, PAD, 256) for h in range(2)]
+    products = [
+        (dot_nt(keys[h], queries[h][some]), dot_nt(values[h], grads[h][some])) for some, h in units
+    ]
+    lows = []
+    for scores, weight_grad in products:
+        sa, sb = scores[:edge], jnp.where(keep, scores[edge:], -1e30)
+        top = jnp.maximum(jnp.max(sa, 0, keepdims=True), jnp.max(sb, 0, keepdims=True))
+        top = top * (scale * LOG2E)
+        weights = jnp.concatenate([jnp.exp2(s * (scale * LOG2E) - top) for s in (sa, sb)], 0)
+        share = 1.0 / jnp.sum(weights, 0, keepdims=True)
+        product = weights * weight_grad
+        row_dot = jnp.sum(product, 0, keepdims=True) * share
+        score_low = (product - weights * row_dot) * share
+        lows.append(((weights * share).astype(BF), score_low.astype(BF)))
     value_grad, key_grad, query_grad = [0.0, 0.0], [0.0, 0.0], [[], []]
-    for start in range(0, PAD, 256):
-        some = slice(start, min(PAD, start + 256))
-        for h in range(2):
-            scores = dot_nt(keys[h], queries[h][some])
-            weight_grad = dot_nt(values[h], grads[h][some])
-            sa, sb = scores[:edge], jnp.where(keep, scores[edge:], -1e30)
-            top = jnp.maximum(jnp.max(sa, 0, keepdims=True), jnp.max(sb, 0, keepdims=True))
-            top = top * (scale * LOG2E)
-            weights = jnp.concatenate(
-                [jnp.exp2(s * (scale * LOG2E) - top) for s in (sa, sb)], 0
-            )
-            weights = weights * (1.0 / jnp.sum(weights, 0, keepdims=True))
-            product = weights * weight_grad
-            score_low = (product - weights * jnp.sum(product, 0, keepdims=True)).astype(BF)
-            value_grad[h] += dot_nn(weights.astype(BF), grad[some])
-            key_grad[h] += dot_nn(score_low, query_right[h][some])
-            query_grad[h].append(dot_tn(score_low, key_right[h]))
+    for (some, h), (weights, score_low) in zip(units, lows):
+        value_grad[h] += dot_nn(weights, grad[some])
+        key_grad[h] += dot_nn(score_low, query_right[h][some])
+        query_grad[h].append(dot_tn(key_right[h], score_low).T)
     query_grad = [jnp.concatenate(q, 0) for q in query_grad]
     o_ref[:, :128] = (jnp.where(low, query_grad[0], key_grad[0]) * scale).astype(BF)
     o_ref[:, 128:256] = jnp.where(low, value_grad[0], query_grad[1] * scale).astype(BF)
@@ -347,9 +368,10 @@
                 BF,
             )
         ],
-        tokens * PAD * cols * 2 * HD * 32,
+        tokens * PAD * cols * 2 * HD * 12,
         after,
         into,
+        LIGHT,
     )[0]
 
 
@@ -377,9 +399,14 @@
     hidden_ref, slope_ref = refs[rows * cols :]
     depth, block = weights[0][0].shape
     normed = cut(normed_ref[...], depth)
-    for j in range(cols):
-        total = sum(dot_nn(n, weights[i][j][...]) for i, n in enumerate(normed))
-        where = slice(j * block, (j + 1) * block)
+    some = min(block, EXPAND_CUT)
+    cuts = [(j, at) for j in range(cols) for at in range(0, block, some)]
+    totals = [
+        sum(dot_nn(n, weights[i][j][:, at : at + some]) for i, n in enumerate(normed))
+        for j, at in cuts
+    ]
+    for (j, at), total in zip(cuts, totals):
+        where = slice(j * block + at, j * block + at + some)
         before = total + bias_ref[:, where]
         below = 0.5 + 0.5 * lax.erf(before * ROOT_HALF)
         hidden_ref[:, where] = (before * below).astype(BF)
@@ -401,24 +428,20 @@
         o_refs[i][...] = ((middle_ref[:, where] + total + bias_ref[:, where]) * valid).astype(BF)
 
 
-def reduce_back_kernel(shape, valid_ref, slope_ref, *refs):
+def reduce_back_kernel(shape, slope_ref, *refs):
     rows, cols = shape
     g_refs, weights = refs[:rows], grid_of(refs[rows : rows + rows * cols], shape)
-    out_low_ref, before_ref, reduce_bias_ref, expand_bias_ref = refs[rows + rows * cols :]
+    before_ref, reduce_bias_ref, expand_bias_ref = refs[rows + rows * cols :]
 
     @pl.when(pl.program_id(0) == 0)
     def _():
         reduce_bias_ref[...] = jnp.zeros_like(reduce_bias_ref)
         expand_bias_ref[...] = jnp.zeros_like(expand_bias_ref)
 
-    valid = valid_ref[pl.program_id(0)].astype(F32)
     block, width = weights[0][0].shape
-    lows = []
-    for i, g in enumerate(g_refs):
-        grad = g[...].astype(F32) * valid
-        add_rows(reduce_bias_ref, grad, i * width)
-        lows.append(grad.astype(BF))
-        out_low_ref[:, i * width : (i + 1) * width] = lows[-1]
+    lows = [g[...] for g in g_refs]
+    for i, low in enumerate(lows):
+        add_rows(reduce_bias_ref, low.astype(F32), i * width)
     for j in range(cols):
         total = sum(dot_nt(low, weights[i][j][...]) for i, low in enumerate(lows))
         where = slice(j * block, (j + 1) * block)
@@ -427,11 +450,14 @@
         before_ref[:, where] = total.astype(BF)
 
 
-def expand_back_kernel(shape, gain_ref, before_ref, middle_ref, out_low_ref, *refs):
+def expand_back_kernel(shape, gain_ref, before_ref, middle_ref, *refs):
     rows, cols = shape
+    g_refs, refs = refs[:rows], refs[rows:]
     count = rows * cols
     expand, output = grid_of(refs[:count], shape), grid_of(refs[count : 2 * count], shape)
-    middle_grad_ref, middle_low_ref, mixed_low_ref, gain_grad, shift_grad, bias_grad = refs[2 * count :]
+    refs = refs[2 * count :]
+    middle_grad_ref, mixed_low_ref, gain_grad, shift_grad, bias_grad = refs[:5]
+    low_refs = refs[5:]
 
     @pl.when(pl.program_id(0) == 0)
     def _():
@@ -450,11 +476,11 @@
         where = slice(i * width, (i + 1) * width)
         add_rows(gain_grad, upstream[i] * scaled[i], i * width)
         add_rows(shift_grad, upstream[i], i * width)
-        grad = out_low_ref[:, where].astype(F32) + part
+        grad = g_refs[i][...].astype(F32) + part
         add_rows(bias_grad, grad, i * width)
         middle_grad_ref[:, where] = grad
         lows.append(grad.astype(BF))
-        middle_low_ref[:, where] = lows[-1]
+        low_refs[i][...] = lows[-1]
     heads = output[0][0].shape[0]
     for j in range(cols):
         total = sum(dot_nt(low, output[i][j][...]) for i, low in enumerate(lows))
@@ -493,26 +519,46 @@
         o_refs[i][...] = total.astype(o_refs[i].dtype)
 
 
-def outer_kernel(a_ref, b_ref, o_ref):
-    o_ref[...] = dot_tn(a_ref[...], b_ref[...]).astype(o_ref.dtype)
-
-
-def outer(left, right, left_part, right_part, name, after=()):
+def outer_kernel(rights, received, whole_width, a_ref, *refs):
+    b_refs, refs = refs[:rights], refs[rights:]
+    received, o_refs = refs[:received], refs[received:]
+    height, width = o_refs[0].shape
+    left = a_ref[...]
+    at = 0
+    for b_ref in b_refs:
+        total = dot_tn(left, b_ref[...])
+        where = slice(at, at + total.shape[1])
+        for ref in received:
+            total += ref[:, where].astype(F32)
+        total = total.astype(BF)
+        if width < whole_width:
+            o_refs[at // width][...] = total
+        else:
+            for n, o_ref in enumerate(o_refs):
+                o_ref[:, where] = total[n * height : (n + 1) * height]
+        at = where.stop
+
+
+def outer(left, rights, left_part, right_part, name, after, received=(), splits=(1, 1)):
     tokens = left.shape[0]
     (li, lw), (ri, rw) = left_part, right_part
     bl, br = min(lw, 1024), 1024 if rw % 1024 == 0 else rw
+    down, across = splits
+    tile = pl.BlockSpec((bl, br), lambda i, j: (i, j))
+    part = pl.BlockSpec((bl // down, br // across), lambda i, j: (i, j))
+    spec = pl.BlockSpec((tokens, br // len(rights)), lambda i, j: (0, ri * (rw // br) + j))
     return call(
-        outer_kernel,
+        partial(outer_kernel, len(rights), len(received), br),
         name,
         (lw // bl, rw // br),
-        [
-            (pl.BlockSpec((tokens, bl), lambda i, j: (0, li * (lw // bl) + i)), left),
-            (pl.BlockSpec((tokens, br), lambda i, j: (0, ri * (rw // br) + j)), right),
-        ],
-        [(pl.BlockSpec((bl, br), lambda i, j: (i, j)), (lw, rw), BF)],
+        [(pl.BlockSpec((tokens, bl), lambda i, j: (0, li * (lw // bl) + i)), left)]
+        + [(spec, right) for right in rights]
+        + [(tile, r) for r in received],
+        [(part, (lw // down, rw // across), BF)] * (down * across),
         tokens * lw * rw,
         after,
-    )[0]
+        weight=LIGHT,
+    )
 
 
 def body(
@@ -542,13 +588,14 @@
     shape = (rows, cols)
     step = (images,)
 
-    def to_tokens(values, after=()):
-        parts = pack_rows(values, row_index, after)
+    local_valid = lax.dynamic_slice_in_dim(image_valid, col_index * local_images, local_images)
+
+    def to_tokens(values, masked, after=()):
+        parts = pack_rows(values, row_index, local_valid, masked, after)
         return [shift(part, "row", -s) if s else part for s, part in enumerate(parts)]
 
-    def from_tokens(parts, dtype):
-        parts = [[shift(a, "row", s) if s else a for a in some] for s, some in enumerate(parts)]
-        return unpack_rows(parts, row_index, dtype)
+    def sent(parts):
+        return [shift(a, "row", s) if s else a for s, a in enumerate(parts)]
 
     features = jnp.stack(
         [first_gain, first_shift, output_bias, second_gain, second_shift, reduce_bias]
@@ -567,10 +614,10 @@
         image_valid, col_index * local_images + row_index * images, images
     )
 
-    inputs = to_tokens(block_input)
-    attend_blocks = gather_shares(attend_weight, hold(fetch_shares(attend_weight), inputs[0]))
-    expand_shares = fetch_shares(hold(expand_weight, inputs[0]))
-    output_blocks = gather_weight(hold(output_weight, inputs))
+    inputs = to_tokens(block_input, False)
+    attend_shares, expand_shares = hold(fetch_shares([attend_weight, expand_weight]), inputs[0])
+    attend_blocks = gather_shares(attend_weight, attend_shares)
+    output_rows = gather_blocks(hold(output_weight, inputs), "row")
 
     def flat(blocks):
         return [(whole(b), b) for some in blocks for b in some]
@@ -602,11 +649,13 @@
         [out(D, BF), out(3 * D, BF)],
         tokens * 3 * D * D,
     )
-    grads = to_tokens(output_grad, (packed,))
+    grads = to_tokens(output_grad, True, (packed,))
     expand_blocks = gather_shares(expand_weight, expand_shares)
-    reduce_shares = fetch_shares(hold(reduce_weight, packed))
-    mixed = attend(packed, (*expand_shares, *reduce_shares, *output_blocks[-1], grads[0]))
-    reduce_blocks = gather_shares(reduce_weight, hold(reduce_shares, mixed))
+    (reduce_shares,) = fetch_shares([hold(reduce_weight, packed)])
+    mixed = attend(packed, 0, None, (*expand_shares, *reduce_shares, grads[0]))
+    reduce_shares = hold(reduce_shares, mixed)
+    mixed = attend(packed, 1, mixed, reduce_shares)
+    output_blocks = [gather_blocks(block, "col") for block in hold(output_rows, mixed)]
     middle, second_normed = call(
         partial(output_kernel, shape),
         "output",
@@ -617,6 +666,7 @@
         [out(D, F32), out(D, BF)],
         tokens * D * D,
     )
+    reduce_blocks = gather_shares(reduce_weight, reduce_shares, second_normed)
     hidden, slope = call(
         partial(expand_kernel, shape),
         "expand",
@@ -625,15 +675,6 @@
         [out(hidden_width, BF), out(hidden_width, BF)],
         tokens * D * hidden_width,
     )
-    out_low, before_low, reduce_bias_grad, expand_bias_grad = call(
-        partial(reduce_back_kernel, shape),
-        "reduce_back",
-        step,
-        [scalars, image(slope)] + row_blocks(grads) + flat(reduce_blocks),
-        [out(D, BF), out(hidden_width, BF), total(D), total(hidden_width)],
-        tokens * D * hidden_width,
-    )
-
     def add_parts(parts, axis, after=None):
         held = parts[0].astype(F32)
         others = [shift(part, axis, s) for s, part in enumerate(parts) if s]
@@ -641,34 +682,61 @@
             held = held + other.astype(F32)
         return held
 
-    def outer_parts(left, right, over_left, name, after=()):
-        lw, rw = left.shape[1], right.shape[1]
-        parts = []
-        for j in reversed(range(cols)):
-            places = ((j, lw // cols), (0, rw)) if over_left else ((0, lw), (j, rw // cols))
-            parts.insert(0, outer(left, right, *places, name, parts[:1] or after))
-        return parts
-
-    def share_of(held, dim, after=None):
-        return add_parts(jnp.split(held, rows, dim), "row", after).astype(BF)
-
-    reduce_held = add_parts(outer_parts(hidden, out_low, True, "reduce_outer"), "col").astype(BF)
-    reduce_share = share_of(reduce_held, 1)
-    middle_grad, middle_low, mixed_low, second_gain_grad, second_shift_grad, output_bias_grad = call(
+    def places(left, rights, over_left, j):
+        lw, rw = left.shape[1], sum(r.shape[1] for r in rights)
+        return ((j, lw // cols), (0, rw)) if over_left else ((0, lw), (j, rw // cols))
+
+    def outer_others(left, rights, over_left, name, after=()):
+        received = []
+        for j in range(1, cols):
+            (block,) = outer(left, rights, *places(left, rights, over_left, j), name, after)
+            received.append(shift(block, "col", j))
+            after = (block,)
+        return received, after
+
+    def outer_own(left, rights, over_left, name, others, after=()):
+        received, order = others
+        splits = (1, rows) if over_left else (rows, 1)
+        where = places(left, rights, over_left, 0)
+        return outer(left, rights, *where, name, (*order, *after), received, splits)
+
+    def share_of(held, after=None):
+        return add_parts(held, "row", after).astype(BF)
+
+    reduce_others = outer_others(hidden, grads, True, "reduce_outer")
+    before_low, reduce_bias_grad, expand_bias_grad = call(
+        partial(reduce_back_kernel, shape),
+        "reduce_back",
+        step,
+        [image(slope)] + row_blocks(grads) + flat(reduce_blocks),
+        [out(hidden_width, BF), total(D), total(hidden_width)],
+        tokens * D * hidden_width,
+        reduce_others[1],
+        weight=LIGHT,
+    )
+    reduce_held = outer_own(hidden, grads, True, "reduce_outer", reduce_others, (before_low,))
+    reduce_share = share_of(reduce_held)
+    expand_others = outer_others(
+        second_normed, [before_low], False, "expand_outer", reduce_held[:1]
+    )
+    middle_grad, mixed_low, second_gain_grad, second_shift_grad, output_bias_grad, *middle_lows = call(
         partial(expand_back_kernel, shape),
         "expand_back",
         step,
-        [full(second_gain), image(before_low), image(middle), image(out_low)]
+        [full(second_gain), image(before_low), image(middle)]
+        + row_blocks(grads)
         + flat(expand_blocks)
         + flat(output_blocks),
-        [out(D, F32), out(D, BF), out(D, BF), total(D), total(D), total(D)],
+        [out(D, F32), out(D, BF), total(D), total(D), total(D)] + [out(width, BF)] * rows,
         tokens * D * (hidden_width + D),
-        (reduce_held,),
-    )
-    expand_held = outer_parts(second_normed, before_low, False, "expand_outer")
-    expand_held = add_parts(expand_held, "col").astype(BF)
-    output_held = outer_parts(mixed, middle_low, True, "output_outer", (reduce_share,))
-    output_held = add_parts(output_held, "col").astype(BF)
+        expand_others[1],
+        weight=LIGHT,
+    )
+    expand_held = outer_own(
+        second_normed, [before_low], False, "expand_outer", expand_others, (middle_grad,)
+    )
+    output_others = outer_others(mixed, middle_lows, True, "output_outer", expand_held[:1])
+    output_held = outer_own(mixed, middle_lows, True, "output_outer", output_others, (reduce_share,))
     results = call(
         partial(reduce_kernel, shape),
         "reduce",
@@ -676,19 +744,18 @@
         [scalars, full(reduce_bias), image(hidden), image(middle)] + flat(reduce_blocks),
         [out(width, BF)] * rows,
         tokens * D * hidden_width,
-        (expand_held, output_held),
-    )
-    block_output = from_tokens([[r] for r in results], BF)
-
-    expand_share = share_of(expand_held, 0, results[0])
-    output_share = share_of(output_held, 1, results[0])
+        output_held[:1],
+        weight=LIGHT,
+    )
+    block_output = unpack_rows([[part] for part in sent(results)], row_index, BF)
+
+    expand_share = share_of(expand_held, results[0])
+    output_share = share_of(output_held, results[0])
     reduce_weight_grad = lax.psum(reduce_share, "dp")
-    expand_weight_grad, output_weight_grad = lax.psum(
-        hold((expand_share, output_share), reduce_weight_grad), "dp"
-    )
+    expand_weight_grad = lax.psum(hold(expand_share, reduce_weight_grad), "dp")
     pairs = 3 * D // (6 * HD) // cols
     counts = [pairs - 2, 1, 1] if pairs > 2 else [pairs]
-    packed_lows, held, shares, halved, pair = [], [], [], [], 0
+    packed_lows, held, shares, pair = [], [], [], 0
     ready = results[:1]
     for g, count in enumerate(counts):
         packed_low = None
@@ -696,18 +763,21 @@
             packed_low = attend_back(
                 packed, mixed_low, cols, pair, slot, count, packed_low, ready
             )
-            ready = (expand_share, output_share, reduce_weight_grad) if pair == 0 else ()
+            ready = (expand_share, output_share) if pair == 0 else ()
             pair += 1
         packed_lows.append(packed_low)
-        parts = outer_parts(first_normed, packed_low, False, "project_outer")
-        held.append(add_parts(parts, "col").astype(BF))
-        shares.append(share_of(held[-1], 0))
-        halved.append(halve(shares[-1], "dp", 1))
-        ready = (held[g],)
-        ready += (shares[g - 1], expand_weight_grad) if g > 0 else ()
-    late = jnp.concatenate(halved[:-1], 1) if len(counts) > 1 else halved[0]
-    late = finish_sum(hold(late, held[-1]), "dp")
-    attend_weight_grad = [late, finish_sum(halved[-1], "dp")] if len(counts) > 1 else [late]
+        ready = (expand_weight_grad, *shares[1:]) if pair == pairs else ()
+        others = outer_others(first_normed, [packed_low], False, "project_outer", ready)
+        held.append(outer_own(first_normed, [packed_low], False, "project_outer", others))
+        shares.append(share_of(held[-1]))
+        ready = (held[g][0],)
+        ready += (shares[g - 1], block_output) if g > 0 else (reduce_weight_grad,)
+    output_weight_grad, first_sum = lax.psum(
+        hold((output_share, shares[0]), expand_weight_grad), "dp"
+    )
+    attend_weight_grad = [first_sum]
+    if len(shares) > 1:
+        attend_weight_grad.append(sum_shares(jnp.concatenate(shares[1:], 1), "dp"))
     attend_weight_grad = jnp.concatenate(attend_weight_grad, 1)
 
     halves = 2 if images % 2 == 0 else 1
@@ -737,13 +807,14 @@
             + [total(p.shape[1]) for p in packed_lows],
             some * PAD * 3 * D * D,
             ready,
+            weight=LIGHT,
         )
-        input_grads.append(results[:rows])
+        input_grads.append(sent(results[:rows]))
         ready = (results[0], shares[-1])
         packed_sums = [v.reshape(cols, -1, 3, HD) for v in results[rows + 2 :]]
         late = (*results[rows : rows + 2], jnp.concatenate(packed_sums, 1))
         sums = late if half == 0 else jax.tree.map(jnp.add, sums, late)
-    input_grad = from_tokens(list(zip(*input_grads)), F32)
+    input_grad = unpack_rows(list(zip(*hold(input_grads, first_sum))), row_index, F32)
     first_gain_grad, first_shift_grad, packed_sums = sums
 
     feature_grads = jnp.concatenate(
@@ -761,7 +832,8 @@
     bias_grads = jnp.concatenate([attend_bias_grad, expand_bias_grad.reshape(cols, -1)], 1)
     bias_grads = add_parts(list(bias_grads), "col")
     feature_grads = sum_all(feature_grads.reshape(-1), "col")
-    small = sum_all(jnp.concatenate([feature_grads, bias_grads]), "dp")
+    small = hold(jnp.concatenate([feature_grads, bias_grads]), input_grads[0][-1])
+    small = hold(sum_all(small, "dp"), input_grads[-1][-1])
     feature_grads, bias_grads = small[: 6 * D].reshape(6, D), small[6 * D :]
     feature_grads = add_parts(jnp.split(feature_grads, rows, 1), "row")
     bias_grads = sum_all(bias_grads, "row")

time: 922 us -> 775 us (0.84)
  Pallas kernels: 586 us -> 512 us
  waiting for transfers between devices: 202 us -> 155 us
  other arithmetic: 51.5 us -> 30.5 us
    pallas_call x25 -> x26, Pallas kernels: 562 us -> 486 us  [call(): pl.pallas_call(body_of, grid=grid, in_specs=[s for s, _ in operands] + [p...]
    convert_element_type x12 -> x6, other arithmetic: 31.2 us -> 12.3 us  [share_of(): return add_parts(held, 'row', after).astype(BF)]
    psum x1 -> x2, waiting for transfers between devices: 34 us -> 15.2 us  [the longest x1 15.2 us: body(): expand_weight_grad = lax.psum(hold(expand_share, reduce_weight_grad), 'dp')]
    ppermute x33 -> x32, waiting for transfers between devices: 52.3 us -> 38.3 us  [shift(): lax.ppermute(values, axis, [(i, (i + step) % size) for i in range(size)])]
    all_gather x3, waiting for transfers between devices: 72.2 us -> 58.2 us  [gather_shares(): blocks = [lax.all_gather(s, 'dp', axis=0, tiled=True) for s in shares]]
    ppermute x18 -> x11, waiting for transfers between devices: 36.8 us -> 33.5 us  [swap(): lax.ppermute(values, axis, [(i, i ^ step) for i in range(lax.axis_size(ax...]
    ppermute x33 -> x32, starting transfers between devices: 22.5 us -> 24.3 us  [shift(): lax.ppermute(values, axis, [(i, (i + step) % size) for i in range(size)])]
  transfers between devices with their start and end apart: 56 -> 49, of which waited for: 23 -> 20; matrix products, arithmetic and copies ran while one was open for 7% -> 4% of each run, Pallas kernels for 53% -> 61%
where the time goes in v2:
time: 775 us; the launch traced here: 766 us
  Pallas kernels  512 us (66%)
  waiting for transfers between devices  155 us (20%)
  starting transfers between devices  34.8 us (4%)
  other arithmetic  30.5 us (4%)
  local copies, waits for them, and re-layouts  18.6 us (2%)
  between operations  15.3 us (2%)
    pallas_call x26, Pallas kernels, call(): pl.pallas_call(body_of, grid=grid, in_specs=[s for s, _ in operands] + [p...  486 us
    all_gather x3, waiting for transfers between devices, gather_shares(): blocks = [lax.all_gather(s, 'dp', axis=0, tiled=True) for s in shares]  58.2 us
    ppermute x32, waiting for transfers between devices, shift(): lax.ppermute(values, axis, [(i, (i + step) % size) for i in range(size)])  38.3 us
    ppermute x11, waiting for transfers between devices, swap(): lax.ppermute(values, axis, [(i, i ^ step) for i in range(lax.axis_size(ax...  33.5 us
    ppermute x32, starting transfers between devices, shift(): lax.ppermute(values, axis, [(i, (i + step) % size) for i in range(size)])  24.3 us
  transfers between devices with their start and end apart: 49, of which 20 were waited for; matrix products, arithmetic and copies ran while one was open for 4% of the time, Pallas kernels for 61%

profile of v2, /device:TPU:0, one launch (start us, length us, event | category | flops | bytes accessed | tf_op | source)
XLA Modules:
  0.0 766.4 jit_solution(18261828299442112561)
XLA Ops:
  26.2 43.8 %all-gather.4.cloned.1.call-done.refs_7_.refs_9_ = bf16[512,1536]{1,0:T(8,128)(2,1)} async-done(((bf16[64,1536]{1,0:T(8,128)(2,1)}), bf16[512,1536]{1,0:T(8,128)(2,1)}) %all-gather.4.cloned.1.call-update) | async-done | bytes 1572880 | tf_op jit(solution)/shard_map/all_gather | solution.py:94
  80.5 22.8 %project.1 = (bf16[2368,1024]{1,0:T(8,128)(2,1)}, bf16[2368,3072]{1,0:T(8,128)(2,1)}) custom-call(f32[1,1024]{1,0:T(1,128)} %get-tuple-element.163.refs_0_, f32[1,1024]{1,0:T(1,128)} %get-tuple-element.162.refs_1_, f32[1,3072]{1,0:T(1,128)} %reshape.82.refs_2_, bf16[2368,512]{1,0:T(8,128)(2,1)} %get-tuple-element.81.refs_3_.refs_4_.refs_5_, ...), custom_call_target="tpu_custom_call" | custom-call | flops 14898167808 | bytes 30560256 | tf_op jit(solution)/shard_map/project/pallas_call | solution.py:57
  106.4 14.4 %all-gather.6.cloned.1.call-done.refs_4_.refs_7_ = bf16[512,2048]{1,0:T(8,128)(2,1)} async-done(((bf16[64,2048]{1,0:T(8,128)(2,1)}), bf16[512,2048]{1,0:T(8,128)(2,1)}) %all-gather.6.cloned.1.call-update) | async-done | bytes 2097168 | tf_op jit(solution)/shard_map/all_gather | solution.py:94
  128.6 24.4 %attend.2.refs_1_ = bf16[2368,1024]{1,0:T(8,128)(2,1)} custom-call(bf16[2368,3072]{1,0:T(8,128)(2,1)} %get-tuple-element.84.refs_0_, bf16[64,2048]{1,0:T(8,128)(2,1)} %slice.87.refs_1_, bf16[256,512]{1,0:T(8,128)(2,1)} %copy-done.21, bf16[2368,512]{1,0:T(8,128)(2,1)} %get-tuple-element.87.refs_3_.refs_1_), custom_call_target="tpu_custom_call" | custom-call | flops 7177502720 | bytes 19398656 | tf_op jit(solution)/shard_map/attend/pallas_call | solution.py:57
  153.0 24.4 %attend.3.refs_3_.refs_0_ = bf16[2368,1024]{1,0:T(8,128)(2,1)} custom-call(bf16[2368,3072]{1,0:T(8,128)(2,1)} %get-tuple-element.84.refs_0_, bf16[2368,1024]{1,0:T(8,128)(2,1)} %attend.2.refs_1_, bf16[256,512]{1,0:T(8,128)(2,1)} %copy-done.21), custom_call_target="tpu_custom_call", output_to_operand_aliasing={{}: (1, {})} | custom-call | flops 7177502720 | bytes 19398656 | tf_op jit(solution)/shard_map/attend/pallas_call | solution.py:57
  180.3 13.0 %output.1 = (f32[2368,1024]{1,0:T(8,128)}, bf16[2368,1024]{1,0:T(8,128)(2,1)}) custom-call(f32[1,1024]{1,0:T(1,128)} %get-tuple-element.166.refs_0_, f32[1,1024]{1,0:T(1,128)} %get-tuple-element.165.refs_1_.refs_0_, f32[1,1024]{1,0:T(1,128)} %get-tuple-element.164.refs_2_, bf16[2368,1024]{1,0:T(8,128)(2,1)} %attend.3.refs_3_.refs_0_, ...), custom_call_target="tpu_custom_call" | custom-call | flops 4966055936 | bytes 26357760 | tf_op jit(solution)/shard_map/output/pallas_call | solution.py:57
  193.3 40.5 %expand.1 = (bf16[2368,4096]{1,0:T(8,128)(2,1)}, bf16[2368,4096]{1,0:T(8,128)(2,1)}) custom-call(f32[1,4096]{1,0:T(1,128)} %bitcast.15, bf16[2368,1024]{1,0:T(8,128)(2,1)} %get-tuple-element.92.refs_1_.refs_0_, bf16[512,2048]{1,0:T(8,128)(2,1)} %refs_5_.3, bf16[512,2048]{1,0:T(8,128)(2,1)} %collective-permute-done.10.refs_3_.refs_6_, ...), custom_call_target="tpu_custom_call" | custom-call | flops 19864223744 | bytes 52051968 | tf_op jit(solution)/shard_map/expand/pallas_call | solution.py:57
  235.2 16.8 %reduce_outer.2.refs_7_.refs_4_ = bf16[2048,1024]{1,0:T(8,128)(2,1)} custom-call(bf16[2368,4096]{1,0:T(8,128)(2,1)} %get-tuple-element.93.refs_0_.refs_2_, bf16[2368,512]{1,0:T(8,128)(2,1)} %get-tuple-element.87.refs_3_.refs_1_, bf16[2368,512]{1,0:T(8,128)(2,1)} %copy-done), custom_call_target="tpu_custom_call" | custom-call | flops 77594624 | bytes 222208 | tf_op jit(solution)/shard_map/reduce_outer/pallas_call | solution.py:57
  252.9 10.1 %collective-permute-done.12.refs_4_.refs_5_ = bf16[2048,512]{1,0:T(8,128)(2,1)S(1)} collective-permute-done((bf16[2048,512]{1,0:T(8,128)(2,1)}, bf16[2048,512]{1,0:T(8,128)(2,1)S(1)}, u32[]{:S(2)}, u32[]{:S(2)}) %collective-permute-start.12) | collective-permute-done | bytes 2097184 | tf_op jit(solution)/shard_map/ppermute | solution.py:72
  265.5 29.6 %reduce_back.1 = (bf16[2368,4096]{1,0:T(8,128)(2,1)}, f32[1,1024]{1,0:T(1,128)}, f32[1,4096]{1,0:T(1,128)}) custom-call(bf16[2368,4096]{1,0:T(8,128)(2,1)} %get-tuple-element.96.refs_0_, bf16[2368,512]{1,0:T(8,128)(2,1)} %get-tuple-element.87.refs_3_.refs_1_, bf16[2368,512]{1,0:T(8,128)(2,1)} %copy-done, bf16[2048,512]{1,0:T(8,128)(2,1)} %refs_4_.1, ...), custom_call_target="tpu_custom_call" | custom-call | flops 155189248 | bytes 406688 | tf_op jit(solution)/shard_map/reduce_back/pallas_call | solution.py:57
  295.2 16.7 %reduce_outer.3 = (bf16[2048,512]{1,0:T(8,128)(2,1)}, bf16[2048,512]{1,0:T(8,128)(2,1)}) custom-call(bf16[2368,4096]{1,0:T(8,128)(2,1)} %get-tuple-element.93.refs_0_.refs_2_, bf16[2368,512]{1,0:T(8,128)(2,1)} %get-tuple-element.87.refs_3_.refs_1_, bf16[2368,512]{1,0:T(8,128)(2,1)} %copy-done, bf16[2048,1024]{1,0:T(8,128)(2,1)} %collective-permute-done.15.refs_3_, ...), custom_call_target="tpu_custom_call" | custom-call | flops 77594624 | bytes 254976 | tf_op jit(solution)/shard_map/reduce_outer/pallas_call | solution.py:57
  311.9 16.6 %expand_outer.2.refs_13_.refs_3_ = bf16[1024,2048]{1,0:T(8,128)(2,1)} custom-call(bf16[2368,1024]{1,0:T(8,128)(2,1)} %get-tuple-element.92.refs_1_.refs_0_, bf16[2368,4096]{1,0:T(8,128)(2,1)} %get-tuple-element.98.refs_5_.refs_1_, bf16[2048,512]{1,0:T(8,128)(2,1)} %get-tuple-element.99.refs_2_), custom_call_target="tpu_custom_call" | custom-call | flops 77594624 | bytes 222208 | tf_op jit(solution)/shard_map/expand_outer/pallas_call | solution.py:57
  330.4 37.9 %expand_back.1 = (f32[2368,1024]{1,0:T(8,128)}, bf16[2368,1024]{1,0:T(8,128)(2,1)}, f32[1,1024]{1,0:T(1,128)}, f32[1,1024]{1,0:T(1,128)}, f32[1,1024]{1,0:T(1,12...) custom-call(f32[1,1024]{1,0:T(1,128)} %get-tuple-element.165.refs_1_.refs_0_, ...), custom_call_target="tpu_custom_call" | custom-call | flops 193986560 | bytes 498816 | tf_op jit(solution)/shard_map/expand_back/pallas_call | solution.py:57
  368.4 17.2 %expand_outer.3 = (bf16[512,2048]{1,0:T(8,128)(2,1)}, bf16[512,2048]{1,0:T(8,128)(2,1)}) custom-call(bf16[2368,1024]{1,0:T(8,128)(2,1)} %get-tuple-element.92.refs_1_.refs_0_, bf16[2368,4096]{1,0:T(8,128)(2,1)} %get-tuple-element.98.refs_5_.refs_1_, bf16[1024,2048]{1,0:T(8,128)(2,1)} %collective-permute-done.16.refs_2_, ...), custom_call_target="tpu_custom_call" | custom-call | flops 77594624 | bytes 254976 | tf_op jit(solution)/shard_map/expand_outer/pallas_call | solution.py:57
  407.1 27.4 %reduce.11 = (bf16[2368,512]{1,0:T(8,128)(2,1)}, bf16[2368,512]{1,0:T(8,128)(2,1)}) custom-call(s32[4]{0:T(128)} %dynamic_slice.33.refs_0_, f32[1,1024]{1,0:T(1,128)} %get-tuple-element.167.refs_1_, bf16[2368,4096]{1,0:T(8,128)(2,1)} %get-tuple-element.93.refs_0_.refs_2_, f32[2368,1024]{1,0:T(8,128)} %get-tuple-element.94.refs_2_.refs_3_, ...), custom_call_target="tpu_custom_call" | custom-call | flops 155189248 | bytes 330784 | tf_op jit(solution)/shard_map/reduce/pallas_call | solution.py:57
  434.5 25.2 %attend_back.4.refs_2_ = bf16[2368,1536]{1,0:T(8,128)(2,1)} custom-call(bf16[2368,3072]{1,0:T(8,128)(2,1)} %get-tuple-element.84.refs_0_, bf16[2368,1024]{1,0:T(8,128)(2,1)} %get-tuple-element.108.refs_1_, bf16[2368,512]{1,0:T(8,128)(2,1)} %get-tuple-element.106.refs_0_.refs_2_), custom_call_target="tpu_custom_call" | custom-call | flops 67289088 | bytes 208384 | tf_op jit(solution)/shard_map/attend_back/pallas_call | solution.py:57
  464.5 25.1 %attend_back.5.refs_1_.refs_2_ = bf16[2368,1536]{1,0:T(8,128)(2,1)} custom-call(bf16[2368,3072]{1,0:T(8,128)(2,1)} %get-tuple-element.84.refs_0_, bf16[2368,1024]{1,0:T(8,128)(2,1)} %get-tuple-element.108.refs_1_, bf16[2368,1536]{1,0:T(8,128)(2,1)} %attend_back.4.refs_2_, bf16[512,2048]{1,0:T(8,128)(2,1)} %add_convert_fusion.refs_3_, ...), custom_call_target="tpu_custom_call", output_to_operand_aliasing={{}: (2, {})} | custom-call | flops 67289088 | bytes 208384 | tf_op jit(solution)/shard_map/attend_back/pallas_call | solution.py:57
  500.0 10.1 %all-reduce.5.cloned.1.call-done.refs_3_ = bf16[2048,512]{1,0:T(8,128)(2,1)} async-done(((bf16[2048,512]{1,0:T(8,128)(2,1)}), bf16[2048,512]{1,0:T(8,128)(2,1)}) %all-reduce.5.cloned.1.call-update) | async-done | bytes 2097168 | tf_op jit(solution)/shard_map/psum | solution.py:754
  519.4 25.2 %attend_back.6.refs_1_.refs_3_ = bf16[2368,768]{1,0:T(8,128)(2,1)} custom-call(bf16[2368,3072]{1,0:T(8,128)(2,1)} %get-tuple-element.84.refs_0_, bf16[2368,1024]{1,0:T(8,128)(2,1)} %get-tuple-element.108.refs_1_, bf16[512,768]{1,0:T(8,128)(2,1)} %get-tuple-element.114.refs_2_, bf16[2048,512]{1,0:T(8,128)(2,1)} %all-reduce.5.cloned.1.call-done.refs_3_), custom_call_target="tpu_custom_call" | custom-call | flops 67289088 | bytes 179968 | tf_op jit(solution)/shard_map/attend_back/pallas_call | solution.py:57
  573.0 25.2 %attend_back.7.refs_1_.refs_4_ = bf16[2368,768]{1,0:T(8,128)(2,1)} custom-call(bf16[2368,3072]{1,0:T(8,128)(2,1)} %get-tuple-element.84.refs_0_, bf16[2368,1024]{1,0:T(8,128)(2,1)} %get-tuple-element.108.refs_1_, bf16[512,384]{1,0:T(8,128)(2,1)} %get-tuple-element.115.refs_2_, bf16[512,768]{1,0:T(8,128)(2,1)} %add_convert_fusion.2.refs_3_, ...), custom_call_target="tpu_custom_call" | custom-call | flops 67289088 | bytes 179968 | tf_op jit(solution)/shard_map/attend_back/pallas_call | solution.py:57
  600.1 15.2 %all-reduce.7.cloned.1.call-done.refs_2_ = bf16[512,2048]{1,0:T(8,128)(2,1)} async-done(((bf16[512,2048]{1,0:T(8,128)(2,1)}), bf16[512,2048]{1,0:T(8,128)(2,1)}) %all-reduce.7.cloned.1.call-update) | async-done | bytes 2097168 | tf_op jit(solution)/shard_map/psum | solution.py:755
  647.4 19.3 %project_back.2 = (f32[1184,512]{1,0:T(8,128)}, bf16[1184,512]{1,0:T(8,128)(2,1)}, f32[1,1024]{1,0:T(1,128)}, f32[1,1024]{1,0:T(1,128)}, f32[1,1536]{1,0:T(1,128)}, /*index=5*/f32[1,768]{1,0:T(1,128)}, f32[1,768]{1,0:T(1,128)}) custom-call(f32[1,1024]{1,0:T(1,128)} %get-tuple-element.163.refs_0_, f32[2368,1024]{1,0:T(8,128)} %get-tuple-element.102.refs_4_.refs_1_, ...), custom_call_target="tpu_custom_call" | custom-call | flops 58195968 | bytes 305088 | tf_op jit(solution)/shard_map/project_back/pallas_call | solution.py:57
  670.6 19.2 %project_back.3 = (f32[1184,512]{1,0:T(8,128)}, bf16[1184,512]{1,0:T(8,128)(2,1)}, f32[1,1024]{1,0:T(1,128)}, f32[1,1024]{1,0:T(1,128)}, f32[1,1536]{1,0:T(1,128)}, /*index=5*/f32[1,768]{1,0:T(1,128)}, f32[1,768]{1,0:T(1,128)}) custom-call(f32[1,1024]{1,0:T(1,128)} %get-tuple-element.163.refs_0_, f32[2368,1024]{1,0:T(8,128)} %get-tuple-element.102.refs_4_.refs_1_, ...), custom_call_target="tpu_custom_call" | custom-call | flops 58195968 | bytes 305088 | tf_op jit(solution)/shard_map/project_back/pallas_call | solution.py:57
  714.4 10.3 %collective-permute-done.39 = bf16[64,768]{1,0:T(8,128)(2,1)S(1)} collective-permute-done((bf16[64,768]{1,0:T(8,128)(2,1)S(1)}, bf16[64,768]{1,0:T(8,128)(2,1)S(1)}, u32[]{:S(2)}, u32[]{:S(2)}) %collective-permute-start.39) | collective-permute-done | bytes 98336 | tf_op jit(solution)/shard_map/ppermute | solution.py:104
  (274 shorter events, 220.6 us)
Async XLA Ops:
  7.2 62.8 %all-gather.4.cloned.1.call-start = ((), (), s32[]{:S(2)}) async-start(), calls=%async_computation | async-start | bytes 1769472 | tf_op jit(solution)/shard_map/all_gather | solution.py:94
  24.2 96.7 %all-gather.6.cloned.1.call-start = ((), (), s32[]{:S(2)}) async-start(), calls=%async_computation.1 | async-start | bytes 2359296 | tf_op jit(solution)/shard_map/all_gather | solution.py:94
  24.2 54.9 %collective-permute-start.2 = (bf16[2368,512]{1,0:T(8,128)(2,1)}, bf16[2368,512]{1,0:T(8,128)(2,1)S(1)}, u32[]{:S(2)}, u32[]{:S(2)}) collective-permute-start(bf16[2368,512]{1,0:T(8,128)(2,1)} %get-tuple-element.82), channel_id=1, source_target_pairs={{0,2},{2,0},{1,3},{3,1},{4,6},{6,4},{5,7},{7,5},{8,10},{10,8},{9,1... | collective-permute-start | bytes 7274504 | tf_op jit(solution)/shard_map/ppermute | solution.py:72
  26.0 226.5 %all-gather.8.cloned.1.call-start = ((), (), s32[]{:S(2)}) async-start(), calls=%async_computation.2 | async-start | bytes 2359296 | tf_op jit(solution)/shard_map/all_gather | solution.py:94
  26.1 53.0 %collective-permute-start.3 = (bf16[512,1536]{1,0:T(8,128)(2,1)}, bf16[512,1536]{1,0:T(8,128)(2,1)}, u32[]{:S(2)}, u32[]{:S(2)}) collective-permute-start(bf16[512,1536]{1,0:T(8,128)(2,1)} %refs_7_.3), channel_id=1, source_target_pairs={{0,1},{1,0},{2,3},{3,2},{4,5},{5,4},{6,7},{7,6},{8,9},{9,8},{10,11... | collective-permute-start | bytes 4718600 | tf_op jit(solution)/shard_map/ppermute | solution.py:72
  104.3 23.6 %collective-permute-start.6 = (bf16[256,512]{1,0:T(8,128)(2,1)S(1)}, bf16[256,512]{1,0:T(8,128)(2,1)S(1)}, u32[]{:S(2)}, u32[]{:S(2)}) collective-permute-start(bf16[256,512]{1,0:T(8,128)(2,1)S(1)} %constant_dynamic-slice_fusion.2), channel_id=1, source_target_pairs={{0,2},{2,0},{1,3},{3,1},{4,6},{6,4},{5,7},{7,5},{8,10},{10,8},{9,1... | collective-permute-start | bytes 786440 | tf_op jit(solution)/shard_map/ppermute | solution.py:72
  105.8 87.5 %collective-permute-start.10 = (bf16[512,2048]{1,0:T(8,128)(2,1)}, bf16[512,2048]{1,0:T(8,128)(2,1)}, u32[]{:S(2)}, u32[]{:S(2)}) collective-permute-start(bf16[512,2048]{1,0:T(8,128)(2,1)} %refs_5_.3), channel_id=1, source_target_pairs={{0,1},{1,0},{2,3},{3,2},{4,5},{5,4},{6,7},{7,6},{8,9},{9,8},{10,11... | collective-permute-start | bytes 6291464 | tf_op jit(solution)/shard_map/ppermute | solution.py:72
  105.8 71.6 %collective-permute-start.7 = (bf16[512,512]{1,0:T(8,128)(2,1)S(1)}, bf16[512,512]{1,0:T(8,128)(2,1)S(1)}, u32[]{:S(2)}, u32[]{:S(2)}) collective-permute-start(bf16[512,512]{1,0:T(8,128)(2,1)S(1)} %copy-done.19), channel_id=1, source_target_pairs={{0,2},{2,0},{1,3},{3,1},{4,6},{6,4},{5,7},{7,5},{8,10},{10,8},{9,1... | collective-permute-start | bytes 1572872 | tf_op jit(solution)/shard_map/ppermute | solution.py:72
  120.8 72.5 %collective-permute-start.11 = (bf16[512,2048]{1,0:T(8,128)(2,1)}, bf16[512,2048]{1,0:T(8,128)(2,1)}, u32[]{:S(2)}, u32[]{:S(2)}) collective-permute-start(bf16[512,2048]{1,0:T(8,128)(2,1)} %all-gather.6.cloned.1.call-done.refs_4_.refs_7_), channel_id=1, source_target_pairs={{0,1},{1,0},{2,3},{3,2},{4,5},{5,4},{6,7},{7,6},{8,9},{9,8},{10,11... | collective-permute-start | bytes 6291464 | tf_op jit(solution)/shard_map/ppermute | solution.py:72
  178.0 55.8 %collective-permute-start.14 = (bf16[2368,512]{1,0:T(8,128)(2,1)}, bf16[2368,512]{1,0:T(8,128)(2,1)S(1)}, u32[]{:S(2)}, u32[]{:S(2)}) collective-permute-start(bf16[2368,512]{1,0:T(8,128)(2,1)} %get-tuple-element.97), channel_id=1, source_target_pairs={{0,2},{2,0},{1,3},{3,1},{4,6},{6,4},{5,7},{7,5},{8,10},{10,8},{9,1... | collective-permute-start | bytes 7274504 | tf_op jit(solution)/shard_map/ppermute | solution.py:72
  252.0 43.1 %collective-permute-start.15 = (bf16[2048,1024]{1,0:T(8,128)(2,1)}, bf16[2048,1024]{1,0:T(8,128)(2,1)}, u32[]{:S(2)}, u32[]{:S(2)}) collective-permute-start(bf16[2048,1024]{1,0:T(8,128)(2,1)} %reduce_outer.2.refs_7_.refs_4_), channel_id=1, source_target_pairs={{0,1},{1,0},{2,3},{3,2},{4,5},{5,4},{6,7},{7,6},{8,9},{9,8},{10,11... | collective-permute-start | bytes 12582920 | tf_op jit(solution)/shard_map/ppermute | solution.py:72
  328.5 39.9 %collective-permute-start.16 = (bf16[1024,2048]{1,0:T(8,128)(2,1)}, bf16[1024,2048]{1,0:T(8,128)(2,1)}, u32[]{:S(2)}, u32[]{:S(2)}) collective-permute-start(bf16[1024,2048]{1,0:T(8,128)(2,1)} %expand_outer.2.refs_13_.refs_3_), channel_id=1, source_target_pairs={{0,1},{1,0},{2,3},{3,2},{4,5},{5,4},{6,7},{7,6},{8,9},{9,8},{10,11... | collective-permute-start | bytes 12582920 | tf_op jit(solution)/shard_map/ppermute | solution.py:72
  328.8 64.3 %collective-permute-start.18 = (bf16[2048,512]{1,0:T(8,128)(2,1)}, bf16[2048,512]{1,0:T(8,128)(2,1)}, u32[]{:S(2)}, u32[]{:S(2)}) collective-permute-start(bf16[2048,512]{1,0:T(8,128)(2,1)} %get-tuple-element.104), channel_id=1, source_target_pairs={{0,2},{2,0},{1,3},{3,1},{4,6},{6,4},{5,7},{7,5},{8,10},{10,8},{9,1... | collective-permute-start | bytes 6291464 | tf_op jit(solution)/shard_map/ppermute | solution.py:72
  385.6 75.1 %collective-permute-start.20 = (bf16[512,2048]{1,0:T(8,128)(2,1)}, bf16[512,2048]{1,0:T(8,128)(2,1)}, u32[]{:S(2)}, u32[]{:S(2)}) collective-permute-start(bf16[512,2048]{1,0:T(8,128)(2,1)} %get-tuple-element.109), channel_id=1, source_target_pairs={{0,2},{2,0},{1,3},{3,1},{4,6},{6,4},{5,7},{7,5},{8,10},{10,8},{9,1... | collective-permute-start | bytes 6291464 | tf_op jit(solution)/shard_map/ppermute | solution.py:72
  404.9 105.3 %all-reduce.5.cloned.1.call-start = ((), (), s32[]{:S(2)}) async-start(), calls=%async_computation.3 | async-start | bytes 4194304 | tf_op jit(solution)/shard_map/psum | solution.py:754
  404.9 54.8 %collective-permute-start.21 = (bf16[512,512]{1,0:T(8,128)(2,1)}, bf16[512,512]{1,0:T(8,128)(2,1)S(1)}, u32[]{:S(2)}, u32[]{:S(2)}) collective-permute-start(bf16[512,512]{1,0:T(8,128)(2,1)} %get-tuple-element.111), channel_id=1, source_target_pairs={{0,2},{2,0},{1,3},{3,1},{4,6},{6,4},{5,7},{7,5},{8,10},{10,8},{9,1... | collective-permute-start | bytes 1572872 | tf_op jit(solution)/shard_map/ppermute | solution.py:72
  489.5 125.7 %all-reduce.7.cloned.1.call-start = ((), (), s32[]{:S(2)}) async-start(), calls=%async_computation.4 | async-start | bytes 4194304 | tf_op jit(solution)/shard_map/psum | solution.py:755
  499.2 63.7 %collective-permute-start.19 = (bf16[2368,512]{1,0:T(8,128)(2,1)}, bf16[2368,512]{1,0:T(8,128)(2,1)S(1)}, u32[]{:S(2)}, u32[]{:S(2)}) collective-permute-start(bf16[2368,512]{1,0:T(8,128)(2,1)} %get-tuple-element.107), channel_id=1, source_target_pairs={{0,2},{2,0},{1,3},{3,1},{4,6},{6,4},{5,7},{7,5},{8,10},{10,8},{9,1... | collective-permute-start | bytes 7274504 | tf_op jit(solution)/shard_map/ppermute | solution.py:72
  561.5 36.7 %collective-permute-start.25 = (bf16[512,384]{1,0:T(8,128)(2,1)}, bf16[512,384]{1,0:T(8,128)(2,1)}, u32[]{:S(2)}, u32[]{:S(2)}) collective-permute-start(bf16[512,384]{1,0:T(8,128)(2,1)} %get-tuple-element.118), channel_id=1, source_target_pairs={{0,2},{2,0},{1,3},{3,1},{4,6},{6,4},{5,7},{7,5},{8,10},{10,8},{9,1... | collective-permute-start | bytes 1179656 | tf_op jit(solution)/shard_map/ppermute | solution.py:72
  598.2 144.3 %all-reduce.9.cloned.1.call-start = ((), (), s32[]{:S(2)}) async-start(), calls=%async_computation.5 | async-start | bytes 2621440 | tf_op jit(solution)/shard_map/psum | solution.py:775
  644.6 49.3 %collective-permute-start.36 = (bf16[256,768]{1,0:T(8,128)(2,1)S(1)}, bf16[256,768]{1,0:T(8,128)(2,1)}, u32[]{:S(2)}, u32[]{:S(2)}) collective-permute-start(bf16[256,768]{1,0:T(8,128)(2,1)S(1)} %fusion), channel_id=1, source_target_pairs={{0,4},{4,0},{8,12},{12,8},{16,20},{20,16},{24,28},{28,24},{1,5},{5... | collective-permute-start | bytes 1179656 | tf_op jit(solution)/shard_map/ppermute | solution.py:104
  669.1 55.8 %collective-permute-start.27 = (bf16[1184,512]{1,0:T(8,128)(2,1)}, bf16[1184,512]{1,0:T(8,128)(2,1)}, u32[]{:S(2)}, u32[]{:S(2)}) collective-permute-start(bf16[1184,512]{1,0:T(8,128)(2,1)} %get-tuple-element.121), channel_id=1, source_target_pairs={{0,2},{2,0},{1,3},{3,1},{4,6},{6,4},{5,7},{7,5},{8,10},{10,8},{9,1... | collective-permute-start | bytes 3637256 | tf_op jit(solution)/shard_map/ppermute | solution.py:72
  691.5 22.9 %collective-permute-start.30 = (f32[6144]{0:T(1024)S(1)}, f32[6144]{0:T(1024)S(1)}, u32[]{:S(2)}, u32[]{:S(2)}) collective-permute-start(f32[6144]{0:T(1024)S(1)} %reshape.83), channel_id=1, source_target_pairs={{0,1},{1,0},{2,3},{3,2},{4,5},{5,4},{6,7},{7,6},{8,9},{9,8},{10,11... | collective-permute-start | bytes 73736 | tf_op jit(solution)/shard_map/ppermute | solution.py:104
  696.7 47.9 %collective-permute-start.29 = (bf16[1184,512]{1,0:T(8,128)(2,1)}, bf16[1184,512]{1,0:T(8,128)(2,1)}, u32[]{:S(2)}, u32[]{:S(2)}) collective-permute-start(bf16[1184,512]{1,0:T(8,128)(2,1)} %get-tuple-element.124), channel_id=1, source_target_pairs={{0,2},{2,0},{1,3},{3,1},{4,6},{6,4},{5,7},{7,5},{8,10},{10,8},{9,1... | collective-permute-start | bytes 3637256 | tf_op jit(solution)/shard_map/ppermute | solution.py:72
  (63 other events, 1103.2 us)
Sparse Core Ops, SparseCore 0:
  24.3 45.6 all-gather.3
  72.7 48.0 all-gather.5
  180.3 46.8 all-gather.7
  409.6 100.5 all-reduce.4
  513.6 101.5 all-reduce.6
  647.5 88.6 all-reduce.8

commit v3 on v2

--- a/solution.py
+++ b/solution.py
@@ -20,6 +20,7 @@
 KEYS_A = 512
 EXPAND_CUT = 1024
 LIGHT = 128
+PIECES = (slice(0, 304), slice(304, PAD))
 QUERY_CUTS = (0, 208, 400, PAD)
 MEBI = 1 << 20
 
@@ -243,17 +244,17 @@
     rows, cols = shape
     x_refs, weights = refs[:rows], grid_of(refs[rows : rows + rows * cols], shape)
     normed_ref, packed_ref = refs[rows + rows * cols :]
-    scaled, _ = normalize([x[...].astype(F32) for x in x_refs])
-    width = scaled[0].shape[1]
+    width, block = weights[0][0].shape
     gains, shifts = cut(gain_ref[...], width), cut(shift_ref[...], width)
-    normed = [(x * g + b).astype(BF) for x, g, b in zip(scaled, gains, shifts)]
-    for i, n in enumerate(normed):
-        normed_ref[:, i * width : (i + 1) * width] = n
-    block = weights[0][0].shape[1]
-    for j in range(cols):
-        total = sum(dot_nn(n, weights[i][j][...]) for i, n in enumerate(normed))
-        where = slice(j * block, (j + 1) * block)
-        packed_ref[:, where] = (total + bias_ref[:, where]).astype(BF)
+    for some in PIECES:
+        scaled, _ = normalize([x[some, :].astype(F32) for x in x_refs])
+        normed = [(x * g + b).astype(BF) for x, g, b in zip(scaled, gains, shifts)]
+        for i, n in enumerate(normed):
+            normed_ref[some, i * width : (i + 1) * width] = n
+        for j in range(cols):
+            total = sum(dot_nn(n, weights[i][j][...]) for i, n in enumerate(normed))
+            where = slice(j * block, (j + 1) * block)
+            packed_ref[some, where] = (total + bias_ref[:, where]).astype(BF)
 
 
 def swap_halves(values):
@@ -288,18 +289,17 @@
         o_ref[units[n][0], :] = (mixed / swap_halves(totals)).astype(BF)
 
 
-def attend(packed, half, into, after):
+def attend(packed, first, some, into, after):
     tokens, width = packed.shape
     pairs = width // (6 * HD)
-    some = pairs // 2
     return call(
         attend_kernel,
         "attend",
         (some, tokens // PAD),
-        [(pl.BlockSpec((PAD, 6 * HD), lambda h, i: (i, half * some + h)), packed)],
+        [(pl.BlockSpec((PAD, 6 * HD), lambda h, i: (i, first + h)), packed)],
         [
             (
-                pl.BlockSpec((PAD, 2 * HD), lambda h, i: (i, half * some + h)),
+                pl.BlockSpec((PAD, 2 * HD), lambda h, i: (i, first + h)),
                 (tokens, pairs * 2 * HD),
                 BF,
             )
@@ -380,17 +380,25 @@
     x_refs, weights = refs[:rows], grid_of(refs[rows : rows + rows * cols], shape)
     middle_ref, normed_ref = refs[rows + rows * cols :]
     block, width = weights[0][0].shape
-    mixed = cut(mixed_ref[...], block)
-    middle = []
-    for i in range(rows):
-        total = sum(dot_nn(m, weights[i][j][...]) for j, m in enumerate(mixed))
-        where = slice(i * width, (i + 1) * width)
-        middle.append(x_refs[i][...].astype(F32) + total + bias_ref[:, where])
-        middle_ref[:, where] = middle[-1]
-    scaled, _ = normalize(middle)
-    for i, x in enumerate(scaled):
-        where = slice(i * width, (i + 1) * width)
-        normed_ref[:, where] = (x * gain_ref[:, where] + shift_ref[:, where]).astype(BF)
+    spans = [slice(i * width, (i + 1) * width) for i in range(rows)]
+    totals = []
+    for some in PIECES:
+        mixed = cut(mixed_ref[some, :], block)
+        totals.append(
+            [
+                sum(dot_nn(m, weights[i][j][...]) for j, m in enumerate(mixed))
+                for i in range(rows)
+            ]
+        )
+    for some, total in zip(PIECES, totals):
+        middle = []
+        for i, where in enumerate(spans):
+            middle.append(x_refs[i][some, :].astype(F32) + total[i] + bias_ref[:, where])
+            middle_ref[some, where] = middle[-1]
+        scaled, _ = normalize(middle)
+        for x, where in zip(scaled, spans):
+            normed = x * gain_ref[:, where] + shift_ref[:, where]
+            normed_ref[some, where] = normed.astype(BF)
 
 
 def expand_kernel(shape, bias_ref, normed_ref, *refs):
@@ -398,20 +406,28 @@
     weights = grid_of(refs[: rows * cols], shape)
     hidden_ref, slope_ref = refs[rows * cols :]
     depth, block = weights[0][0].shape
-    normed = cut(normed_ref[...], depth)
-    some = min(block, EXPAND_CUT)
-    cuts = [(j, at) for j in range(cols) for at in range(0, block, some)]
+    cuts = [
+        (some, j, at)
+        for some in PIECES
+        for j in range(cols)
+        for at in range(0, block, min(block, EXPAND_CUT))
+    ]
+    normed = {some.start: cut(normed_ref[some, :], depth) for some in PIECES}
+    wide = min(block, EXPAND_CUT)
     totals = [
-        sum(dot_nn(n, weights[i][j][:, at : at + some]) for i, n in enumerate(normed))
-        for j, at in cuts
+        sum(
+            dot_nn(n, weights[i][j][:, at : at + wide])
+            for i, n in enumerate(normed[some.start])
+        )
+        for some, j, at in cuts
     ]
-    for (j, at), total in zip(cuts, totals):
-        where = slice(j * block + at, j * block + at + some)
+    for (some, j, at), total in zip(cuts, totals):
+        where = slice(j * block + at, j * block + at + wide)
         before = total + bias_ref[:, where]
         below = 0.5 + 0.5 * lax.erf(before * ROOT_HALF)
-        hidden_ref[:, where] = (before * below).astype(BF)
+        hidden_ref[some, where] = (before * below).astype(BF)
         density = jnp.exp2(before * before * (-0.5 * LOG2E)) * DENSITY
-        slope_ref[:, where] = (below + before * density).astype(BF)
+        slope_ref[some, where] = (below + before * density).astype(BF)
 
 
 def reduce_kernel(shape, valid_ref, bias_ref, hidden_ref, middle_ref, *refs):
@@ -465,26 +481,33 @@
             ref[...] = jnp.zeros_like(ref)
 
     width, block = expand[0][0].shape
-    upstream = [
-        sum(dot_nt(before_ref[:, j * block : (j + 1) * block], expand[i][j][...]) for j in range(cols))
-        for i in range(rows)
+    spans = [slice(i * width, (i + 1) * width) for i in range(rows)]
+    heads = output[0][0].shape[0]
+    upstreams = [
+        [
+            sum(
+                dot_nt(before_ref[some, j * block : (j + 1) * block], expand[i][j][...])
+                for j in range(cols)
+            )
+            for i in range(rows)
+        ]
+        for some in PIECES
     ]
-    scaled, inverse = normalize(cut(middle_ref[...], width))
-    parts = norm_back(upstream, scaled, inverse, cut(gain_ref[...], width))
-    lows = []
-    for i, part in enumerate(parts):
-        where = slice(i * width, (i + 1) * width)
-        add_rows(gain_grad, upstream[i] * scaled[i], i * width)
-        add_rows(shift_grad, upstream[i], i * width)
-        grad = g_refs[i][...].astype(F32) + part
-        add_rows(bias_grad, grad, i * width)
-        middle_grad_ref[:, where] = grad
-        lows.append(grad.astype(BF))
-        low_refs[i][...] = lows[-1]
-    heads = output[0][0].shape[0]
-    for j in range(cols):
-        total = sum(dot_nt(low, output[i][j][...]) for i, low in enumerate(lows))
-        mixed_low_ref[:, j * heads : (j + 1) * heads] = total.astype(BF)
+    for some, upstream in zip(PIECES, upstreams):
+        scaled, inverse = normalize(cut(middle_ref[some, :], width))
+        parts = norm_back(upstream, scaled, inverse, cut(gain_ref[...], width))
+        lows = []
+        for i, part in enumerate(parts):
+            add_rows(gain_grad, upstream[i] * scaled[i], i * width)
+            add_rows(shift_grad, upstream[i], i * width)
+            grad = g_refs[i][some, :].astype(F32) + part
+            add_rows(bias_grad, grad, i * width)
+            middle_grad_ref[some, spans[i]] = grad
+            lows.append(grad.astype(BF))
+            low_refs[i][some, :] = lows[-1]
+        for j in range(cols):
+            total = sum(dot_nt(low, output[i][j][...]) for i, low in enumerate(lows))
+            mixed_low_ref[some, j * heads : (j + 1) * heads] = total.astype(BF)
 
 
 def project_back_kernel(shape, parts, gain_ref, middle_ref, *refs):
@@ -500,23 +523,28 @@
             ref[...] = jnp.zeros_like(ref)
 
     width = weights[0][0].shape[0]
-    upstream = [0.0] * rows
-    at = 0
     for p in range(parts):
         add_rows(bias_grads[p], packed[p][...].astype(F32))
-        some = packed[p].shape[1] // cols
-        for j in range(cols):
-            grad = packed[p][:, j * some : (j + 1) * some]
-            for i in range(rows):
-                upstream[i] += dot_nt(grad, weights[i][j][:, at : at + some])
-        at += some
-    scaled, inverse = normalize([x[...].astype(F32) for x in x_refs])
-    grads = norm_back(upstream, scaled, inverse, cut(gain_ref[...], width))
-    for i, grad in enumerate(grads):
-        add_rows(gain_grad, upstream[i] * scaled[i], i * width)
-        add_rows(shift_grad, upstream[i], i * width)
-        total = middle_ref[:, i * width : (i + 1) * width] + grad
-        o_refs[i][...] = total.astype(o_refs[i].dtype)
+    upstreams = []
+    for piece in PIECES:
+        upstream = [0.0] * rows
+        at = 0
+        for p in range(parts):
+            some = packed[p].shape[1] // cols
+            for j in range(cols):
+                grad = packed[p][piece, j * some : (j + 1) * some]
+                for i in range(rows):
+                    upstream[i] += dot_nt(grad, weights[i][j][:, at : at + some])
+            at += some
+        upstreams.append(upstream)
+    for piece, upstream in zip(PIECES, upstreams):
+        scaled, inverse = normalize([x[piece, :].astype(F32) for x in x_refs])
+        grads = norm_back(upstream, scaled, inverse, cut(gain_ref[...], width))
+        for i, grad in enumerate(grads):
+            add_rows(gain_grad, upstream[i] * scaled[i], i * width)
+            add_rows(shift_grad, upstream[i], i * width)
+            total = middle_ref[piece, i * width : (i + 1) * width] + grad
+            o_refs[i][piece, :] = total.astype(o_refs[i].dtype)
 
 
 def outer_kernel(rights, received, whole_width, a_ref, *refs):
@@ -557,7 +585,7 @@
         [(part, (lw // down, rw // across), BF)] * (down * across),
         tokens * lw * rw,
         after,
-        weight=LIGHT,
+        weight=1 if name in ("reduce_outer", "expand_outer") else LIGHT,
     )
 
 
@@ -650,11 +678,12 @@
         tokens * 3 * D * D,
     )
     grads = to_tokens(output_grad, True, (packed,))
-    expand_blocks = gather_shares(expand_weight, expand_shares)
     (reduce_shares,) = fetch_shares([hold(reduce_weight, packed)])
-    mixed = attend(packed, 0, None, (*expand_shares, *reduce_shares, grads[0]))
+    pairs = packed.shape[1] // (6 * HD)
+    mixed = attend(packed, 0, pairs // 4, None, (*expand_shares, *reduce_shares, grads[0]))
+    expand_blocks = gather_shares(expand_weight, expand_shares, mixed)
     reduce_shares = hold(reduce_shares, mixed)
-    mixed = attend(packed, 1, mixed, reduce_shares)
+    mixed = attend(packed, pairs // 4, pairs - pairs // 4, mixed, reduce_shares)
     output_blocks = [gather_blocks(block, "col") for block in hold(output_rows, mixed)]
     middle, second_normed = call(
         partial(output_kernel, shape),
@@ -674,6 +703,7 @@
         [full(expand_bias), image(second_normed)] + flat(expand_blocks),
         [out(hidden_width, BF), out(hidden_width, BF)],
         tokens * D * hidden_width,
+        (*reduce_blocks[0][1:], *reduce_blocks[-1][:1]),
     )
     def add_parts(parts, axis, after=None):
         held = parts[0].astype(F32)
@@ -701,9 +731,13 @@
         return outer(left, rights, *where, name, (*order, *after), received, splits)
 
     def share_of(held, after=None):
-        return add_parts(held, "row", after).astype(BF)
-
-    reduce_others = outer_others(hidden, grads, True, "reduce_outer")
+        received = [shift(part, "row", s) for s, part in enumerate(held) if s]
+        total = held[0].astype(F32)
+        for part in received if after is None else hold(received, after):
+            total = total + part.astype(F32)
+        return total.astype(BF), received
+
+    reduce_others = outer_others(hidden, grads, True, "reduce_outer", reduce_blocks[-1][:1])
     before_low, reduce_bias_grad, expand_bias_grad = call(
         partial(reduce_back_kernel, shape),
         "reduce_back",
@@ -715,7 +749,7 @@
         weight=LIGHT,
     )
     reduce_held = outer_own(hidden, grads, True, "reduce_outer", reduce_others, (before_low,))
-    reduce_share = share_of(reduce_held)
+    reduce_share, reduce_received = share_of(reduce_held)
     expand_others = outer_others(
         second_normed, [before_low], False, "expand_outer", reduce_held[:1]
     )
@@ -733,10 +767,10 @@
         weight=LIGHT,
     )
     expand_held = outer_own(
-        second_normed, [before_low], False, "expand_outer", expand_others, (middle_grad,)
+        second_normed, [before_low], False, "expand_outer", expand_others, (middle_grad, *reduce_received)
     )
     output_others = outer_others(mixed, middle_lows, True, "output_outer", expand_held[:1])
-    output_held = outer_own(mixed, middle_lows, True, "output_outer", output_others, (reduce_share,))
+    output_held = outer_own(mixed, middle_lows, True, "output_outer", output_others)
     results = call(
         partial(reduce_kernel, shape),
         "reduce",
@@ -749,13 +783,13 @@
     )
     block_output = unpack_rows([[part] for part in sent(results)], row_index, BF)
 
-    expand_share = share_of(expand_held, results[0])
-    output_share = share_of(output_held, results[0])
     reduce_weight_grad = lax.psum(reduce_share, "dp")
-    expand_weight_grad = lax.psum(hold(expand_share, reduce_weight_grad), "dp")
+    expand_share, _ = share_of(expand_held, reduce_weight_grad)
+    output_share, output_received = share_of(output_held)
+    expand_weight_grad, output_weight_grad = lax.psum((expand_share, output_share), "dp")
     pairs = 3 * D // (6 * HD) // cols
     counts = [pairs - 2, 1, 1] if pairs > 2 else [pairs]
-    packed_lows, held, shares, pair = [], [], [], 0
+    packed_lows, held, shares, halved, arrived, pair = [], [], [], [], (), 0
     ready = results[:1]
     for g, count in enumerate(counts):
         packed_low = None
@@ -763,22 +797,28 @@
             packed_low = attend_back(
                 packed, mixed_low, cols, pair, slot, count, packed_low, ready
             )
-            ready = (expand_share, output_share) if pair == 0 else ()
+            ready = output_received if pair == 0 else ()
             pair += 1
         packed_lows.append(packed_low)
-        ready = (expand_weight_grad, *shares[1:]) if pair == pairs else ()
-        others = outer_others(first_normed, [packed_low], False, "project_outer", ready)
-        held.append(outer_own(first_normed, [packed_low], False, "project_outer", others))
-        shares.append(share_of(held[-1]))
+        last, own_last = (reduce_weight_grad,) if g == 0 else (), ()
+        if g == 2:
+            last, own_last = (expand_weight_grad, halved[1]), (halved[2],)
+        others = outer_others(first_normed, [packed_low], False, "project_outer", last)
+        held.append(outer_own(first_normed, [packed_low], False, "project_outer", others, own_last))
         ready = (held[g][0],)
-        ready += (shares[g - 1], block_output) if g > 0 else (reduce_weight_grad,)
-    output_weight_grad, first_sum = lax.psum(
-        hold((output_share, shares[0]), expand_weight_grad), "dp"
-    )
-    attend_weight_grad = [first_sum]
-    if len(shares) > 1:
-        attend_weight_grad.append(sum_shares(jnp.concatenate(shares[1:], 1), "dp"))
-    attend_weight_grad = jnp.concatenate(attend_weight_grad, 1)
+        if g == 0:
+            shares.append(share_of(held[0])[0])
+            halved.append(shares[0])
+            for hop in steps_of("dp"):
+                halved.append(halve(halved[-1], "dp", hop))
+        elif g == 1:
+            shares.append(share_of(held[1])[0])
+            ready += (block_output, shares[0])
+        else:
+            ready += (halved[3],)
+    joined = halved[-1:]
+    for hop in reversed(steps_of("dp")):
+        joined.append(join(joined[-1], "dp", hop))
 
     halves = 2 if images % 2 == 0 else 1
     some = images // halves
@@ -810,12 +850,19 @@
             weight=LIGHT,
         )
         input_grads.append(sent(results[:rows]))
-        ready = (results[0], shares[-1])
+        if half == 0 and len(counts) > 1:
+            share, arrived = share_of(held[-1], results[0])
+            shares.append(share)
+        ready = (results[0], *arrived, joined[1])
         packed_sums = [v.reshape(cols, -1, 3, HD) for v in results[rows + 2 :]]
         late = (*results[rows : rows + 2], jnp.concatenate(packed_sums, 1))
         sums = late if half == 0 else jax.tree.map(jnp.add, sums, late)
-    input_grad = unpack_rows(list(zip(*hold(input_grads, first_sum))), row_index, F32)
+    input_grad = unpack_rows(list(zip(*input_grads)), row_index, F32)
     first_gain_grad, first_shift_grad, packed_sums = sums
+    attend_weight_grad = joined[-1:]
+    if len(shares) > 1:
+        attend_weight_grad.append(sum_shares(jnp.concatenate(shares[1:], 1), "dp"))
+    attend_weight_grad = jnp.concatenate(attend_weight_grad, 1)
 
     feature_grads = jnp.concatenate(
         [

time: 775 us -> 778 us (level)
  starting transfers between devices: 34.8 us -> 47.3 us
    psum x2 -> x1, waiting for transfers between devices: 15.2 us -> 38.2 us  [body(): lax.psum((expand_share, output_share), 'dp')]
    all_gather x3, waiting for transfers between devices: 58.2 us -> 44 us  [gather_shares(): blocks = [lax.all_gather(s, 'dp', axis=0, tiled=True) for s in shares]]
    ppermute x11 -> x17, starting transfers between devices: 9.87 us -> 23.2 us  [swap(): lax.ppermute(values, axis, [(i, i ^ step) for i in range(lax.axis_size(ax...]
    psum x1, waiting for transfers between devices: 10.1 us -> 0.02 us  [body(): reduce_weight_grad = lax.psum(reduce_share, 'dp')]
    ppermute x11 -> x17, waiting for transfers between devices: 33.5 us -> 30.7 us  [swap(): lax.ppermute(values, axis, [(i, i ^ step) for i in range(lax.axis_size(ax...]
  transfers between devices with their start and end apart: 49 -> 54, of which waited for: 20 -> 18; matrix products, arithmetic and copies ran while one was open for 4% -> 5% of each run, Pallas kernels for 61% -> 58%
where the time goes in v3:
time: 778 us; the launch traced here: 769 us
  Pallas kernels  505 us (65%)
  waiting for transfers between devices  151 us (19%)
  starting transfers between devices  47.3 us (6%)
  other arithmetic  31.1 us (4%)
  local copies, waits for them, and re-layouts  20.1 us (3%)
  between operations  15 us (2%)
    pallas_call x26, Pallas kernels, call(): pl.pallas_call(body_of, grid=grid, in_specs=[s for s, _ in operands] + [p...  479 us
    all_gather x3, waiting for transfers between devices, gather_shares(): blocks = [lax.all_gather(s, 'dp', axis=0, tiled=True) for s in shares]  44 us
    psum x1, waiting for transfers between devices, body(): lax.psum((expand_share, output_share), 'dp')  38.2 us
    ppermute x32, waiting for transfers between devices, shift(): lax.ppermute(values, axis, [(i, (i + step) % size) for i in range(size)])  38 us
    ppermute x17, waiting for transfers between devices, swap(): lax.ppermute(values, axis, [(i, i ^ step) for i in range(lax.axis_size(ax...  30.7 us
    ppermute x32, starting transfers between devices, shift(): lax.ppermute(values, axis, [(i, (i + step) % size) for i in range(size)])  23.8 us
    ppermute x17, starting transfers between devices, swap(): lax.ppermute(values, axis, [(i, i ^ step) for i in range(lax.axis_size(ax...  23.2 us
  transfers between devices with their start and end apart: 54, of which 18 were waited for; matrix products, arithmetic and copies ran while one was open for 5% of the time, Pallas kernels for 58%

profile of v3, /device:TPU:0, one launch (start us, length us, event | category | flops | bytes accessed | tf_op | source)
XLA Modules:
  0.0 769.3 jit_solution(15495204561890707861)
XLA Ops:
  26.0 44.0 %all-gather.4.cloned.1.call-done.refs_7_.refs_9_ = bf16[512,1536]{1,0:T(8,128)(2,1)} async-done(((bf16[64,1536]{1,0:T(8,128)(2,1)}), bf16[512,1536]{1,0:T(8,128)(2,1)}) %all-gather.4.cloned.1.call-update) | async-done | bytes 1572880 | tf_op jit(solution)/shard_map/all_gather | solution.py:95
  80.5 22.0 %project.1 = (bf16[2368,1024]{1,0:T(8,128)(2,1)}, bf16[2368,3072]{1,0:T(8,128)(2,1)}) custom-call(f32[1,1024]{1,0:T(1,128)} %get-tuple-element.151.refs_0_, f32[1,1024]{1,0:T(1,128)} %get-tuple-element.150.refs_1_, f32[1,3072]{1,0:T(1,128)} %reshape.82.refs_2_, bf16[2368,512]{1,0:T(8,128)(2,1)} %get-tuple-element.75.refs_3_.refs_4_.refs_5_, ...), custom_call_target="tpu_custom_call" | custom-call | flops 14898167808 | bytes 30560256 | tf_op jit(solution)/shard_map/project/pallas_call | solution.py:58
  112.8 13.1 %attend.2.refs_1_ = bf16[2368,1024]{1,0:T(8,128)(2,1)} custom-call(bf16[2368,3072]{1,0:T(8,128)(2,1)} %get-tuple-element.78.refs_0_, bf16[64,2048]{1,0:T(8,128)(2,1)} %slice.87.refs_1_, bf16[256,512]{1,0:T(8,128)(2,1)} %copy-done.18, bf16[2368,512]{1,0:T(8,128)(2,1)} %get-tuple-element.81.refs_3_.refs_1_), custom_call_target="tpu_custom_call" | custom-call | flops 3588751360 | bytes 19398656 | tf_op jit(solution)/shard_map/attend/pallas_call | solution.py:58
  127.2 35.7 %attend.3.refs_3_.refs_0_ = bf16[2368,1024]{1,0:T(8,128)(2,1)} custom-call(bf16[2368,3072]{1,0:T(8,128)(2,1)} %get-tuple-element.78.refs_0_, bf16[2368,1024]{1,0:T(8,128)(2,1)} %attend.2.refs_1_, bf16[256,512]{1,0:T(8,128)(2,1)} %copy-done.18), custom_call_target="tpu_custom_call", output_to_operand_aliasing={{}: (1, {})} | custom-call | flops 10766254080 | bytes 19398656 | tf_op jit(solution)/shard_map/attend/pallas_call | solution.py:58
  167.1 12.9 %output.1 = (f32[2368,1024]{1,0:T(8,128)}, bf16[2368,1024]{1,0:T(8,128)(2,1)}) custom-call(f32[1,1024]{1,0:T(1,128)} %get-tuple-element.154.refs_0_, f32[1,1024]{1,0:T(1,128)} %get-tuple-element.153.refs_1_.refs_0_, f32[1,1024]{1,0:T(1,128)} %get-tuple-element.152.refs_2_, bf16[2368,1024]{1,0:T(8,128)(2,1)} %attend.3.refs_3_.refs_0_, ...), custom_call_target="tpu_custom_call" | custom-call | flops 4966055936 | bytes 26357760 | tf_op jit(solution)/shard_map/output/pallas_call | solution.py:58
  180.0 35.7 %expand.1 = (bf16[2368,4096]{1,0:T(8,128)(2,1)}, bf16[2368,4096]{1,0:T(8,128)(2,1)}) custom-call(f32[1,4096]{1,0:T(1,128)} %bitcast.15, bf16[2368,1024]{1,0:T(8,128)(2,1)} %get-tuple-element.86.refs_1_.refs_0_, bf16[512,2048]{1,0:T(8,128)(2,1)} %refs_5_.3, bf16[512,2048]{1,0:T(8,128)(2,1)} %collective-permute-done.10.refs_3_.refs_6_, ...), custom_call_target="tpu_custom_call" | custom-call | flops 19864223744 | bytes 52051968 | tf_op jit(solution)/shard_map/expand/pallas_call | solution.py:58
  221.6 16.8 %reduce_outer.2.refs_7_.refs_4_ = bf16[2048,1024]{1,0:T(8,128)(2,1)} custom-call(bf16[2368,4096]{1,0:T(8,128)(2,1)} %get-tuple-element.89.refs_0_.refs_2_, bf16[2368,512]{1,0:T(8,128)(2,1)} %get-tuple-element.81.refs_3_.refs_1_, bf16[2368,512]{1,0:T(8,128)(2,1)} %copy-done, bf16[2048,512]{1,0:T(8,128)(2,1)} %all-gather.8.cloned.1.call-done.refs_7_.refs_3_.refs_5_.refs_6_), custom_call_target="tpu_custom_call" | custom-call | flops 9932111872 | bytes 28442624 | tf_op jit(solution)/shard_map/reduce_outer/pallas_call | solution.py:58
  239.0 9.5 %collective-permute-done.13.refs_6_.refs_7_ = bf16[2048,512]{1,0:T(8,128)(2,1)S(1)} collective-permute-done((bf16[2048,512]{1,0:T(8,128)(2,1)}, bf16[2048,512]{1,0:T(8,128)(2,1)S(1)}, u32[]{:S(2)}, u32[]{:S(2)}) %collective-permute-start.13) | collective-permute-done | bytes 2097184 | tf_op jit(solution)/shard_map/ppermute | solution.py:73
  249.8 29.6 %reduce_back.1 = (bf16[2368,4096]{1,0:T(8,128)(2,1)}, f32[1,1024]{1,0:T(1,128)}, f32[1,4096]{1,0:T(1,128)}) custom-call(bf16[2368,4096]{1,0:T(8,128)(2,1)} %get-tuple-element.91.refs_0_, bf16[2368,512]{1,0:T(8,128)(2,1)} %get-tuple-element.81.refs_3_.refs_1_, bf16[2368,512]{1,0:T(8,128)(2,1)} %copy-done, bf16[2048,512]{1,0:T(8,128)(2,1)} %refs_4_.1, ...), custom_call_target="tpu_custom_call" | custom-call | flops 155189248 | bytes 406688 | tf_op jit(solution)/shard_map/reduce_back/pallas_call | solution.py:58
  279.5 16.7 %reduce_outer.3 = (bf16[2048,512]{1,0:T(8,128)(2,1)}, bf16[2048,512]{1,0:T(8,128)(2,1)}) custom-call(bf16[2368,4096]{1,0:T(8,128)(2,1)} %get-tuple-element.89.refs_0_.refs_2_, bf16[2368,512]{1,0:T(8,128)(2,1)} %get-tuple-element.81.refs_3_.refs_1_, bf16[2368,512]{1,0:T(8,128)(2,1)} %copy-done, bf16[2048,1024]{1,0:T(8,128)(2,1)} %collective-permute-done.15.refs_3_, ...), custom_call_target="tpu_custom_call" | custom-call | flops 9932111872 | bytes 32636928 | tf_op jit(solution)/shard_map/reduce_outer/pallas_call | solution.py:58
  296.1 16.6 %expand_outer.2.refs_13_.refs_3_ = bf16[1024,2048]{1,0:T(8,128)(2,1)} custom-call(bf16[2368,1024]{1,0:T(8,128)(2,1)} %get-tuple-element.86.refs_1_.refs_0_, bf16[2368,4096]{1,0:T(8,128)(2,1)} %get-tuple-element.93.refs_5_.refs_1_, bf16[2048,512]{1,0:T(8,128)(2,1)} %get-tuple-element.94.refs_2_), custom_call_target="tpu_custom_call" | custom-call | flops 9932111872 | bytes 28442624 | tf_op jit(solution)/shard_map/expand_outer/pallas_call | solution.py:58
  314.5 37.4 %expand_back.1 = (f32[2368,1024]{1,0:T(8,128)}, bf16[2368,1024]{1,0:T(8,128)(2,1)}, f32[1,1024]{1,0:T(1,128)}, f32[1,1024]{1,0:T(1,128)}, f32[1,1024]{1,0:T(1,12...) custom-call(f32[1,1024]{1,0:T(1,128)} %get-tuple-element.153.refs_1_.refs_0_, ...), custom_call_target="tpu_custom_call" | custom-call | flops 193986560 | bytes 498816 | tf_op jit(solution)/shard_map/expand_back/pallas_call | solution.py:58
  365.3 17.3 %expand_outer.3 = (bf16[512,2048]{1,0:T(8,128)(2,1)}, bf16[512,2048]{1,0:T(8,128)(2,1)}) custom-call(bf16[2368,1024]{1,0:T(8,128)(2,1)} %get-tuple-element.86.refs_1_.refs_0_, bf16[2368,4096]{1,0:T(8,128)(2,1)} %get-tuple-element.93.refs_5_.refs_1_, bf16[1024,2048]{1,0:T(8,128)(2,1)} %collective-permute-done.16.refs_2_, ...), custom_call_target="tpu_custom_call" | custom-call | flops 9932111872 | bytes 32636928 | tf_op jit(solution)/shard_map/expand_outer/pallas_call | solution.py:58
  403.3 27.2 %reduce.11 = (bf16[2368,512]{1,0:T(8,128)(2,1)}, bf16[2368,512]{1,0:T(8,128)(2,1)}) custom-call(s32[4]{0:T(128)} %dynamic_slice.51.refs_0_, f32[1,1024]{1,0:T(1,128)} %get-tuple-element.155.refs_1_, bf16[2368,4096]{1,0:T(8,128)(2,1)} %get-tuple-element.89.refs_0_.refs_2_, f32[2368,1024]{1,0:T(8,128)} %get-tuple-element.90.refs_2_.refs_3_, ...), custom_call_target="tpu_custom_call" | custom-call | flops 155189248 | bytes 330784 | tf_op jit(solution)/shard_map/reduce/pallas_call | solution.py:58
  431.9 25.2 %attend_back.4.refs_2_ = bf16[2368,1536]{1,0:T(8,128)(2,1)} custom-call(bf16[2368,3072]{1,0:T(8,128)(2,1)} %get-tuple-element.78.refs_0_, bf16[2368,1024]{1,0:T(8,128)(2,1)} %get-tuple-element.103.refs_1_, bf16[2368,512]{1,0:T(8,128)(2,1)} %get-tuple-element.101.refs_0_.refs_2_), custom_call_target="tpu_custom_call" | custom-call | flops 67289088 | bytes 208384 | tf_op jit(solution)/shard_map/attend_back/pallas_call | solution.py:58
  457.9 25.5 %attend_back.5.refs_1_.refs_2_ = bf16[2368,1536]{1,0:T(8,128)(2,1)} custom-call(bf16[2368,3072]{1,0:T(8,128)(2,1)} %get-tuple-element.78.refs_0_, bf16[2368,1024]{1,0:T(8,128)(2,1)} %get-tuple-element.103.refs_1_, bf16[2368,1536]{1,0:T(8,128)(2,1)} %attend_back.4.refs_2_, bf16[512,512]{1,0:T(8,128)(2,1)} %copy-done.12), custom_call_target="tpu_custom_call", output_to_operand_aliasing={{}: (2, {})} | custom-call | flops 67289088 | bytes 208384 | tf_op jit(solution)/shard_map/attend_back/pallas_call | solution.py:58
  483.4 9.1 %project_outer.6.refs_3_ = bf16[1024,768]{1,0:T(8,128)(2,1)} custom-call(bf16[2368,1024]{1,0:T(8,128)(2,1)} %get-tuple-element.105.refs_0_, bf16[2368,1536]{1,0:T(8,128)(2,1)} %attend_back.5.refs_1_.refs_2_, bf16[2048,512]{1,0:T(8,128)(2,1)} %all-reduce.4.cloned.1.call-done.refs_2_), custom_call_target="tpu_custom_call" | custom-call | flops 29097984 | bytes 107008 | tf_op jit(solution)/shard_map/project_outer/pallas_call | solution.py:58
  497.3 9.3 %project_outer.7 = (bf16[512,768]{1,0:T(8,128)(2,1)}, bf16[512,768]{1,0:T(8,128)(2,1)}) custom-call(bf16[2368,1024]{1,0:T(8,128)(2,1)} %get-tuple-element.105.refs_0_, bf16[2368,1536]{1,0:T(8,128)(2,1)} %attend_back.5.refs_1_.refs_2_, bf16[1024,768]{1,0:T(8,128)(2,1)} %collective-permute-done.21.refs_2_, bf16[1024,768]{1,0:T(8,128)(2,1)} %project_outer.6.refs_3_), custom_call_target="tpu_custom_call" | custom-call | flops 29097984 | bytes 119296 | tf_op jit(solution)/shard_map/project_outer/pallas_call | solution.py:58
  507.4 25.2 %attend_back.6.refs_1_.refs_3_ = bf16[2368,768]{1,0:T(8,128)(2,1)} custom-call(bf16[2368,3072]{1,0:T(8,128)(2,1)} %get-tuple-element.78.refs_0_, bf16[2368,1024]{1,0:T(8,128)(2,1)} %get-tuple-element.103.refs_1_, bf16[512,768]{1,0:T(8,128)(2,1)} %get-tuple-element.106.refs_2_), custom_call_target="tpu_custom_call" | custom-call | flops 67289088 | bytes 179968 | tf_op jit(solution)/shard_map/attend_back/pallas_call | solution.py:58
  554.4 25.3 %attend_back.7.refs_1_.refs_4_ = bf16[2368,768]{1,0:T(8,128)(2,1)} custom-call(bf16[2368,3072]{1,0:T(8,128)(2,1)} %get-tuple-element.78.refs_0_, bf16[2368,1024]{1,0:T(8,128)(2,1)} %get-tuple-element.103.refs_1_, bf16[512,384]{1,0:T(8,128)(2,1)} %get-tuple-element.107.refs_2_, bf16[4616,512]{1,0:T(8,128)(2,1)} %unpack_rows.2.refs_3_, bf16[512,768]{1,0:T(8,128)(2,1)} %copy-done.7), custom_call_target="tpu_custom_call" | custom-call | flops 67289088 | bytes 179968 | tf_op jit(solution)/shard_map/attend_back/pallas_call | solution.py:58
  580.5 38.2 %all-reduce.6.cloned.1.call-done = (bf16[512,2048]{1,0:T(8,128)(2,1)}, bf16[512,512]{1,0:T(8,128)(2,1)}) async-done(((bf16[512,2048]{1,0:T(8,128)(2,1)}, bf16[512,512]{1,0:T(8,128)(2,1)}), (bf16[512,2048]{1,0:T(8,128)(2,1)}, bf16[512,512]{1,0:T(8,128)(2,1)})) %all-reduce.6.cloned.1.call-update) | async-done | bytes 2621456 | tf_op jit(solution)/shard_map/psum | solution.py:789
  653.2 18.6 %project_back.2 = (f32[1184,512]{1,0:T(8,128)}, bf16[1184,512]{1,0:T(8,128)(2,1)}, f32[1,1024]{1,0:T(1,128)}, f32[1,1024]{1,0:T(1,128)}, f32[1,1536]{1,0:T(1,128)}, /*index=5*/f32[1,768]{1,0:T(1,128)}, f32[1,768]{1,0:T(1,128)}) custom-call(f32[1,1024]{1,0:T(1,128)} %get-tuple-element.151.refs_0_, f32[2368,1024]{1,0:T(8,128)} %get-tuple-element.97.refs_4_.refs_1_, ...), custom_call_target="tpu_custom_call" | custom-call | flops 58195968 | bytes 305088 | tf_op jit(solution)/shard_map/project_back/pallas_call | solution.py:58
  675.6 18.7 %project_back.3 = (f32[1184,512]{1,0:T(8,128)}, bf16[1184,512]{1,0:T(8,128)(2,1)}, f32[1,1024]{1,0:T(1,128)}, f32[1,1024]{1,0:T(1,128)}, f32[1,1536]{1,0:T(1,128)}, /*index=5*/f32[1,768]{1,0:T(1,128)}, f32[1,768]{1,0:T(1,128)}) custom-call(f32[1,1024]{1,0:T(1,128)} %get-tuple-element.151.refs_0_, f32[2368,1024]{1,0:T(8,128)} %get-tuple-element.97.refs_4_.refs_1_, ...), custom_call_target="tpu_custom_call" | custom-call | flops 58195968 | bytes 305088 | tf_op jit(solution)/shard_map/project_back/pallas_call | solution.py:58
  701.6 10.2 %collective-permute-done.42 = bf16[256,768]{1,0:T(8,128)(2,1)S(1)} collective-permute-done((bf16[256,768]{1,0:T(8,128)(2,1)}, bf16[256,768]{1,0:T(8,128)(2,1)S(1)}, u32[]{:S(2)}, u32[]{:S(2)}) %collective-permute-start.42) | collective-permute-done | bytes 393248 | tf_op jit(solution)/shard_map/ppermute | solution.py:105
  (302 shorter events, 214.5 us)
Async XLA Ops:
  7.2 62.8 %all-gather.4.cloned.1.call-start = ((), (), s32[]{:S(2)}) async-start(), calls=%async_computation | async-start | bytes 1769472 | tf_op jit(solution)/shard_map/all_gather | solution.py:95
  24.2 103.0 %all-gather.6.cloned.1.call-start = ((), (), s32[]{:S(2)}) async-start(), calls=%async_computation.1 | async-start | bytes 2359296 | tf_op jit(solution)/shard_map/all_gather | solution.py:95
  24.2 54.9 %collective-permute-start.2 = (bf16[2368,512]{1,0:T(8,128)(2,1)}, bf16[2368,512]{1,0:T(8,128)(2,1)S(1)}, u32[]{:S(2)}, u32[]{:S(2)}) collective-permute-start(bf16[2368,512]{1,0:T(8,128)(2,1)} %get-tuple-element.76), channel_id=1, source_target_pairs={{0,2},{2,0},{1,3},{3,1},{4,6},{6,4},{5,7},{7,5},{8,10},{10,8},{9,1... | collective-permute-start | bytes 7274504 | tf_op jit(solution)/shard_map/ppermute | solution.py:73
  26.0 53.1 %collective-permute-start.3 = (bf16[512,1536]{1,0:T(8,128)(2,1)}, bf16[512,1536]{1,0:T(8,128)(2,1)}, u32[]{:S(2)}, u32[]{:S(2)}) collective-permute-start(bf16[512,1536]{1,0:T(8,128)(2,1)} %refs_7_.3), channel_id=1, source_target_pairs={{0,1},{1,0},{2,3},{3,2},{4,5},{5,4},{6,7},{7,6},{8,9},{9,8},{10,11... | collective-permute-start | bytes 4718600 | tf_op jit(solution)/shard_map/ppermute | solution.py:73
  70.0 110.0 %all-gather.8.cloned.1.call-start = ((), (), s32[]{:S(2)}) async-start(), calls=%async_computation.2 | async-start | bytes 2359296 | tf_op jit(solution)/shard_map/all_gather | solution.py:95
  125.9 357.5 %all-reduce.4.cloned.1.call-start = ((), (), s32[]{:S(2)}) async-start(), calls=%async_computation.3 | async-start | bytes 4194304 | tf_op jit(solution)/shard_map/psum | solution.py:786
  125.9 54.1 %collective-permute-start.12 = (bf16[2048,512]{1,0:T(8,128)(2,1)}, bf16[2048,512]{1,0:T(8,128)(2,1)}, u32[]{:S(2)}, u32[]{:S(2)}) collective-permute-start(bf16[2048,512]{1,0:T(8,128)(2,1)} %refs_4_.1), channel_id=1, source_target_pairs={{0,1},{1,0},{2,3},{3,2},{4,5},{5,4},{6,7},{7,6},{8,9},{9,8},{10,11... | collective-permute-start | bytes 6291464 | tf_op jit(solution)/shard_map/ppermute | solution.py:73
  126.0 54.0 %collective-permute-start.10 = (bf16[512,2048]{1,0:T(8,128)(2,1)}, bf16[512,2048]{1,0:T(8,128)(2,1)}, u32[]{:S(2)}, u32[]{:S(2)}) collective-permute-start(bf16[512,2048]{1,0:T(8,128)(2,1)} %refs_5_.3), channel_id=1, source_target_pairs={{0,1},{1,0},{2,3},{3,2},{4,5},{5,4},{6,7},{7,6},{8,9},{9,8},{10,11... | collective-permute-start | bytes 6291464 | tf_op jit(solution)/shard_map/ppermute | solution.py:73
  126.5 36.4 %collective-permute-start.7 = (bf16[512,512]{1,0:T(8,128)(2,1)S(1)}, bf16[512,512]{1,0:T(8,128)(2,1)}, u32[]{:S(2)}, u32[]{:S(2)}) collective-permute-start(bf16[512,512]{1,0:T(8,128)(2,1)S(1)} %copy-done.23), channel_id=1, source_target_pairs={{0,2},{2,0},{1,3},{3,1},{4,6},{6,4},{5,7},{7,5},{8,10},{10,8},{9,1... | collective-permute-start | bytes 1572872 | tf_op jit(solution)/shard_map/ppermute | solution.py:73
  127.2 52.9 %collective-permute-start.11 = (bf16[512,2048]{1,0:T(8,128)(2,1)}, bf16[512,2048]{1,0:T(8,128)(2,1)}, u32[]{:S(2)}, u32[]{:S(2)}) collective-permute-start(bf16[512,2048]{1,0:T(8,128)(2,1)} %all-gather.6.cloned.1.call-done.refs_4_.refs_7_), channel_id=1, source_target_pairs={{0,1},{1,0},{2,3},{3,2},{4,5},{5,4},{6,7},{7,6},{8,9},{9,8},{10,11... | collective-permute-start | bytes 6291464 | tf_op jit(solution)/shard_map/ppermute | solution.py:73
  165.1 55.1 %collective-permute-start.14 = (bf16[2368,512]{1,0:T(8,128)(2,1)}, bf16[2368,512]{1,0:T(8,128)(2,1)S(1)}, u32[]{:S(2)}, u32[]{:S(2)}) collective-permute-start(bf16[2368,512]{1,0:T(8,128)(2,1)} %get-tuple-element.92), channel_id=1, source_target_pairs={{0,2},{2,0},{1,3},{3,1},{4,6},{6,4},{5,7},{7,5},{8,10},{10,8},{9,1... | collective-permute-start | bytes 7274504 | tf_op jit(solution)/shard_map/ppermute | solution.py:73
  238.5 41.0 %collective-permute-start.15 = (bf16[2048,1024]{1,0:T(8,128)(2,1)}, bf16[2048,1024]{1,0:T(8,128)(2,1)}, u32[]{:S(2)}, u32[]{:S(2)}) collective-permute-start(bf16[2048,1024]{1,0:T(8,128)(2,1)} %reduce_outer.2.refs_7_.refs_4_), channel_id=1, source_target_pairs={{0,1},{1,0},{2,3},{3,2},{4,5},{5,4},{6,7},{7,6},{8,9},{9,8},{10,11... | collective-permute-start | bytes 12582920 | tf_op jit(solution)/shard_map/ppermute | solution.py:73
  312.7 52.6 %collective-permute-start.16 = (bf16[1024,2048]{1,0:T(8,128)(2,1)}, bf16[1024,2048]{1,0:T(8,128)(2,1)}, u32[]{:S(2)}, u32[]{:S(2)}) collective-permute-start(bf16[1024,2048]{1,0:T(8,128)(2,1)} %expand_outer.2.refs_13_.refs_3_), channel_id=1, source_target_pairs={{0,1},{1,0},{2,3},{3,2},{4,5},{5,4},{6,7},{7,6},{8,9},{9,8},{10,11... | collective-permute-start | bytes 12582920 | tf_op jit(solution)/shard_map/ppermute | solution.py:73
  313.1 47.9 %collective-permute-start.17 = (bf16[2048,512]{1,0:T(8,128)(2,1)}, bf16[2048,512]{1,0:T(8,128)(2,1)S(1)}, u32[]{:S(2)}, u32[]{:S(2)}) collective-permute-start(bf16[2048,512]{1,0:T(8,128)(2,1)} %get-tuple-element.98), channel_id=1, source_target_pairs={{0,2},{2,0},{1,3},{3,1},{4,6},{6,4},{5,7},{7,5},{8,10},{10,8},{9,1... | collective-permute-start | bytes 6291464 | tf_op jit(solution)/shard_map/ppermute | solution.py:73
  365.2 253.5 %all-reduce.6.cloned.1.call-start = ((), (), s32[]{:S(2)}) async-start(), calls=%async_computation.4 | async-start | bytes 5242880 | tf_op jit(solution)/shard_map/psum | solution.py:789
  382.6 111.0 %collective-permute-start.24 = (bf16[512,2048]{1,0:T(8,128)(2,1)}, bf16[512,2048]{1,0:T(8,128)(2,1)}, u32[]{:S(2)}, u32[]{:S(2)}) collective-permute-start(bf16[512,2048]{1,0:T(8,128)(2,1)} %get-tuple-element.109), channel_id=1, source_target_pairs={{0,2},{2,0},{1,3},{3,1},{4,6},{6,4},{5,7},{7,5},{8,10},{10,8},{9,1... | collective-permute-start | bytes 6291464 | tf_op jit(solution)/shard_map/ppermute | solution.py:73
  402.1 55.1 %collective-permute-start.20 = (bf16[512,512]{1,0:T(8,128)(2,1)}, bf16[512,512]{1,0:T(8,128)(2,1)S(1)}, u32[]{:S(2)}, u32[]{:S(2)}) collective-permute-start(bf16[512,512]{1,0:T(8,128)(2,1)} %get-tuple-element.104), channel_id=1, source_target_pairs={{0,2},{2,0},{1,3},{3,1},{4,6},{6,4},{5,7},{7,5},{8,10},{10,8},{9,1... | collective-permute-start | bytes 1572872 | tf_op jit(solution)/shard_map/ppermute | solution.py:73
  430.5 110.8 %collective-permute-start.19 = (bf16[2368,512]{1,0:T(8,128)(2,1)}, bf16[2368,512]{1,0:T(8,128)(2,1)}, u32[]{:S(2)}, u32[]{:S(2)}) collective-permute-start(bf16[2368,512]{1,0:T(8,128)(2,1)} %get-tuple-element.102), channel_id=1, source_target_pairs={{0,2},{2,0},{1,3},{3,1},{4,6},{6,4},{5,7},{7,5},{8,10},{10,8},{9,1... | collective-permute-start | bytes 7274504 | tf_op jit(solution)/shard_map/ppermute | solution.py:73
  506.6 32.9 %collective-permute-start.23 = (bf16[512,768]{1,0:T(8,128)(2,1)}, bf16[512,768]{1,0:T(8,128)(2,1)S(1)}, u32[]{:S(2)}, u32[]{:S(2)}) collective-permute-start(bf16[512,768]{1,0:T(8,128)(2,1)} %get-tuple-element.108), channel_id=1, source_target_pairs={{0,2},{2,0},{1,3},{3,1},{4,6},{6,4},{5,7},{7,5},{8,10},{10,8},{9,1... | collective-permute-start | bytes 2359304 | tf_op jit(solution)/shard_map/ppermute | solution.py:73
  539.8 39.9 %collective-permute-start.25 = (bf16[256,768]{1,0:T(8,128)(2,1)S(1)}, bf16[256,768]{1,0:T(8,128)(2,1)S(1)}, u32[]{:S(2)}, u32[]{:S(2)}) collective-permute-start(bf16[256,768]{1,0:T(8,128)(2,1)S(1)} %constant_dynamic-slice_fusion.4), channel_id=1, source_target_pairs={{0,4},{4,0},{8,12},{12,8},{16,20},{20,16},{24,28},{28,24},{1,5},{5... | collective-permute-start | bytes 1179656 | tf_op jit(solution)/shard_map/ppermute | solution.py:105
  643.4 31.4 %collective-permute-start.29 = (bf16[512,384]{1,0:T(8,128)(2,1)}, bf16[512,384]{1,0:T(8,128)(2,1)S(1)}, u32[]{:S(2)}, u32[]{:S(2)}) collective-permute-start(bf16[512,384]{1,0:T(8,128)(2,1)} %get-tuple-element.113), channel_id=1, source_target_pairs={{0,2},{2,0},{1,3},{3,1},{4,6},{6,4},{5,7},{7,5},{8,10},{10,8},{9,1... | collective-permute-start | bytes 1179656 | tf_op jit(solution)/shard_map/ppermute | solution.py:73
  653.2 67.0 %collective-permute-start.39 = (bf16[128,768]{1,0:T(8,128)(2,1)}, bf16[128,768]{1,0:T(8,128)(2,1)S(1)}, u32[]{:S(2)}, u32[]{:S(2)}) collective-permute-start(bf16[128,768]{1,0:T(8,128)(2,1)} %maximum_select_fusion.4.refs_13_), channel_id=1, source_target_pairs={{0,8},{4,12},{8,0},{12,4},{16,24},{20,28},{24,16},{28,20},{1,9},{5... | collective-permute-start | bytes 589832 | tf_op jit(solution)/shard_map/ppermute | solution.py:105
  674.1 53.7 %collective-permute-start.31 = (bf16[1184,512]{1,0:T(8,128)(2,1)}, bf16[1184,512]{1,0:T(8,128)(2,1)}, u32[]{:S(2)}, u32[]{:S(2)}) collective-permute-start(bf16[1184,512]{1,0:T(8,128)(2,1)} %get-tuple-element.115), channel_id=1, source_target_pairs={{0,2},{2,0},{1,3},{3,1},{4,6},{6,4},{5,7},{7,5},{8,10},{10,8},{9,1... | collective-permute-start | bytes 3637256 | tf_op jit(solution)/shard_map/ppermute | solution.py:73
  695.8 29.1 %collective-permute-start.33 = (f32[6144]{0:T(1024)S(1)}, f32[6144]{0:T(1024)S(1)}, u32[]{:S(2)}, u32[]{:S(2)}) collective-permute-start(f32[6144]{0:T(1024)S(1)} %reshape.83), channel_id=1, source_target_pairs={{0,1},{1,0},{2,3},{3,2},{4,5},{5,4},{6,7},{7,6},{8,9},{9,8},{10,11... | collective-permute-start | bytes 73736 | tf_op jit(solution)/shard_map/ppermute | solution.py:105
  (73 other events, 1079.3 us)
Sparse Core Ops, SparseCore 0:
  24.3 45.6 all-gather.3
  72.7 48.2 all-gather.5
  126.0 49.6 all-gather.7
  365.4 102.9 all-reduce.3
  497.5 121.1 all-reduce.5

commit v4 on v3

--- a/solution.py
+++ b/solution.py
@@ -771,38 +771,42 @@
     )
     output_others = outer_others(mixed, middle_lows, True, "output_outer", expand_held[:1])
     output_held = outer_own(mixed, middle_lows, True, "output_outer", output_others)
-    results = call(
-        partial(reduce_kernel, shape),
-        "reduce",
-        step,
-        [scalars, full(reduce_bias), image(hidden), image(middle)] + flat(reduce_blocks),
-        [out(width, BF)] * rows,
-        tokens * D * hidden_width,
-        output_held[:1],
-        weight=LIGHT,
-    )
-    block_output = unpack_rows([[part] for part in sent(results)], row_index, BF)
 
     reduce_weight_grad = lax.psum(reduce_share, "dp")
-    expand_share, _ = share_of(expand_held, reduce_weight_grad)
+    expand_share, expand_received = share_of(expand_held)
     output_share, output_received = share_of(output_held)
-    expand_weight_grad, output_weight_grad = lax.psum((expand_share, output_share), "dp")
+    expand_weight_grad, output_weight_grad = lax.psum(
+        hold((expand_share, output_share), reduce_weight_grad), "dp"
+    )
     pairs = 3 * D // (6 * HD) // cols
     counts = [pairs - 2, 1, 1] if pairs > 2 else [pairs]
     packed_lows, held, shares, halved, arrived, pair = [], [], [], [], (), 0
-    ready = results[:1]
+    ready = output_held[:1]
     for g, count in enumerate(counts):
         packed_low = None
         for slot in range(count):
             packed_low = attend_back(
                 packed, mixed_low, cols, pair, slot, count, packed_low, ready
             )
-            ready = output_received if pair == 0 else ()
+            ready = []
+            if pair == 0:
+                results = call(
+                    partial(reduce_kernel, shape),
+                    "reduce",
+                    step,
+                    [scalars, full(reduce_bias), image(hidden), image(middle)] + flat(reduce_blocks),
+                    [out(width, BF)] * rows,
+                    tokens * D * hidden_width,
+                    (packed_low,),
+                    weight=LIGHT,
+                )
+                block_output = unpack_rows([[part] for part in sent(results)], row_index, BF)
+                ready = [results[0], *expand_received, *output_received]
             pair += 1
         packed_lows.append(packed_low)
         last, own_last = (reduce_weight_grad,) if g == 0 else (), ()
         if g == 2:
-            last, own_last = (expand_weight_grad, halved[1]), (halved[2],)
+            last, own_last = (halved[1],), (halved[2],)
         others = outer_others(first_normed, [packed_low], False, "project_outer", last)
         held.append(outer_own(first_normed, [packed_low], False, "project_outer", others, own_last))
         ready = (held[g][0],)
@@ -811,11 +815,12 @@
             halved.append(shares[0])
             for hop in steps_of("dp"):
                 halved.append(halve(halved[-1], "dp", hop))
+            ready += (block_output,)
         elif g == 1:
             shares.append(share_of(held[1])[0])
-            ready += (block_output, shares[0])
+            ready += (shares[0],)
         else:
-            ready += (halved[3],)
+            ready += (halved[3], expand_weight_grad)
     joined = halved[-1:]
     for hop in reversed(steps_of("dp")):
         joined.append(join(joined[-1], "dp", hop))

time: 778 us -> 770 us (0.990)
  waiting for transfers between devices: 151 us -> 139 us
    psum x1, waiting for transfers between devices: 38.2 us -> 10.4 us  [body(): lax.psum(hold((expand_share, output_share), reduce_weight_grad), 'dp')]
    ppermute x17, waiting for transfers between devices: 30.7 us -> 40.9 us  [swap(): lax.ppermute(values, axis, [(i, i ^ step) for i in range(lax.axis_size(ax...]
  transfers between devices with their start and end apart: 54 -> 54, of which waited for: 18 -> 23; matrix products, arithmetic and copies ran while one was open for 5% -> 5% of each run, Pallas kernels for 58% -> 57%
where the time goes in v4:
time: 770 us; the launch traced here: 761 us
  Pallas kernels  505 us (66%)
  waiting for transfers between devices  139 us (18%)
  starting transfers between devices  47.8 us (6%)
  other arithmetic  31.1 us (4%)
  local copies, waits for them, and re-layouts  23.3 us (3%)
  between operations  15 us (2%)
    pallas_call x26, Pallas kernels, call(): pl.pallas_call(body_of, grid=grid, in_specs=[s for s, _ in operands] + [p...  479 us
    all_gather x3, waiting for transfers between devices, gather_shares(): blocks = [lax.all_gather(s, 'dp', axis=0, tiled=True) for s in shares]  44 us
    ppermute x32, waiting for transfers between devices, shift(): lax.ppermute(values, axis, [(i, (i + step) % size) for i in range(size)])  41.9 us
    ppermute x17, waiting for transfers between devices, swap(): lax.ppermute(values, axis, [(i, i ^ step) for i in range(lax.axis_size(ax...  40.9 us
    ppermute x32, starting transfers between devices, shift(): lax.ppermute(values, axis, [(i, (i + step) % size) for i in range(size)])  23.9 us
    ppermute x17, starting transfers between devices, swap(): lax.ppermute(values, axis, [(i, i ^ step) for i in range(lax.axis_size(ax...  23.7 us
  transfers between devices with their start and end apart: 54, of which 23 were waited for; matrix products, arithmetic and copies ran while one was open for 5% of the time, Pallas kernels for 57%

profile of v4, /device:TPU:0, one launch (start us, length us, event | category | flops | bytes accessed | tf_op | source)
XLA Modules:
  0.0 761.1 jit_solution(8976893848907864900)
XLA Ops:
  26.0 44.0 %all-gather.4.cloned.1.call-done.refs_7_.refs_9_ = bf16[512,1536]{1,0:T(8,128)(2,1)} async-done(((bf16[64,1536]{1,0:T(8,128)(2,1)}), bf16[512,1536]{1,0:T(8,128)(2,1)}) %all-gather.4.cloned.1.call-update) | async-done | bytes 1572880 | tf_op jit(solution)/shard_map/all_gather | solution.py:95
  80.5 22.0 %project.1 = (bf16[2368,1024]{1,0:T(8,128)(2,1)}, bf16[2368,3072]{1,0:T(8,128)(2,1)}) custom-call(f32[1,1024]{1,0:T(1,128)} %get-tuple-element.153.refs_0_, f32[1,1024]{1,0:T(1,128)} %get-tuple-element.152.refs_1_, f32[1,3072]{1,0:T(1,128)} %reshape.82.refs_2_, bf16[2368,512]{1,0:T(8,128)(2,1)} %get-tuple-element.76.refs_3_.refs_4_.refs_5_, ...), custom_call_target="tpu_custom_call" | custom-call | flops 14898167808 | bytes 30560256 | tf_op jit(solution)/shard_map/project/pallas_call | solution.py:58
  112.8 13.1 %attend.2.refs_1_ = bf16[2368,1024]{1,0:T(8,128)(2,1)} custom-call(bf16[2368,3072]{1,0:T(8,128)(2,1)} %get-tuple-element.79.refs_0_, bf16[64,2048]{1,0:T(8,128)(2,1)} %slice.87.refs_1_, bf16[256,512]{1,0:T(8,128)(2,1)} %copy-done.20, bf16[2368,512]{1,0:T(8,128)(2,1)} %get-tuple-element.82.refs_3_.refs_1_), custom_call_target="tpu_custom_call" | custom-call | flops 3588751360 | bytes 19398656 | tf_op jit(solution)/shard_map/attend/pallas_call | solution.py:58
  127.2 35.7 %attend.3.refs_3_.refs_0_ = bf16[2368,1024]{1,0:T(8,128)(2,1)} custom-call(bf16[2368,3072]{1,0:T(8,128)(2,1)} %get-tuple-element.79.refs_0_, bf16[2368,1024]{1,0:T(8,128)(2,1)} %attend.2.refs_1_, bf16[256,512]{1,0:T(8,128)(2,1)} %copy-done.20), custom_call_target="tpu_custom_call", output_to_operand_aliasing={{}: (1, {})} | custom-call | flops 10766254080 | bytes 19398656 | tf_op jit(solution)/shard_map/attend/pallas_call | solution.py:58
  167.1 12.9 %output.1 = (f32[2368,1024]{1,0:T(8,128)}, bf16[2368,1024]{1,0:T(8,128)(2,1)}) custom-call(f32[1,1024]{1,0:T(1,128)} %get-tuple-element.156.refs_0_, f32[1,1024]{1,0:T(1,128)} %get-tuple-element.155.refs_1_.refs_0_, f32[1,1024]{1,0:T(1,128)} %get-tuple-element.154.refs_2_, bf16[2368,1024]{1,0:T(8,128)(2,1)} %attend.3.refs_3_.refs_0_, ...), custom_call_target="tpu_custom_call" | custom-call | flops 4966055936 | bytes 26357760 | tf_op jit(solution)/shard_map/output/pallas_call | solution.py:58
  180.0 35.7 %expand.1 = (bf16[2368,4096]{1,0:T(8,128)(2,1)}, bf16[2368,4096]{1,0:T(8,128)(2,1)}) custom-call(f32[1,4096]{1,0:T(1,128)} %bitcast.15, bf16[2368,1024]{1,0:T(8,128)(2,1)} %get-tuple-element.87.refs_1_.refs_0_, bf16[512,2048]{1,0:T(8,128)(2,1)} %refs_5_.3, bf16[512,2048]{1,0:T(8,128)(2,1)} %collective-permute-done.10.refs_3_.refs_6_, ...), custom_call_target="tpu_custom_call" | custom-call | flops 19864223744 | bytes 52051968 | tf_op jit(solution)/shard_map/expand/pallas_call | solution.py:58
  221.6 16.8 %reduce_outer.2.refs_7_.refs_4_ = bf16[2048,1024]{1,0:T(8,128)(2,1)} custom-call(bf16[2368,4096]{1,0:T(8,128)(2,1)} %get-tuple-element.90.refs_0_.refs_2_, bf16[2368,512]{1,0:T(8,128)(2,1)} %get-tuple-element.82.refs_3_.refs_1_, bf16[2368,512]{1,0:T(8,128)(2,1)} %copy-done, bf16[2048,512]{1,0:T(8,128)(2,1)} %all-gather.8.cloned.1.call-done.refs_7_.refs_3_.refs_5_.refs_6_), custom_call_target="tpu_custom_call" | custom-call | flops 9932111872 | bytes 28442624 | tf_op jit(solution)/shard_map/reduce_outer/pallas_call | solution.py:58
  239.0 9.5 %collective-permute-done.13.refs_6_.refs_7_ = bf16[2048,512]{1,0:T(8,128)(2,1)S(1)} collective-permute-done((bf16[2048,512]{1,0:T(8,128)(2,1)}, bf16[2048,512]{1,0:T(8,128)(2,1)S(1)}, u32[]{:S(2)}, u32[]{:S(2)}) %collective-permute-start.13) | collective-permute-done | bytes 2097184 | tf_op jit(solution)/shard_map/ppermute | solution.py:73
  249.8 29.6 %reduce_back.1 = (bf16[2368,4096]{1,0:T(8,128)(2,1)}, f32[1,1024]{1,0:T(1,128)}, f32[1,4096]{1,0:T(1,128)}) custom-call(bf16[2368,4096]{1,0:T(8,128)(2,1)} %get-tuple-element.92.refs_0_, bf16[2368,512]{1,0:T(8,128)(2,1)} %get-tuple-element.82.refs_3_.refs_1_, bf16[2368,512]{1,0:T(8,128)(2,1)} %copy-done, bf16[2048,512]{1,0:T(8,128)(2,1)} %refs_4_.1, ...), custom_call_target="tpu_custom_call" | custom-call | flops 155189248 | bytes 406688 | tf_op jit(solution)/shard_map/reduce_back/pallas_call | solution.py:58
  279.4 16.7 %reduce_outer.3 = (bf16[2048,512]{1,0:T(8,128)(2,1)}, bf16[2048,512]{1,0:T(8,128)(2,1)}) custom-call(bf16[2368,4096]{1,0:T(8,128)(2,1)} %get-tuple-element.90.refs_0_.refs_2_, bf16[2368,512]{1,0:T(8,128)(2,1)} %get-tuple-element.82.refs_3_.refs_1_, bf16[2368,512]{1,0:T(8,128)(2,1)} %copy-done, bf16[2048,1024]{1,0:T(8,128)(2,1)} %collective-permute-done.15.refs_3_, ...), custom_call_target="tpu_custom_call" | custom-call | flops 9932111872 | bytes 32636928 | tf_op jit(solution)/shard_map/reduce_outer/pallas_call | solution.py:58
  296.1 16.6 %expand_outer.2.refs_13_.refs_3_ = bf16[1024,2048]{1,0:T(8,128)(2,1)} custom-call(bf16[2368,1024]{1,0:T(8,128)(2,1)} %get-tuple-element.87.refs_1_.refs_0_, bf16[2368,4096]{1,0:T(8,128)(2,1)} %get-tuple-element.94.refs_5_.refs_1_, bf16[2048,512]{1,0:T(8,128)(2,1)} %get-tuple-element.95.refs_2_), custom_call_target="tpu_custom_call" | custom-call | flops 9932111872 | bytes 28442624 | tf_op jit(solution)/shard_map/expand_outer/pallas_call | solution.py:58
  314.5 37.5 %expand_back.1 = (f32[2368,1024]{1,0:T(8,128)}, bf16[2368,1024]{1,0:T(8,128)(2,1)}, f32[1,1024]{1,0:T(1,128)}, f32[1,1024]{1,0:T(1,128)}, f32[1,1024]{1,0:T(1,12...) custom-call(f32[1,1024]{1,0:T(1,128)} %get-tuple-element.155.refs_1_.refs_0_, ...), custom_call_target="tpu_custom_call" | custom-call | flops 193986560 | bytes 498816 | tf_op jit(solution)/shard_map/expand_back/pallas_call | solution.py:58
  362.3 17.1 %expand_outer.3 = (bf16[512,2048]{1,0:T(8,128)(2,1)}, bf16[512,2048]{1,0:T(8,128)(2,1)}) custom-call(bf16[2368,1024]{1,0:T(8,128)(2,1)} %get-tuple-element.87.refs_1_.refs_0_, bf16[2368,4096]{1,0:T(8,128)(2,1)} %get-tuple-element.94.refs_5_.refs_1_, bf16[1024,2048]{1,0:T(8,128)(2,1)} %collective-permute-done.16.refs_2_, ...), custom_call_target="tpu_custom_call" | custom-call | flops 9932111872 | bytes 32636928 | tf_op jit(solution)/shard_map/expand_outer/pallas_call | solution.py:58
  404.3 25.2 %attend_back.4.refs_8_.refs_2_ = bf16[2368,1536]{1,0:T(8,128)(2,1)} custom-call(bf16[2368,3072]{1,0:T(8,128)(2,1)} %get-tuple-element.79.refs_0_, bf16[2368,1024]{1,0:T(8,128)(2,1)} %get-tuple-element.96.refs_1_, bf16[512,512]{1,0:T(8,128)(2,1)} %get-tuple-element.102.refs_2_), custom_call_target="tpu_custom_call" | custom-call | flops 67289088 | bytes 208384 | tf_op jit(solution)/shard_map/attend_back/pallas_call | solution.py:58
  429.5 27.3 %reduce.11 = (bf16[2368,512]{1,0:T(8,128)(2,1)}, bf16[2368,512]{1,0:T(8,128)(2,1)}) custom-call(s32[4]{0:T(128)} %dynamic_slice.51.refs_0_, f32[1,1024]{1,0:T(1,128)} %get-tuple-element.157.refs_1_, bf16[2368,4096]{1,0:T(8,128)(2,1)} %get-tuple-element.90.refs_0_.refs_2_, f32[2368,1024]{1,0:T(8,128)} %get-tuple-element.91.refs_2_.refs_3_, ...), custom_call_target="tpu_custom_call" | custom-call | flops 155189248 | bytes 330784 | tf_op jit(solution)/shard_map/reduce/pallas_call | solution.py:58
  459.7 25.5 %attend_back.5.refs_1_.refs_2_ = bf16[2368,1536]{1,0:T(8,128)(2,1)} custom-call(bf16[2368,3072]{1,0:T(8,128)(2,1)} %get-tuple-element.79.refs_0_, bf16[2368,1024]{1,0:T(8,128)(2,1)} %get-tuple-element.96.refs_1_, bf16[2368,1536]{1,0:T(8,128)(2,1)} %attend_back.4.refs_8_.refs_2_, ...), custom_call_target="tpu_custom_call", output_to_operand_aliasing={{}: (2, {})} | custom-call | flops 67289088 | bytes 208384 | tf_op jit(solution)/shard_map/attend_back/pallas_call | solution.py:58
  501.1 9.3 %project_outer.7 = (bf16[512,768]{1,0:T(8,128)(2,1)}, bf16[512,768]{1,0:T(8,128)(2,1)}) custom-call(bf16[2368,1024]{1,0:T(8,128)(2,1)} %get-tuple-element.107.refs_0_, bf16[2368,1536]{1,0:T(8,128)(2,1)} %attend_back.5.refs_1_.refs_2_, bf16[1024,768]{1,0:T(8,128)(2,1)} %copy-done.18, bf16[1024,768]{1,0:T(8,128)(2,1)} %project_outer.6.refs_3_), custom_call_target="tpu_custom_call" | custom-call | flops 29097984 | bytes 119296 | tf_op jit(solution)/shard_map/project_outer/pallas_call | solution.py:58
  521.2 25.2 %attend_back.6.refs_1_.refs_3_ = bf16[2368,768]{1,0:T(8,128)(2,1)} custom-call(bf16[2368,3072]{1,0:T(8,128)(2,1)} %get-tuple-element.79.refs_0_, bf16[2368,1024]{1,0:T(8,128)(2,1)} %get-tuple-element.96.refs_1_, bf16[512,768]{1,0:T(8,128)(2,1)} %get-tuple-element.108.refs_2_, bf16[4616,512]{1,0:T(8,128)(2,1)} %unpack_rows.2.refs_3_), custom_call_target="tpu_custom_call" | custom-call | flops 67289088 | bytes 179968 | tf_op jit(solution)/shard_map/attend_back/pallas_call | solution.py:58
  563.4 25.3 %attend_back.7.refs_1_.refs_4_ = bf16[2368,768]{1,0:T(8,128)(2,1)} custom-call(bf16[2368,3072]{1,0:T(8,128)(2,1)} %get-tuple-element.79.refs_0_, bf16[2368,1024]{1,0:T(8,128)(2,1)} %get-tuple-element.96.refs_1_, bf16[512,384]{1,0:T(8,128)(2,1)} %get-tuple-element.109.refs_2_, bf16[512,768]{1,0:T(8,128)(2,1)} %copy-done.8), custom_call_target="tpu_custom_call" | custom-call | flops 67289088 | bytes 179968 | tf_op jit(solution)/shard_map/attend_back/pallas_call | solution.py:58
  619.2 13.2 %collective-permute-done.30 = bf16[64,768]{1,0:T(8,128)(2,1)S(1)} collective-permute-done((bf16[64,768]{1,0:T(8,128)(2,1)S(1)}, bf16[64,768]{1,0:T(8,128)(2,1)S(1)}, u32[]{:S(2)}, u32[]{:S(2)}) %collective-permute-start.30) | collective-permute-done | bytes 98336 | tf_op jit(solution)/shard_map/ppermute | solution.py:105
  633.1 10.4 %all-reduce.6.cloned.1.call-done = (bf16[512,2048]{1,0:T(8,128)(2,1)}, bf16[512,512]{1,0:T(8,128)(2,1)}) async-done(((bf16[512,2048]{1,0:T(8,128)(2,1)}, bf16[512,512]{1,0:T(8,128)(2,1)}), (bf16[512,2048]{1,0:T(8,128)(2,1)}, bf16[512,512]{1,0:T(8,128)(2,1)})) %all-reduce.6.cloned.1.call-update) | async-done | bytes 2621456 | tf_op jit(solution)/shard_map/psum | solution.py:778
  643.6 18.4 %project_back.2 = (f32[1184,512]{1,0:T(8,128)}, bf16[1184,512]{1,0:T(8,128)(2,1)}, f32[1,1024]{1,0:T(1,128)}, f32[1,1024]{1,0:T(1,128)}, f32[1,1536]{1,0:T(1,128)}, /*index=5*/f32[1,768]{1,0:T(1,128)}, f32[1,768]{1,0:T(1,128)}) custom-call(f32[1,1024]{1,0:T(1,128)} %get-tuple-element.153.refs_0_, f32[2368,1024]{1,0:T(8,128)} %get-tuple-element.99.refs_4_.refs_1_, ...), custom_call_target="tpu_custom_call" | custom-call | flops 58195968 | bytes 305088 | tf_op jit(solution)/shard_map/project_back/pallas_call | solution.py:58
  666.6 18.6 %project_back.3 = (f32[1184,512]{1,0:T(8,128)}, bf16[1184,512]{1,0:T(8,128)(2,1)}, f32[1,1024]{1,0:T(1,128)}, f32[1,1024]{1,0:T(1,128)}, f32[1,1536]{1,0:T(1,128)}, /*index=5*/f32[1,768]{1,0:T(1,128)}, f32[1,768]{1,0:T(1,128)}) custom-call(f32[1,1024]{1,0:T(1,128)} %get-tuple-element.153.refs_0_, f32[2368,1024]{1,0:T(8,128)} %get-tuple-element.99.refs_4_.refs_1_, ...), custom_call_target="tpu_custom_call" | custom-call | flops 58195968 | bytes 305088 | tf_op jit(solution)/shard_map/project_back/pallas_call | solution.py:58
  692.6 10.1 %collective-permute-done.42 = bf16[256,768]{1,0:T(8,128)(2,1)S(1)} collective-permute-done((bf16[256,768]{1,0:T(8,128)(2,1)}, bf16[256,768]{1,0:T(8,128)(2,1)S(1)}, u32[]{:S(2)}, u32[]{:S(2)}) %collective-permute-start.42) | collective-permute-done | bytes 393248 | tf_op jit(solution)/shard_map/ppermute | solution.py:105
  (306 shorter events, 230.4 us)
Async XLA Ops:
  7.2 62.8 %all-gather.4.cloned.1.call-start = ((), (), s32[]{:S(2)}) async-start(), calls=%async_computation | async-start | bytes 1769472 | tf_op jit(solution)/shard_map/all_gather | solution.py:95
  24.2 103.0 %all-gather.6.cloned.1.call-start = ((), (), s32[]{:S(2)}) async-start(), calls=%async_computation.1 | async-start | bytes 2359296 | tf_op jit(solution)/shard_map/all_gather | solution.py:95
  24.2 54.9 %collective-permute-start.2 = (bf16[2368,512]{1,0:T(8,128)(2,1)}, bf16[2368,512]{1,0:T(8,128)(2,1)S(1)}, u32[]{:S(2)}, u32[]{:S(2)}) collective-permute-start(bf16[2368,512]{1,0:T(8,128)(2,1)} %get-tuple-element.77), channel_id=1, source_target_pairs={{0,2},{2,0},{1,3},{3,1},{4,6},{6,4},{5,7},{7,5},{8,10},{10,8},{9,1... | collective-permute-start | bytes 7274504 | tf_op jit(solution)/shard_map/ppermute | solution.py:73
  26.0 53.1 %collective-permute-start.3 = (bf16[512,1536]{1,0:T(8,128)(2,1)}, bf16[512,1536]{1,0:T(8,128)(2,1)}, u32[]{:S(2)}, u32[]{:S(2)}) collective-permute-start(bf16[512,1536]{1,0:T(8,128)(2,1)} %refs_7_.3), channel_id=1, source_target_pairs={{0,1},{1,0},{2,3},{3,2},{4,5},{5,4},{6,7},{7,6},{8,9},{9,8},{10,11... | collective-permute-start | bytes 4718600 | tf_op jit(solution)/shard_map/ppermute | solution.py:73
  70.0 110.0 %all-gather.8.cloned.1.call-start = ((), (), s32[]{:S(2)}) async-start(), calls=%async_computation.2 | async-start | bytes 2359296 | tf_op jit(solution)/shard_map/all_gather | solution.py:95
  125.9 361.4 %all-reduce.4.cloned.1.call-start = ((), (), s32[]{:S(2)}) async-start(), calls=%async_computation.3 | async-start | bytes 4194304 | tf_op jit(solution)/shard_map/psum | solution.py:775
  125.9 54.1 %collective-permute-start.12 = (bf16[2048,512]{1,0:T(8,128)(2,1)}, bf16[2048,512]{1,0:T(8,128)(2,1)}, u32[]{:S(2)}, u32[]{:S(2)}) collective-permute-start(bf16[2048,512]{1,0:T(8,128)(2,1)} %refs_4_.1), channel_id=1, source_target_pairs={{0,1},{1,0},{2,3},{3,2},{4,5},{5,4},{6,7},{7,6},{8,9},{9,8},{10,11... | collective-permute-start | bytes 6291464 | tf_op jit(solution)/shard_map/ppermute | solution.py:73
  126.0 54.0 %collective-permute-start.10 = (bf16[512,2048]{1,0:T(8,128)(2,1)}, bf16[512,2048]{1,0:T(8,128)(2,1)}, u32[]{:S(2)}, u32[]{:S(2)}) collective-permute-start(bf16[512,2048]{1,0:T(8,128)(2,1)} %refs_5_.3), channel_id=1, source_target_pairs={{0,1},{1,0},{2,3},{3,2},{4,5},{5,4},{6,7},{7,6},{8,9},{9,8},{10,11... | collective-permute-start | bytes 6291464 | tf_op jit(solution)/shard_map/ppermute | solution.py:73
  126.5 36.4 %collective-permute-start.7 = (bf16[512,512]{1,0:T(8,128)(2,1)S(1)}, bf16[512,512]{1,0:T(8,128)(2,1)}, u32[]{:S(2)}, u32[]{:S(2)}) collective-permute-start(bf16[512,512]{1,0:T(8,128)(2,1)S(1)} %copy-done.25), channel_id=1, source_target_pairs={{0,2},{2,0},{1,3},{3,1},{4,6},{6,4},{5,7},{7,5},{8,10},{10,8},{9,1... | collective-permute-start | bytes 1572872 | tf_op jit(solution)/shard_map/ppermute | solution.py:73
  127.2 52.9 %collective-permute-start.11 = (bf16[512,2048]{1,0:T(8,128)(2,1)}, bf16[512,2048]{1,0:T(8,128)(2,1)}, u32[]{:S(2)}, u32[]{:S(2)}) collective-permute-start(bf16[512,2048]{1,0:T(8,128)(2,1)} %all-gather.6.cloned.1.call-done.refs_4_.refs_7_), channel_id=1, source_target_pairs={{0,1},{1,0},{2,3},{3,2},{4,5},{5,4},{6,7},{7,6},{8,9},{9,8},{10,11... | collective-permute-start | bytes 6291464 | tf_op jit(solution)/shard_map/ppermute | solution.py:73
  165.1 55.1 %collective-permute-start.14 = (bf16[2368,512]{1,0:T(8,128)(2,1)}, bf16[2368,512]{1,0:T(8,128)(2,1)S(1)}, u32[]{:S(2)}, u32[]{:S(2)}) collective-permute-start(bf16[2368,512]{1,0:T(8,128)(2,1)} %get-tuple-element.93), channel_id=1, source_target_pairs={{0,2},{2,0},{1,3},{3,1},{4,6},{6,4},{5,7},{7,5},{8,10},{10,8},{9,1... | collective-permute-start | bytes 7274504 | tf_op jit(solution)/shard_map/ppermute | solution.py:73
  238.5 41.0 %collective-permute-start.15 = (bf16[2048,1024]{1,0:T(8,128)(2,1)}, bf16[2048,1024]{1,0:T(8,128)(2,1)}, u32[]{:S(2)}, u32[]{:S(2)}) collective-permute-start(bf16[2048,1024]{1,0:T(8,128)(2,1)} %reduce_outer.2.refs_7_.refs_4_), channel_id=1, source_target_pairs={{0,1},{1,0},{2,3},{3,2},{4,5},{5,4},{6,7},{7,6},{8,9},{9,8},{10,11... | collective-permute-start | bytes 12582920 | tf_op jit(solution)/shard_map/ppermute | solution.py:73
  312.7 48.3 %collective-permute-start.16 = (bf16[1024,2048]{1,0:T(8,128)(2,1)}, bf16[1024,2048]{1,0:T(8,128)(2,1)}, u32[]{:S(2)}, u32[]{:S(2)}) collective-permute-start(bf16[1024,2048]{1,0:T(8,128)(2,1)} %expand_outer.2.refs_13_.refs_3_), channel_id=1, source_target_pairs={{0,1},{1,0},{2,3},{3,2},{4,5},{5,4},{6,7},{7,6},{8,9},{9,8},{10,11... | collective-permute-start | bytes 12582920 | tf_op jit(solution)/shard_map/ppermute | solution.py:73
  313.1 47.9 %collective-permute-start.17 = (bf16[2048,512]{1,0:T(8,128)(2,1)}, bf16[2048,512]{1,0:T(8,128)(2,1)S(1)}, u32[]{:S(2)}, u32[]{:S(2)}) collective-permute-start(bf16[2048,512]{1,0:T(8,128)(2,1)} %get-tuple-element.100), channel_id=1, source_target_pairs={{0,2},{2,0},{1,3},{3,1},{4,6},{6,4},{5,7},{7,5},{8,10},{10,8},{9,1... | collective-permute-start | bytes 6291464 | tf_op jit(solution)/shard_map/ppermute | solution.py:73
  379.4 78.7 %collective-permute-start.20 = (bf16[512,2048]{1,0:T(8,128)(2,1)}, bf16[512,2048]{1,0:T(8,128)(2,1)S(1)}, u32[]{:S(2)}, u32[]{:S(2)}) collective-permute-start(bf16[512,2048]{1,0:T(8,128)(2,1)} %get-tuple-element.105), channel_id=1, source_target_pairs={{0,2},{2,0},{1,3},{3,1},{4,6},{6,4},{5,7},{7,5},{8,10},{10,8},{9,1... | collective-permute-start | bytes 6291464 | tf_op jit(solution)/shard_map/ppermute | solution.py:73
  385.0 258.6 %all-reduce.6.cloned.1.call-start = ((), (), s32[]{:S(2)}) async-start(), calls=%async_computation.4 | async-start | bytes 5242880 | tf_op jit(solution)/shard_map/psum | solution.py:778
  403.0 55.2 %collective-permute-start.21 = (bf16[512,512]{1,0:T(8,128)(2,1)}, bf16[512,512]{1,0:T(8,128)(2,1)S(1)}, u32[]{:S(2)}, u32[]{:S(2)}) collective-permute-start(bf16[512,512]{1,0:T(8,128)(2,1)} %get-tuple-element.106), channel_id=1, source_target_pairs={{0,2},{2,0},{1,3},{3,1},{4,6},{6,4},{5,7},{7,5},{8,10},{10,8},{9,1... | collective-permute-start | bytes 1572872 | tf_op jit(solution)/shard_map/ppermute | solution.py:73
  456.8 58.9 %collective-permute-start.19 = (bf16[2368,512]{1,0:T(8,128)(2,1)}, bf16[2368,512]{1,0:T(8,128)(2,1)}, u32[]{:S(2)}, u32[]{:S(2)}) collective-permute-start(bf16[2368,512]{1,0:T(8,128)(2,1)} %get-tuple-element.104), channel_id=1, source_target_pairs={{0,2},{2,0},{1,3},{3,1},{4,6},{6,4},{5,7},{7,5},{8,10},{10,8},{9,1... | collective-permute-start | bytes 7274504 | tf_op jit(solution)/shard_map/ppermute | solution.py:73
  510.4 42.9 %collective-permute-start.24 = (bf16[512,768]{1,0:T(8,128)(2,1)}, bf16[512,768]{1,0:T(8,128)(2,1)S(1)}, u32[]{:S(2)}, u32[]{:S(2)}) collective-permute-start(bf16[512,768]{1,0:T(8,128)(2,1)} %get-tuple-element.110), channel_id=1, source_target_pairs={{0,2},{2,0},{1,3},{3,1},{4,6},{6,4},{5,7},{7,5},{8,10},{10,8},{9,1... | collective-permute-start | bytes 2359304 | tf_op jit(solution)/shard_map/ppermute | solution.py:73
  553.5 35.2 %collective-permute-start.25 = (bf16[256,768]{1,0:T(8,128)(2,1)S(1)}, bf16[256,768]{1,0:T(8,128)(2,1)S(1)}, u32[]{:S(2)}, u32[]{:S(2)}) collective-permute-start(bf16[256,768]{1,0:T(8,128)(2,1)S(1)} %constant_dynamic-slice_fusion.4), channel_id=1, source_target_pairs={{0,4},{4,0},{8,12},{12,8},{16,20},{20,16},{24,28},{28,24},{1,5},{5... | collective-permute-start | bytes 1179656 | tf_op jit(solution)/shard_map/ppermute | solution.py:105
  615.1 50.6 %collective-permute-start.29 = (bf16[512,384]{1,0:T(8,128)(2,1)}, bf16[512,384]{1,0:T(8,128)(2,1)S(1)}, u32[]{:S(2)}, u32[]{:S(2)}) collective-permute-start(bf16[512,384]{1,0:T(8,128)(2,1)} %get-tuple-element.114), channel_id=1, source_target_pairs={{0,2},{2,0},{1,3},{3,1},{4,6},{6,4},{5,7},{7,5},{8,10},{10,8},{9,1... | collective-permute-start | bytes 1179656 | tf_op jit(solution)/shard_map/ppermute | solution.py:73
  633.1 78.0 %collective-permute-start.39 = (bf16[128,768]{1,0:T(8,128)(2,1)}, bf16[128,768]{1,0:T(8,128)(2,1)S(1)}, u32[]{:S(2)}, u32[]{:S(2)}) collective-permute-start(bf16[128,768]{1,0:T(8,128)(2,1)} %maximum_select_fusion.4.refs_13_), channel_id=1, source_target_pairs={{0,8},{4,12},{8,0},{12,4},{16,24},{20,28},{24,16},{28,20},{1,9},{5... | collective-permute-start | bytes 589832 | tf_op jit(solution)/shard_map/ppermute | solution.py:105
  664.3 54.6 %collective-permute-start.31 = (bf16[1184,512]{1,0:T(8,128)(2,1)}, bf16[1184,512]{1,0:T(8,128)(2,1)}, u32[]{:S(2)}, u32[]{:S(2)}) collective-permute-start(bf16[1184,512]{1,0:T(8,128)(2,1)} %get-tuple-element.116), channel_id=1, source_target_pairs={{0,2},{2,0},{1,3},{3,1},{4,6},{6,4},{5,7},{7,5},{8,10},{10,8},{9,1... | collective-permute-start | bytes 3637256 | tf_op jit(solution)/shard_map/ppermute | solution.py:73
  686.7 29.3 %collective-permute-start.33 = (f32[6144]{0:T(1024)S(1)}, f32[6144]{0:T(1024)S(1)}, u32[]{:S(2)}, u32[]{:S(2)}) collective-permute-start(f32[6144]{0:T(1024)S(1)} %reshape.83), channel_id=1, source_target_pairs={{0,1},{1,0},{2,3},{3,2},{4,5},{5,4},{6,7},{7,6},{8,9},{9,8},{10,11... | collective-permute-start | bytes 73736 | tf_op jit(solution)/shard_map/ppermute | solution.py:105
  (75 other events, 1111.6 us)
Sparse Core Ops, SparseCore 0:
  24.3 45.6 all-gather.3
  72.7 48.2 all-gather.5
  126.0 49.7 all-gather.7
  385.1 102.1 all-reduce.3
  515.8 127.6 all-reduce.5

commit v5 on v4

--- a/solution.py
+++ b/solution.py
@@ -774,13 +774,11 @@
 
     reduce_weight_grad = lax.psum(reduce_share, "dp")
     expand_share, expand_received = share_of(expand_held)
-    output_share, output_received = share_of(output_held)
-    expand_weight_grad, output_weight_grad = lax.psum(
-        hold((expand_share, output_share), reduce_weight_grad), "dp"
-    )
+    output_share, _ = share_of(output_held)
+    expand_weight_grad = lax.psum(hold(expand_share, reduce_weight_grad), "dp")
     pairs = 3 * D // (6 * HD) // cols
     counts = [pairs - 2, 1, 1] if pairs > 2 else [pairs]
-    packed_lows, held, shares, halved, arrived, pair = [], [], [], [], (), 0
+    packed_lows, held, shares, arrived, pair = [], [], [], (), 0
     ready = output_held[:1]
     for g, count in enumerate(counts):
         packed_low = None
@@ -801,29 +799,20 @@
                     weight=LIGHT,
                 )
                 block_output = unpack_rows([[part] for part in sent(results)], row_index, BF)
-                ready = [results[0], *expand_received, *output_received]
+                ready = [results[0], *expand_received]
             pair += 1
         packed_lows.append(packed_low)
-        last, own_last = (reduce_weight_grad,) if g == 0 else (), ()
+        last = (reduce_weight_grad,) if g == 0 else (block_output,)
         if g == 2:
-            last, own_last = (halved[1],), (halved[2],)
+            last = (expand_weight_grad, output_share, *shares)
         others = outer_others(first_normed, [packed_low], False, "project_outer", last)
-        held.append(outer_own(first_normed, [packed_low], False, "project_outer", others, own_last))
+        held.append(outer_own(first_normed, [packed_low], False, "project_outer", others))
         ready = (held[g][0],)
-        if g == 0:
-            shares.append(share_of(held[0])[0])
-            halved.append(shares[0])
-            for hop in steps_of("dp"):
-                halved.append(halve(halved[-1], "dp", hop))
-            ready += (block_output,)
-        elif g == 1:
-            shares.append(share_of(held[1])[0])
-            ready += (shares[0],)
-        else:
-            ready += (halved[3], expand_weight_grad)
-    joined = halved[-1:]
-    for hop in reversed(steps_of("dp")):
-        joined.append(join(joined[-1], "dp", hop))
+        if g < 2:
+            shares.append(share_of(held[g])[0])
+    output_weight_grad, first_sum = lax.psum(
+        hold((output_share, shares[0]), expand_weight_grad), "dp"
+    )
 
     halves = 2 if images % 2 == 0 else 1
     some = images // halves
@@ -858,13 +847,13 @@
         if half == 0 and len(counts) > 1:
             share, arrived = share_of(held[-1], results[0])
             shares.append(share)
-        ready = (results[0], *arrived, joined[1])
+        ready = (results[0], *arrived)
         packed_sums = [v.reshape(cols, -1, 3, HD) for v in results[rows + 2 :]]
         late = (*results[rows : rows + 2], jnp.concatenate(packed_sums, 1))
         sums = late if half == 0 else jax.tree.map(jnp.add, sums, late)
     input_grad = unpack_rows(list(zip(*input_grads)), row_index, F32)
     first_gain_grad, first_shift_grad, packed_sums = sums
-    attend_weight_grad = joined[-1:]
+    attend_weight_grad = [first_sum]
     if len(shares) > 1:
         attend_weight_grad.append(sum_shares(jnp.concatenate(shares[1:], 1), "dp"))
     attend_weight_grad = jnp.concatenate(attend_weight_grad, 1)

time: 770 us -> 761 us (0.988)
  starting transfers between devices: 47.8 us -> 36.7 us
    ppermute x17 -> x11, waiting for transfers between devices: 40.9 us -> 22.9 us  [swap(): lax.ppermute(values, axis, [(i, i ^ step) for i in range(lax.axis_size(ax...]
    ppermute x32, waiting for transfers between devices: 41.9 us -> 54.4 us  [shift(): lax.ppermute(values, axis, [(i, (i + step) % size) for i in range(size)])]
    ppermute x17 -> x11, starting transfers between devices: 23.7 us -> 13.8 us  [swap(): lax.ppermute(values, axis, [(i, i ^ step) for i in range(lax.axis_size(ax...]
    psum x1 -> x2, waiting for transfers between devices: 10.4 us -> 20.3 us  [the longest x1 20 us: body(): lax.psum(hold((output_share, shares[0]), expand_weight_grad), 'dp')]
  transfers between devices with their start and end apart: 54 -> 49, of which waited for: 23 -> 22; matrix products, arithmetic and copies ran while one was open for 5% -> 4% of each run, Pallas kernels for 57% -> 56%
where the time goes in v5:
time: 761 us; the launch traced here: 752 us
  Pallas kernels  505 us (66%)
  waiting for transfers between devices  146 us (19%)
  starting transfers between devices  36.7 us (5%)
  other arithmetic  27.1 us (4%)
  local copies, waits for them, and re-layouts  22.3 us (3%)
  between operations  15.3 us (2%)
    pallas_call x26, Pallas kernels, call(): pl.pallas_call(body_of, grid=grid, in_specs=[s for s, _ in operands] + [p...  479 us
    ppermute x32, waiting for transfers between devices, shift(): lax.ppermute(values, axis, [(i, (i + step) % size) for i in range(size)])  54.4 us
    all_gather x3, waiting for transfers between devices, gather_shares(): blocks = [lax.all_gather(s, 'dp', axis=0, tiled=True) for s in shares]  44 us
    ppermute x11, waiting for transfers between devices, swap(): lax.ppermute(values, axis, [(i, i ^ step) for i in range(lax.axis_size(ax...  22.9 us
    ppermute x32, starting transfers between devices, shift(): lax.ppermute(values, axis, [(i, (i + step) % size) for i in range(size)])  22.7 us
    psum x1, waiting for transfers between devices, body(): lax.psum(hold((output_share, shares[0]), expand_weight_grad), 'dp')  20 us
  transfers between devices with their start and end apart: 49, of which 22 were waited for; matrix products, arithmetic and copies ran while one was open for 4% of the time, Pallas kernels for 56%

profile of v5, /device:TPU:0, one launch (start us, length us, event | category | flops | bytes accessed | tf_op | source)
XLA Modules:
  0.0 752.4 jit_solution(3932782304666161167)
XLA Ops:
  26.0 44.0 %all-gather.4.cloned.1.call-done.refs_7_.refs_9_ = bf16[512,1536]{1,0:T(8,128)(2,1)} async-done(((bf16[64,1536]{1,0:T(8,128)(2,1)}), bf16[512,1536]{1,0:T(8,128)(2,1)}) %all-gather.4.cloned.1.call-update) | async-done | bytes 1572880 | tf_op jit(solution)/shard_map/all_gather | solution.py:95
  80.5 22.1 %project.1 = (bf16[2368,1024]{1,0:T(8,128)(2,1)}, bf16[2368,3072]{1,0:T(8,128)(2,1)}) custom-call(f32[1,1024]{1,0:T(1,128)} %get-tuple-element.155.refs_0_, f32[1,1024]{1,0:T(1,128)} %get-tuple-element.154.refs_1_, f32[1,3072]{1,0:T(1,128)} %reshape.82.refs_2_, bf16[2368,512]{1,0:T(8,128)(2,1)} %get-tuple-element.77.refs_3_.refs_4_.refs_5_, ...), custom_call_target="tpu_custom_call" | custom-call | flops 14898167808 | bytes 30560256 | tf_op jit(solution)/shard_map/project/pallas_call | solution.py:58
  112.8 13.1 %attend.2.refs_1_ = bf16[2368,1024]{1,0:T(8,128)(2,1)} custom-call(bf16[2368,3072]{1,0:T(8,128)(2,1)} %get-tuple-element.80.refs_0_, bf16[64,2048]{1,0:T(8,128)(2,1)} %slice.87.refs_1_, bf16[256,512]{1,0:T(8,128)(2,1)} %copy-done.15, bf16[2368,512]{1,0:T(8,128)(2,1)} %get-tuple-element.83.refs_3_.refs_1_), custom_call_target="tpu_custom_call" | custom-call | flops 3588751360 | bytes 19398656 | tf_op jit(solution)/shard_map/attend/pallas_call | solution.py:58
  127.3 35.7 %attend.3.refs_3_.refs_0_ = bf16[2368,1024]{1,0:T(8,128)(2,1)} custom-call(bf16[2368,3072]{1,0:T(8,128)(2,1)} %get-tuple-element.80.refs_0_, bf16[2368,1024]{1,0:T(8,128)(2,1)} %attend.2.refs_1_, bf16[256,512]{1,0:T(8,128)(2,1)} %copy-done.15), custom_call_target="tpu_custom_call", output_to_operand_aliasing={{}: (1, {})} | custom-call | flops 10766254080 | bytes 19398656 | tf_op jit(solution)/shard_map/attend/pallas_call | solution.py:58
  167.2 13.0 %output.1 = (f32[2368,1024]{1,0:T(8,128)}, bf16[2368,1024]{1,0:T(8,128)(2,1)}) custom-call(f32[1,1024]{1,0:T(1,128)} %get-tuple-element.158.refs_0_, f32[1,1024]{1,0:T(1,128)} %get-tuple-element.157.refs_1_.refs_0_, f32[1,1024]{1,0:T(1,128)} %get-tuple-element.156.refs_2_, bf16[2368,1024]{1,0:T(8,128)(2,1)} %attend.3.refs_3_.refs_0_, ...), custom_call_target="tpu_custom_call" | custom-call | flops 4966055936 | bytes 26357760 | tf_op jit(solution)/shard_map/output/pallas_call | solution.py:58
  180.2 35.7 %expand.1 = (bf16[2368,4096]{1,0:T(8,128)(2,1)}, bf16[2368,4096]{1,0:T(8,128)(2,1)}) custom-call(f32[1,4096]{1,0:T(1,128)} %bitcast.15, bf16[2368,1024]{1,0:T(8,128)(2,1)} %get-tuple-element.88.refs_1_.refs_0_, bf16[512,2048]{1,0:T(8,128)(2,1)} %refs_5_.3, bf16[512,2048]{1,0:T(8,128)(2,1)} %collective-permute-done.10.refs_3_.refs_6_, ...), custom_call_target="tpu_custom_call" | custom-call | flops 19864223744 | bytes 52051968 | tf_op jit(solution)/shard_map/expand/pallas_call | solution.py:58
  221.7 16.8 %reduce_outer.2.refs_7_.refs_4_ = bf16[2048,1024]{1,0:T(8,128)(2,1)} custom-call(bf16[2368,4096]{1,0:T(8,128)(2,1)} %get-tuple-element.91.refs_0_.refs_2_, bf16[2368,512]{1,0:T(8,128)(2,1)} %get-tuple-element.83.refs_3_.refs_1_, bf16[2368,512]{1,0:T(8,128)(2,1)} %copy-done, bf16[2048,512]{1,0:T(8,128)(2,1)} %all-gather.8.cloned.1.call-done.refs_7_.refs_3_.refs_5_.refs_6_), custom_call_target="tpu_custom_call" | custom-call | flops 9932111872 | bytes 28442624 | tf_op jit(solution)/shard_map/reduce_outer/pallas_call | solution.py:58
  239.1 9.5 %collective-permute-done.13.refs_6_.refs_7_ = bf16[2048,512]{1,0:T(8,128)(2,1)S(1)} collective-permute-done((bf16[2048,512]{1,0:T(8,128)(2,1)}, bf16[2048,512]{1,0:T(8,128)(2,1)S(1)}, u32[]{:S(2)}, u32[]{:S(2)}) %collective-permute-start.13) | collective-permute-done | bytes 2097184 | tf_op jit(solution)/shard_map/ppermute | solution.py:73
  249.9 29.6 %reduce_back.1 = (bf16[2368,4096]{1,0:T(8,128)(2,1)}, f32[1,1024]{1,0:T(1,128)}, f32[1,4096]{1,0:T(1,128)}) custom-call(bf16[2368,4096]{1,0:T(8,128)(2,1)} %get-tuple-element.93.refs_0_, bf16[2368,512]{1,0:T(8,128)(2,1)} %get-tuple-element.83.refs_3_.refs_1_, bf16[2368,512]{1,0:T(8,128)(2,1)} %copy-done, bf16[2048,512]{1,0:T(8,128)(2,1)} %refs_4_.1, ...), custom_call_target="tpu_custom_call" | custom-call | flops 155189248 | bytes 406688 | tf_op jit(solution)/shard_map/reduce_back/pallas_call | solution.py:58
  279.6 16.7 %reduce_outer.3 = (bf16[2048,512]{1,0:T(8,128)(2,1)}, bf16[2048,512]{1,0:T(8,128)(2,1)}) custom-call(bf16[2368,4096]{1,0:T(8,128)(2,1)} %get-tuple-element.91.refs_0_.refs_2_, bf16[2368,512]{1,0:T(8,128)(2,1)} %get-tuple-element.83.refs_3_.refs_1_, bf16[2368,512]{1,0:T(8,128)(2,1)} %copy-done, bf16[2048,1024]{1,0:T(8,128)(2,1)} %collective-permute-done.15.refs_3_, ...), custom_call_target="tpu_custom_call" | custom-call | flops 9932111872 | bytes 32636928 | tf_op jit(solution)/shard_map/reduce_outer/pallas_call | solution.py:58
  296.2 16.6 %expand_outer.2.refs_13_.refs_3_ = bf16[1024,2048]{1,0:T(8,128)(2,1)} custom-call(bf16[2368,1024]{1,0:T(8,128)(2,1)} %get-tuple-element.88.refs_1_.refs_0_, bf16[2368,4096]{1,0:T(8,128)(2,1)} %get-tuple-element.95.refs_5_.refs_1_, bf16[2048,512]{1,0:T(8,128)(2,1)} %get-tuple-element.96.refs_2_), custom_call_target="tpu_custom_call" | custom-call | flops 9932111872 | bytes 28442624 | tf_op jit(solution)/shard_map/expand_outer/pallas_call | solution.py:58
  314.5 37.5 %expand_back.1 = (f32[2368,1024]{1,0:T(8,128)}, bf16[2368,1024]{1,0:T(8,128)(2,1)}, f32[1,1024]{1,0:T(1,128)}, f32[1,1024]{1,0:T(1,128)}, f32[1,1024]{1,0:T(1,12...) custom-call(f32[1,1024]{1,0:T(1,128)} %get-tuple-element.157.refs_1_.refs_0_, ...), custom_call_target="tpu_custom_call" | custom-call | flops 193986560 | bytes 498816 | tf_op jit(solution)/shard_map/expand_back/pallas_call | solution.py:58
  362.4 17.1 %expand_outer.3 = (bf16[512,2048]{1,0:T(8,128)(2,1)}, bf16[512,2048]{1,0:T(8,128)(2,1)}) custom-call(bf16[2368,1024]{1,0:T(8,128)(2,1)} %get-tuple-element.88.refs_1_.refs_0_, bf16[2368,4096]{1,0:T(8,128)(2,1)} %get-tuple-element.95.refs_5_.refs_1_, bf16[1024,2048]{1,0:T(8,128)(2,1)} %collective-permute-done.16.refs_2_, ...), custom_call_target="tpu_custom_call" | custom-call | flops 9932111872 | bytes 32636928 | tf_op jit(solution)/shard_map/expand_outer/pallas_call | solution.py:58
  403.1 25.2 %attend_back.4.refs_8_.refs_2_ = bf16[2368,1536]{1,0:T(8,128)(2,1)} custom-call(bf16[2368,3072]{1,0:T(8,128)(2,1)} %get-tuple-element.80.refs_0_, bf16[2368,1024]{1,0:T(8,128)(2,1)} %get-tuple-element.97.refs_1_, bf16[512,512]{1,0:T(8,128)(2,1)} %get-tuple-element.103.refs_2_), custom_call_target="tpu_custom_call" | custom-call | flops 67289088 | bytes 208384 | tf_op jit(solution)/shard_map/attend_back/pallas_call | solution.py:58
  428.4 27.3 %reduce.11 = (bf16[2368,512]{1,0:T(8,128)(2,1)}, bf16[2368,512]{1,0:T(8,128)(2,1)}) custom-call(s32[4]{0:T(128)} %dynamic_slice.33.refs_0_, f32[1,1024]{1,0:T(1,128)} %get-tuple-element.159.refs_1_, bf16[2368,4096]{1,0:T(8,128)(2,1)} %get-tuple-element.91.refs_0_.refs_2_, f32[2368,1024]{1,0:T(8,128)} %get-tuple-element.92.refs_2_.refs_3_, ...), custom_call_target="tpu_custom_call" | custom-call | flops 155189248 | bytes 330784 | tf_op jit(solution)/shard_map/reduce/pallas_call | solution.py:58
  457.7 25.5 %attend_back.5.refs_1_.refs_2_ = bf16[2368,1536]{1,0:T(8,128)(2,1)} custom-call(bf16[2368,3072]{1,0:T(8,128)(2,1)} %get-tuple-element.80.refs_0_, bf16[2368,1024]{1,0:T(8,128)(2,1)} %get-tuple-element.97.refs_1_, bf16[2368,1536]{1,0:T(8,128)(2,1)} %attend_back.4.refs_8_.refs_2_, ...), custom_call_target="tpu_custom_call", output_to_operand_aliasing={{}: (2, {})} | custom-call | flops 67289088 | bytes 208384 | tf_op jit(solution)/shard_map/attend_back/pallas_call | solution.py:58
  487.4 9.1 %project_outer.6.refs_3_ = bf16[1024,768]{1,0:T(8,128)(2,1)} custom-call(bf16[2368,1024]{1,0:T(8,128)(2,1)} %get-tuple-element.107.refs_0_, bf16[2368,1536]{1,0:T(8,128)(2,1)} %attend_back.5.refs_1_.refs_2_, bf16[2048,512]{1,0:T(8,128)(2,1)} %all-reduce.5.cloned.1.call-done.refs_2_), custom_call_target="tpu_custom_call" | custom-call | flops 29097984 | bytes 107008 | tf_op jit(solution)/shard_map/project_outer/pallas_call | solution.py:58
  500.4 10.4 %collective-permute-done.19.refs_1_ = bf16[2368,512]{1,0:T(8,128)(2,1)} collective-permute-done((bf16[2368,512]{1,0:T(8,128)(2,1)}, bf16[2368,512]{1,0:T(8,128)(2,1)}, u32[]{:S(2)}, u32[]{:S(2)}) %collective-permute-start.19) | collective-permute-done | bytes 2424864 | tf_op jit(solution)/shard_map/ppermute | solution.py:73
  517.4 9.3 %project_outer.7 = (bf16[512,768]{1,0:T(8,128)(2,1)}, bf16[512,768]{1,0:T(8,128)(2,1)}) custom-call(bf16[2368,1024]{1,0:T(8,128)(2,1)} %get-tuple-element.107.refs_0_, bf16[2368,1536]{1,0:T(8,128)(2,1)} %attend_back.5.refs_1_.refs_2_, bf16[1024,768]{1,0:T(8,128)(2,1)} %copy-done.13, bf16[1024,768]{1,0:T(8,128)(2,1)} %project_outer.6.refs_3_), custom_call_target="tpu_custom_call" | custom-call | flops 29097984 | bytes 119296 | tf_op jit(solution)/shard_map/project_outer/pallas_call | solution.py:58
  526.7 25.2 %attend_back.6.refs_1_.refs_3_ = bf16[2368,768]{1,0:T(8,128)(2,1)} custom-call(bf16[2368,3072]{1,0:T(8,128)(2,1)} %get-tuple-element.80.refs_0_, bf16[2368,1024]{1,0:T(8,128)(2,1)} %get-tuple-element.97.refs_1_, bf16[512,768]{1,0:T(8,128)(2,1)} %get-tuple-element.108.refs_2_), custom_call_target="tpu_custom_call" | custom-call | flops 67289088 | bytes 179968 | tf_op jit(solution)/shard_map/attend_back/pallas_call | solution.py:58
  574.5 25.3 %attend_back.7.refs_1_.refs_4_ = bf16[2368,768]{1,0:T(8,128)(2,1)} custom-call(bf16[2368,3072]{1,0:T(8,128)(2,1)} %get-tuple-element.80.refs_0_, bf16[2368,1024]{1,0:T(8,128)(2,1)} %get-tuple-element.97.refs_1_, bf16[512,384]{1,0:T(8,128)(2,1)} %get-tuple-element.109.refs_2_), custom_call_target="tpu_custom_call" | custom-call | flops 67289088 | bytes 179968 | tf_op jit(solution)/shard_map/attend_back/pallas_call | solution.py:58
  620.5 18.4 %project_back.2 = (f32[1184,512]{1,0:T(8,128)}, bf16[1184,512]{1,0:T(8,128)(2,1)}, f32[1,1024]{1,0:T(1,128)}, f32[1,1024]{1,0:T(1,128)}, f32[1,1536]{1,0:T(1,128)}, /*index=5*/f32[1,768]{1,0:T(1,128)}, f32[1,768]{1,0:T(1,128)}) custom-call(f32[1,1024]{1,0:T(1,128)} %get-tuple-element.155.refs_0_, f32[2368,1024]{1,0:T(8,128)} %get-tuple-element.100.refs_4_.refs_1_, ...), custom_call_target="tpu_custom_call" | custom-call | flops 58195968 | bytes 305088 | tf_op jit(solution)/shard_map/project_back/pallas_call | solution.py:58
  642.9 18.9 %project_back.3 = (f32[1184,512]{1,0:T(8,128)}, bf16[1184,512]{1,0:T(8,128)(2,1)}, f32[1,1024]{1,0:T(1,128)}, f32[1,1024]{1,0:T(1,128)}, f32[1,1536]{1,0:T(1,128)}, /*index=5*/f32[1,768]{1,0:T(1,128)}, f32[1,768]{1,0:T(1,128)}) custom-call(f32[1,1024]{1,0:T(1,128)} %get-tuple-element.155.refs_0_, f32[2368,1024]{1,0:T(8,128)} %get-tuple-element.100.refs_4_.refs_1_, ...), custom_call_target="tpu_custom_call" | custom-call | flops 58195968 | bytes 305088 | tf_op jit(solution)/shard_map/project_back/pallas_call | solution.py:58
  707.2 20.0 %all-reduce.9.cloned.1.call-done = (bf16[512,768]{1,0:T(8,128)(2,1)}, bf16[512,512]{1,0:T(8,128)(2,1)}) async-done(((bf16[512,768]{1,0:T(8,128)(2,1)}, bf16[512,512]{1,0:T(8,128)(2,1)}), (bf16[512,768]{1,0:T(8,128)(2,1)}, bf16[512,512]{1,0:T(8,128)(2,1)})) %all-reduce.9.cloned.1.call-update) | async-done | bytes 1310736 | tf_op jit(solution)/shard_map/psum | solution.py:813
  (282 shorter events, 215.3 us)
Async XLA Ops:
  7.2 62.8 %all-gather.4.cloned.1.call-start = ((), (), s32[]{:S(2)}) async-start(), calls=%async_computation | async-start | bytes 1769472 | tf_op jit(solution)/shard_map/all_gather | solution.py:95
  24.2 103.1 %all-gather.6.cloned.1.call-start = ((), (), s32[]{:S(2)}) async-start(), calls=%async_computation.1 | async-start | bytes 2359296 | tf_op jit(solution)/shard_map/all_gather | solution.py:95
  24.2 54.9 %collective-permute-start.2 = (bf16[2368,512]{1,0:T(8,128)(2,1)}, bf16[2368,512]{1,0:T(8,128)(2,1)S(1)}, u32[]{:S(2)}, u32[]{:S(2)}) collective-permute-start(bf16[2368,512]{1,0:T(8,128)(2,1)} %get-tuple-element.78), channel_id=1, source_target_pairs={{0,2},{2,0},{1,3},{3,1},{4,6},{6,4},{5,7},{7,5},{8,10},{10,8},{9,1... | collective-permute-start | bytes 7274504 | tf_op jit(solution)/shard_map/ppermute | solution.py:73
  26.0 53.1 %collective-permute-start.3 = (bf16[512,1536]{1,0:T(8,128)(2,1)}, bf16[512,1536]{1,0:T(8,128)(2,1)}, u32[]{:S(2)}, u32[]{:S(2)}) collective-permute-start(bf16[512,1536]{1,0:T(8,128)(2,1)} %refs_7_.3), channel_id=1, source_target_pairs={{0,1},{1,0},{2,3},{3,2},{4,5},{5,4},{6,7},{7,6},{8,9},{9,8},{10,11... | collective-permute-start | bytes 4718600 | tf_op jit(solution)/shard_map/ppermute | solution.py:73
  70.0 110.1 %all-gather.8.cloned.1.call-start = ((), (), s32[]{:S(2)}) async-start(), calls=%async_computation.2 | async-start | bytes 2359296 | tf_op jit(solution)/shard_map/all_gather | solution.py:95
  125.9 361.4 %all-reduce.5.cloned.1.call-start = ((), (), s32[]{:S(2)}) async-start(), calls=%async_computation.3 | async-start | bytes 4194304 | tf_op jit(solution)/shard_map/psum | solution.py:775
  126.0 54.1 %collective-permute-start.12 = (bf16[2048,512]{1,0:T(8,128)(2,1)}, bf16[2048,512]{1,0:T(8,128)(2,1)}, u32[]{:S(2)}, u32[]{:S(2)}) collective-permute-start(bf16[2048,512]{1,0:T(8,128)(2,1)} %refs_4_.1), channel_id=1, source_target_pairs={{0,1},{1,0},{2,3},{3,2},{4,5},{5,4},{6,7},{7,6},{8,9},{9,8},{10,11... | collective-permute-start | bytes 6291464 | tf_op jit(solution)/shard_map/ppermute | solution.py:73
  126.1 54.1 %collective-permute-start.10 = (bf16[512,2048]{1,0:T(8,128)(2,1)}, bf16[512,2048]{1,0:T(8,128)(2,1)}, u32[]{:S(2)}, u32[]{:S(2)}) collective-permute-start(bf16[512,2048]{1,0:T(8,128)(2,1)} %refs_5_.3), channel_id=1, source_target_pairs={{0,1},{1,0},{2,3},{3,2},{4,5},{5,4},{6,7},{7,6},{8,9},{9,8},{10,11... | collective-permute-start | bytes 6291464 | tf_op jit(solution)/shard_map/ppermute | solution.py:73
  126.6 36.4 %collective-permute-start.7 = (bf16[512,512]{1,0:T(8,128)(2,1)S(1)}, bf16[512,512]{1,0:T(8,128)(2,1)}, u32[]{:S(2)}, u32[]{:S(2)}) collective-permute-start(bf16[512,512]{1,0:T(8,128)(2,1)S(1)} %copy-done.20), channel_id=1, source_target_pairs={{0,2},{2,0},{1,3},{3,1},{4,6},{6,4},{5,7},{7,5},{8,10},{10,8},{9,1... | collective-permute-start | bytes 1572872 | tf_op jit(solution)/shard_map/ppermute | solution.py:73
  127.3 52.9 %collective-permute-start.11 = (bf16[512,2048]{1,0:T(8,128)(2,1)}, bf16[512,2048]{1,0:T(8,128)(2,1)}, u32[]{:S(2)}, u32[]{:S(2)}) collective-permute-start(bf16[512,2048]{1,0:T(8,128)(2,1)} %all-gather.6.cloned.1.call-done.refs_4_.refs_7_), channel_id=1, source_target_pairs={{0,1},{1,0},{2,3},{3,2},{4,5},{5,4},{6,7},{7,6},{8,9},{9,8},{10,11... | collective-permute-start | bytes 6291464 | tf_op jit(solution)/shard_map/ppermute | solution.py:73
  165.2 55.1 %collective-permute-start.14 = (bf16[2368,512]{1,0:T(8,128)(2,1)}, bf16[2368,512]{1,0:T(8,128)(2,1)S(1)}, u32[]{:S(2)}, u32[]{:S(2)}) collective-permute-start(bf16[2368,512]{1,0:T(8,128)(2,1)} %get-tuple-element.94), channel_id=1, source_target_pairs={{0,2},{2,0},{1,3},{3,1},{4,6},{6,4},{5,7},{7,5},{8,10},{10,8},{9,1... | collective-permute-start | bytes 7274504 | tf_op jit(solution)/shard_map/ppermute | solution.py:73
  238.6 41.0 %collective-permute-start.15 = (bf16[2048,1024]{1,0:T(8,128)(2,1)}, bf16[2048,1024]{1,0:T(8,128)(2,1)}, u32[]{:S(2)}, u32[]{:S(2)}) collective-permute-start(bf16[2048,1024]{1,0:T(8,128)(2,1)} %reduce_outer.2.refs_7_.refs_4_), channel_id=1, source_target_pairs={{0,1},{1,0},{2,3},{3,2},{4,5},{5,4},{6,7},{7,6},{8,9},{9,8},{10,11... | collective-permute-start | bytes 12582920 | tf_op jit(solution)/shard_map/ppermute | solution.py:73
  312.8 48.3 %collective-permute-start.16 = (bf16[1024,2048]{1,0:T(8,128)(2,1)}, bf16[1024,2048]{1,0:T(8,128)(2,1)}, u32[]{:S(2)}, u32[]{:S(2)}) collective-permute-start(bf16[1024,2048]{1,0:T(8,128)(2,1)} %expand_outer.2.refs_13_.refs_3_), channel_id=1, source_target_pairs={{0,1},{1,0},{2,3},{3,2},{4,5},{5,4},{6,7},{7,6},{8,9},{9,8},{10,11... | collective-permute-start | bytes 12582920 | tf_op jit(solution)/shard_map/ppermute | solution.py:73
  313.2 47.9 %collective-permute-start.17 = (bf16[2048,512]{1,0:T(8,128)(2,1)}, bf16[2048,512]{1,0:T(8,128)(2,1)S(1)}, u32[]{:S(2)}, u32[]{:S(2)}) collective-permute-start(bf16[2048,512]{1,0:T(8,128)(2,1)} %get-tuple-element.101), channel_id=1, source_target_pairs={{0,2},{2,0},{1,3},{3,1},{4,6},{6,4},{5,7},{7,5},{8,10},{10,8},{9,1... | collective-permute-start | bytes 6291464 | tf_op jit(solution)/shard_map/ppermute | solution.py:73
  379.5 76.8 %collective-permute-start.20 = (bf16[512,2048]{1,0:T(8,128)(2,1)}, bf16[512,2048]{1,0:T(8,128)(2,1)S(1)}, u32[]{:S(2)}, u32[]{:S(2)}) collective-permute-start(bf16[512,2048]{1,0:T(8,128)(2,1)} %get-tuple-element.106), channel_id=1, source_target_pairs={{0,2},{2,0},{1,3},{3,1},{4,6},{6,4},{5,7},{7,5},{8,10},{10,8},{9,1... | collective-permute-start | bytes 6291464 | tf_op jit(solution)/shard_map/ppermute | solution.py:73
  385.0 217.1 %all-reduce.7.cloned.1.call-start = ((), (), s32[]{:S(2)}) async-start(), calls=%async_computation.4 | async-start | bytes 4194304 | tf_op jit(solution)/shard_map/psum | solution.py:778
  455.7 55.0 %collective-permute-start.19 = (bf16[2368,512]{1,0:T(8,128)(2,1)}, bf16[2368,512]{1,0:T(8,128)(2,1)}, u32[]{:S(2)}, u32[]{:S(2)}) collective-permute-start(bf16[2368,512]{1,0:T(8,128)(2,1)} %get-tuple-element.105), channel_id=1, source_target_pairs={{0,2},{2,0},{1,3},{3,1},{4,6},{6,4},{5,7},{7,5},{8,10},{10,8},{9,1... | collective-permute-start | bytes 7274504 | tf_op jit(solution)/shard_map/ppermute | solution.py:73
  559.3 40.5 %collective-permute-start.24 = (bf16[512,768]{1,0:T(8,128)(2,1)S(1)}, bf16[512,768]{1,0:T(8,128)(2,1)S(1)}, u32[]{:S(2)}, u32[]{:S(2)}) collective-permute-start(bf16[512,768]{1,0:T(8,128)(2,1)S(1)} %copy-done.40), channel_id=1, source_target_pairs={{0,2},{2,0},{1,3},{3,1},{4,6},{6,4},{5,7},{7,5},{8,10},{10,8},{9,1... | collective-permute-start | bytes 2359304 | tf_op jit(solution)/shard_map/ppermute | solution.py:73
  568.8 32.1 %collective-permute-start.25 = (bf16[512,384]{1,0:T(8,128)(2,1)}, bf16[512,384]{1,0:T(8,128)(2,1)S(1)}, u32[]{:S(2)}, u32[]{:S(2)}) collective-permute-start(bf16[512,384]{1,0:T(8,128)(2,1)} %get-tuple-element.113), channel_id=1, source_target_pairs={{0,2},{2,0},{1,3},{3,1},{4,6},{6,4},{5,7},{7,5},{8,10},{10,8},{9,1... | collective-permute-start | bytes 1179656 | tf_op jit(solution)/shard_map/ppermute | solution.py:73
  608.8 118.4 %all-reduce.9.cloned.1.call-start = ((), (), s32[]{:S(2)}) async-start(), calls=%async_computation.5 | async-start | bytes 2621440 | tf_op jit(solution)/shard_map/psum | solution.py:813
  642.2 49.1 %collective-permute-start.28 = (bf16[1184,512]{1,0:T(8,128)(2,1)}, bf16[1184,512]{1,0:T(8,128)(2,1)}, u32[]{:S(2)}, u32[]{:S(2)}) collective-permute-start(bf16[1184,512]{1,0:T(8,128)(2,1)} %get-tuple-element.118), channel_id=1, source_target_pairs={{0,2},{2,0},{1,3},{3,1},{4,6},{6,4},{5,7},{7,5},{8,10},{10,8},{9,1... | collective-permute-start | bytes 3637256 | tf_op jit(solution)/shard_map/ppermute | solution.py:73
  668.6 60.8 %collective-permute-start.29 = (bf16[1184,512]{1,0:T(8,128)(2,1)}, bf16[1184,512]{1,0:T(8,128)(2,1)}, u32[]{:S(2)}, u32[]{:S(2)}) collective-permute-start(bf16[1184,512]{1,0:T(8,128)(2,1)} %get-tuple-element.119), channel_id=1, source_target_pairs={{0,2},{2,0},{1,3},{3,1},{4,6},{6,4},{5,7},{7,5},{8,10},{10,8},{9,1... | collective-permute-start | bytes 3637256 | tf_op jit(solution)/shard_map/ppermute | solution.py:73
  691.3 39.7 %collective-permute-start.40 = (bf16[128,768]{1,0:T(8,128)(2,1)S(1)}, bf16[128,768]{1,0:T(8,128)(2,1)S(1)}, u32[]{:S(2)}, u32[]{:S(2)}) collective-permute-start(bf16[128,768]{1,0:T(8,128)(2,1)S(1)} %maximum_select_fusion.2), channel_id=1, source_target_pairs={{0,8},{4,12},{8,0},{12,4},{16,24},{20,28},{24,16},{28,20},{1,9},{5... | collective-permute-start | bytes 589832 | tf_op jit(solution)/shard_map/ppermute | solution.py:105
  700.1 29.2 %collective-permute-start.34 = (f32[9216]{0:T(1024)S(1)}, f32[9216]{0:T(1024)S(1)}, u32[]{:S(2)}, u32[]{:S(2)}) collective-permute-start(f32[9216]{0:T(1024)S(1)} %add.131), channel_id=1, source_target_pairs={{0,16},{4,20},{8,24},{12,28},{16,0},{20,4},{24,8},{28,12},{1,17},{... | collective-permute-start | bytes 110600 | tf_op jit(solution)/shard_map/ppermute | solution.py:105
  (67 other events, 1013.9 us)
Sparse Core Ops, SparseCore 0:
  24.3 45.6 all-gather.3
  72.7 48.2 all-gather.5
  126.1 49.6 all-gather.7
  385.2 102.1 all-reduce.4
  500.5 101.6 all-reduce.6
  642.0 85.1 all-reduce.8
